TPU v7x, 32 devices: a whole 2x2x4 slice. The times are simulated.
32 devices in a mesh: dp: 4 (over y, x), side: 2 (over core), blk: 4 (over z).
Axes of the slice: x: 2, y: 2, z: 4, core: 2. Of those that a mesh axis runs over, the one named last changes fastest.
Arguments:
- feats: bfloat16 [1024, 8, 8, 512], P(('dp', 'side', 'blk')), may hold values from -8 to 8
- size_group: int32 [1024], P(('dp', 'side', 'blk')), may hold values from 0 to 1
- labels: int32 [1024], P(('dp', 'side', 'blk')), may hold values from 0 to 9
- class_wt: int32 [10], replicated, may hold values from 1 to 5
- owners: int32 [18], replicated, may hold values from 0 to 3, as said below
- basis_in: bfloat16 [2, 512, 512], replicated, may hold values from -2 to 2
- basis_out: bfloat16 [2, 512, 512], replicated, may hold values from -2 to 2
- scales: float32 [9216, 512], P(('dp', 'blk'), 'side'), may hold values from 3e-06 to 3e-05
- master: float32 [40, 512, 512], P('blk', 'side'), may hold values from -0.09375 to 0.09375
- moment1: float32 [40, 512, 512], P('blk', 'side'), may hold values from -1.25 to 1.25
- moment2: float32 [40, 512, 512], P('blk', 'side'), may hold values from 0.0001953125 to 0.001953125
- norm_params: float32 [2, 2, 512], replicated, may hold values from 0.5 to 1.5
- norm_m: float32 [2, 2, 512], replicated, may hold values from -0.0009765625 to 0.0009765625
- norm_v: float32 [2, 2, 512], replicated, may hold values from 1.953125e-10 to 1.171875e-09
- head: float32 [513, 10], replicated, may hold values from -0.25 to 0.25
- head_m: float32 [513, 10], replicated, may hold values from -0.009765625 to 0.009765625
- head_v: float32 [513, 10], replicated, may hold values from 1.953125e-08 to 1.171875e-07
Outputs:
- loss_sum: float32 [], replicated
- weight_total: float32 [], replicated
- new_scales: float32 [9216, 512], P(('dp', 'blk'), 'side')
- new_master: float32 [40, 512, 512], P('blk', 'side')
- new_moment1: float32 [40, 512, 512], P('blk', 'side')
- new_moment2: float32 [40, 512, 512], P('blk', 'side')
- new_norm: float32 [2, 2, 512], replicated
- new_norm_m: float32 [2, 2, 512], replicated
- new_norm_v: float32 [2, 2, 512], replicated
- new_head: float32 [513, 10], replicated
- new_head_m: float32 [513, 10], replicated
- new_head_v: float32 [513, 10], replicated
Inputs may be any that keep to these rules, and one draw needn't show every extreme that they name: Each of the 4 owners holds at most 10 of the 18 matrices, and one owner holds exactly 10.
All inputs are finite; a program needn't handle non-finite values.
Results may differ from a plain program's by a relative error of at most 0.0067.
Values may be sent and summed in bfloat16 or wider, within the bound.
A program may use at most 256 MiB of HBM per device.

v0:
```python
import jax
import jax.numpy as jnp
from jax import lax
from jax.sharding import PartitionSpec as P

L = 2
TAPS = 9
STEP = 10


EPS_NORM = 1e-05
DAMPING = 0.001
DECAY = 0.95
BETA_ONE = 0.9
BETA_TWO = 0.999
ADAM_EPS = 1e-08
WEIGHT_DECAY = 0.01
RATE_CONV = 0.01
RATE_NORM = 0.5
RATE_HEAD = 0.02


def adamw(weight_now, first_now, second_now, gradient, rate):
    first_new = BETA_ONE * first_now + (1.0 - BETA_ONE) * gradient
    second_new = BETA_TWO * second_now + (1.0 - BETA_TWO) * gradient * gradient
    first_hat = first_new / (1.0 - BETA_ONE**STEP)
    second_hat = second_new / (1.0 - BETA_TWO**STEP)
    weight_new = weight_now - rate * (
        first_hat / (jnp.sqrt(second_hat) + ADAM_EPS) + WEIGHT_DECAY * weight_now
    )
    return (weight_new, first_new, second_new)


def pad_cells(values):
    return jnp.pad(values, ((0, 0), (1, 1), (1, 1), (0, 0)))


def conv_forward(inputs, kernel):
    side_len = inputs.shape[1]
    padded = pad_cells(inputs)
    total = None
    for tap in range(TAPS):
        shifted = padded[:, tap // 3 : tap // 3 + side_len, tap % 3 : tap % 3 + side_len]
        term = jnp.einsum("npqc,co->npqo", shifted, kernel[tap], preferred_element_type=jnp.float32)
        total = term if total is None else total + term
    return total


def conv_backward(grads, kernel):
    side_len = grads.shape[1]
    total = None
    for tap in range(TAPS):
        offset_row = tap // 3
        offset_col = tap % 3
        term = jnp.einsum("npqo,co->npqc", grads, kernel[tap], preferred_element_type=jnp.float32)
        term = jnp.pad(
            term, ((0, 0), (offset_row, 2 - offset_row), (offset_col, 2 - offset_col), (0, 0))
        )
        total = term if total is None else total + term
    return total[:, 1 : side_len + 1, 1 : side_len + 1]


def tap_sums(act_proj, grad_proj):
    side_len = act_proj.shape[1]
    padded = pad_cells(act_proj)
    firsts, seconds = ([], [])
    for tap in range(TAPS):
        shifted = padded[:, tap // 3 : tap // 3 + side_len, tap % 3 : tap % 3 + side_len]
        each = jnp.einsum("npqi,npqj->nij", shifted, grad_proj, preferred_element_type=jnp.float32)
        firsts.append(jnp.sum(each, axis=0))
        seconds.append(jnp.sum(each * each, axis=0))
    return jnp.concatenate([jnp.stack(firsts), jnp.stack(seconds)], axis=-1)


def shards(
    feats,
    size_group,
    labels,
    class_wt,
    owners,
    basis_in,
    basis_out,
    scales,
    master,
    moment1,
    moment2,
    norm_params,
    norm_m,
    norm_v,
    head,
    head_m,
    head_v,
):
    count_img = feats.shape[0]
    side_len = feats.shape[1]
    width = feats.shape[3]
    half = width // 2
    n_dp = lax.axis_size("dp")
    n_side = lax.axis_size("side")
    n_blk = lax.axis_size("blk")
    slots_dev = master.shape[0]
    matrices = owners.shape[0]
    block_rows = scales.shape[0]
    images_all = count_img * n_dp * n_side * n_blk
    index = jnp.arange(matrices)
    earlier = (owners[:, None] == owners[None, :]) & (index[None, :] < index[:, None])
    slot = owners * slots_dev + jnp.sum(earlier.astype(jnp.int32), axis=1)
    pieces = lax.all_gather(master.astype(jnp.bfloat16), ("side", "blk"), axis=0, tiled=True)
    pieces = pieces.reshape(n_side, n_blk * slots_dev, master.shape[1], width)
    pick = (slot[:, None] == jnp.arange(n_blk * slots_dev)[None, :]).astype(jnp.bfloat16)
    kernels = jnp.einsum("ms,hsrc->mhrc", pick, pieces, preferred_element_type=jnp.float32)
    kernels = kernels.astype(jnp.bfloat16).reshape(L, TAPS, width, width)
    line = jnp.arange(side_len)
    inner = (line[:, None] < side_len // 2) & (line[None, :] < side_len // 2)
    cell_mask = jnp.where((size_group == 1)[:, None, None], True, inner[None]).astype(jnp.float32)
    mask_four = cell_mask[..., None]
    pixels = jnp.sum(cell_mask, axis=(1, 2))
    class_hot = labels[:, None] == jnp.arange(class_wt.shape[0])[None, :]
    weight = jnp.sum(jnp.where(class_hot, class_wt[None, :], 0), axis=1).astype(jnp.float32)
    hot_float = class_hot.astype(jnp.float32)
    count_all, weight_all = lax.psum((jnp.sum(pixels), jnp.sum(weight)), ("dp", "side", "blk"))
    current = (feats.astype(jnp.float32) * mask_four).astype(jnp.bfloat16)
    kept = []
    act_out = None
    for layer in range(L):
        conv_out = conv_forward(current, kernels[layer])
        masked = conv_out * mask_four
        col_sum, sq_sum = lax.psum(
            (jnp.sum(masked, axis=(0, 1, 2)), jnp.sum(masked * conv_out, axis=(0, 1, 2))),
            ("dp", "side", "blk"),
        )
        average = col_sum / count_all
        inv_std = lax.rsqrt(sq_sum / count_all - average * average + EPS_NORM)
        normed = (conv_out - average) * inv_std
        pre_act = norm_params[layer, 0] * normed + norm_params[layer, 1]
        act_out = jax.nn.silu(pre_act) * mask_four
        kept.append((current, normed, pre_act, inv_std))
        current = act_out.astype(jnp.bfloat16)
    pooled = jnp.sum(act_out, axis=(1, 2)) / pixels[:, None]
    pooled_low = pooled.astype(jnp.bfloat16)
    head_low = head[:width].astype(jnp.bfloat16)
    logits = jnp.dot(pooled_low, head_low, preferred_element_type=jnp.float32) + head[width]
    log_prob = jax.nn.log_softmax(logits, axis=-1)
    loss_local = -jnp.sum(weight * jnp.sum(hot_float * log_prob, axis=1))
    d_logits = weight[:, None] * (jnp.exp(log_prob) - hot_float)
    grad_weights = jnp.dot(
        pooled_low.astype(jnp.float32).T, d_logits, precision=lax.Precision.HIGHEST
    )
    grad_head = jnp.concatenate([grad_weights, jnp.sum(d_logits, axis=0)[None]], axis=0)
    loss_all, head_all = lax.psum((loss_local, grad_head), ("dp", "side", "blk"))
    d_pooled = jnp.dot(d_logits, head_low.astype(jnp.float32).T, precision=lax.Precision.HIGHEST)
    d_act = d_pooled[:, None, None, :] / pixels[:, None, None, None] * mask_four
    terms = [None] * L
    grad_norm = [None] * L
    for layer in reversed(range(L)):
        inputs, normed, pre_act, inv_std = kept[layer]
        sigma = jax.nn.sigmoid(pre_act)
        d_pre = d_act * mask_four * sigma * (1.0 + pre_act * (1.0 - sigma))
        gamma_sum, beta_sum = lax.psum(
            (jnp.sum(d_pre * normed, axis=(0, 1, 2)), jnp.sum(d_pre, axis=(0, 1, 2))),
            ("dp", "side", "blk"),
        )
        grad_norm[layer] = jnp.stack([gamma_sum, beta_sum])
        gamma = norm_params[layer, 0]
        d_conv = (
            mask_four
            * inv_std
            * (
                gamma * d_pre
                - gamma * beta_sum / count_all
                - normed * gamma * gamma_sum / count_all
            )
        )
        grad_low = d_conv.astype(jnp.bfloat16)
        if layer > 0:
            d_act = conv_backward(grad_low, kernels[layer])
        act_proj = jnp.einsum(
            "npqc,ci->npqi", inputs, basis_in[layer], preferred_element_type=jnp.float32
        ).astype(jnp.bfloat16)
        grad_proj = jnp.einsum(
            "npqo,oj->npqj", grad_low, basis_out[layer], preferred_element_type=jnp.float32
        ).astype(jnp.bfloat16)
        terms[layer] = tap_sums(act_proj, grad_proj)
    whole = jnp.stack(terms).reshape(n_dp, n_blk, block_rows, 2, 2, half)
    whole = whole.transpose(0, 4, 1, 2, 3, 5).reshape(n_dp * 2 * n_blk * block_rows, 2 * half)
    reduced = lax.psum_scatter(whole, ("dp", "side", "blk"), scatter_dimension=0, tiled=True)
    proj_sum = reduced[:, :half]
    proj_square = reduced[:, half:]
    new_scales = DECAY * scales + (1.0 - DECAY) * proj_square / images_all
    divided = (proj_sum / weight_all / (new_scales + DAMPING)).astype(jnp.bfloat16)
    spread = lax.all_gather(divided, ("dp", "side", "blk"), axis=0, tiled=True)
    spread = spread.reshape(n_dp, 2, n_blk, block_rows, half).transpose(0, 2, 3, 1, 4)
    precond_all = spread.reshape(matrices, width, width)
    slot_ids = lax.axis_index("blk") * slots_dev + jnp.arange(slots_dev)
    owned = (slot[None, :] == slot_ids[:, None]).astype(jnp.bfloat16)
    chosen = jnp.einsum(
        "qm,mij->qij", owned, precond_all, preferred_element_type=jnp.float32
    ).astype(jnp.bfloat16)
    layer_hot = (index[:, None] // TAPS == jnp.arange(L)[None, :]).astype(jnp.bfloat16)
    slot_layer = jnp.dot(owned, layer_hot, preferred_element_type=jnp.float32).astype(jnp.bfloat16)
    half_rows = lax.dynamic_slice_in_dim(
        basis_in, lax.axis_index("side") * master.shape[1], master.shape[1], 1
    )
    rows_slot = jnp.einsum(
        "ql,lci->qci", slot_layer, half_rows, preferred_element_type=jnp.float32
    ).astype(jnp.bfloat16)
    cols_slot = jnp.einsum(
        "ql,loj->qoj", slot_layer, basis_out, preferred_element_type=jnp.float32
    ).astype(jnp.bfloat16)
    turned = jnp.einsum(
        "qci,qij->qcj", rows_slot, chosen, preferred_element_type=jnp.float32
    ).astype(jnp.bfloat16)
    slot_grad = jnp.einsum("qcj,qoj->qco", turned, cols_slot, preferred_element_type=jnp.float32)
    new_master, new_moment1, new_moment2 = adamw(master, moment1, moment2, slot_grad, RATE_CONV)
    new_norm, new_norm_m, new_norm_v = adamw(
        norm_params, norm_m, norm_v, jnp.stack(grad_norm) / weight_all, RATE_NORM
    )
    new_head, new_head_m, new_head_v = adamw(head, head_m, head_v, head_all / weight_all, RATE_HEAD)
    return (
        loss_all,
        weight_all,
        new_scales,
        new_master,
        new_moment1,
        new_moment2,
        new_norm,
        new_norm_m,
        new_norm_v,
        new_head,
        new_head_m,
        new_head_v,
    )


def solution(mesh):
    return jax.shard_map(
        shards,
        mesh=mesh,
        in_specs=(
            P(("dp", "side", "blk"), None, None, None),
            P(("dp", "side", "blk")),
            P(("dp", "side", "blk")),
            P(),
            P(),
            P(),
            P(),
            P(("dp", "blk"), "side"),
            P("blk", "side", None),
            P("blk", "side", None),
            P("blk", "side", None),
            P(),
            P(),
            P(),
            P(),
            P(),
            P(),
        ),
        out_specs=(
            P(),
            P(),
            P(("dp", "blk"), "side"),
            P("blk", "side", None),
            P("blk", "side", None),
            P("blk", "side", None),
            P(),
            P(),
            P(),
            P(),
            P(),
            P(),
        ),
        check_vma=False,
    )
```

profile of v0, /device:TPU:0, one launch (start us, length us, event | category | flops | bytes accessed | tf_op | source)
XLA Modules:
  0.0 1439.7 jit_solution(2503617249993847779)
XLA Ops:
  18.0 182.0 %all-gather.3.cloned.1.call-done = bf16[80,256,512]{2,1,0:T(8,128)(2,1)} async-done(((bf16[10,256,512]{2,1,0:T(8,128)(2,1)}), bf16[80,256,512]{2,1,0:T(8,128)(2,1)}) %all-gather.3.cloned.1.call-update) | async-done | bytes 20971536 | tf_op jit(solution)/shard_map/all_gather | solution.py:108
  200.0 24.8 %fusion.25 = bf16[18,2,256,512]{3,0,2,1:T(8,128)(2,1)} fusion(bf16[2,40,256,512]{3,2,1,0:T(8,128)(2,1)} %bitcast.369, s32[18]{0:T(128)S(1)} %multiply_add_fusion.3), kind=kOutput, calls=%fused_computation.98 | convolution fusion | flops 382206656 | bytes 30408776 | tf_op jit(solution)/shard_map/ms,hsrc->mhrc/dot_general | solution.py:111
  224.8 35.4 %fusion.150 = (bf16[1,2,256,512]{3,0,2,1:T(2,128)(2,1)}, bf16[1,2,256,512]{3,0,2,1:T(2,128)(2,1)}, bf16[1,2,256,512]{3,0,2,1:T(2,128)(2,1)}, bf16[1,2,256,512]{3...) fusion(bf16[18,2,256,512]{3,0,2,1:T(8,128)(2,1)} %fusion.25), kind=kLoop, calls=%fused_computation.323 | loop fusion | bytes 18874368 | tf_op jit(solution)/shard_map/slice | solution.py:44
  285.6 11.1 multiply_reduce_fusion.1
  296.7 51.2 %all-reduce.16 = (f32[512]{0:T(512)S(1)}, f32[]{:T(128)}, f32[512]{0:T(512)S(1)}) all-reduce(f32[512]{0:T(512)S(1)} %get-tuple-element.53, f32[]{:T(128)} %get-tuple-element.59, f32[512]{0:T(512)S(1)} %get-tuple-element.52), channel_id=1, replica_groups=mesh['dp'=4,'side'=2,'blk'=4] {'dp','side','blk'}, use_global_device_ids=true, to_apply=%region_7.8 | all-reduce | flops 1025 | bytes 8200 | tf_op jit(solution)/shard_map/psum | solution.py:128
  375.4 11.0 multiply_reduce_fusion
  386.4 41.0 %all-reduce.15 = (f32[512]{0:T(512)S(1)}, f32[512]{0:T(512)S(1)}) all-reduce(f32[512]{0:T(512)S(1)} %get-tuple-element.51, f32[512]{0:T(512)S(1)} %get-tuple-element.50), channel_id=1, replica_groups=mesh['dp'=4,'side'=2,'blk'=4] {'dp','side','blk'}, use_global_device_ids=true, to_apply=%region_11.12 | all-reduce | flops 1024 | bytes 8192 | tf_op jit(solution)/shard_map/psum | solution.py:128
  435.2 39.4 %all-reduce.14 = (f32[512]{0:T(512)S(1)}, f32[512]{0:T(512)S(1)}) all-reduce(f32[512]{0:T(512)S(1)} %get-tuple-element.49, f32[512]{0:T(512)S(1)} %get-tuple-element.48), channel_id=1, replica_groups=mesh['dp'=4,'side'=2,'blk'=4] {'dp','side','blk'}, use_global_device_ids=true, to_apply=%region_24.25 | all-reduce | flops 1024 | bytes 8192 | tf_op jit(solution)/shard_map/psum | solution.py:159
  512.5 12.3 pad_add_fusion
  524.9 13.5 fusion.144
  538.4 41.6 %all-reduce.13 = (f32[]{:T(128)}, f32[]{:T(128)}, f32[512]{0:T(512)S(1)}, f32[512]{0:T(512)S(1)}, f32[513,10]{0,1:T(8,128)}) all-reduce(f32[]{:T(128)S(6)} %neg.14, f32[]{:T(128)} %get-tuple-element.60, f32[512]{0:T(512)S(1)} %get-tuple-element.55, ...), channel_id=1, replica_groups=mesh['dp'=4,'side'=2,'blk'=4] {'dp','side','blk'}, use_global_device_ids=true, to_apply=%region_18.19 | all-reduce | flops 6156 | bytes 49248 | tf_op jit(solution)/shard_map/psum | solution.py:150
  586.8 6.9 bitcast_reduce_fusion.17
  600.5 6.9 bitcast_reduce_fusion.15
  607.4 7.2 bitcast_reduce_fusion.14
  635.2 7.0 bitcast_reduce_fusion.10
  642.2 6.9 bitcast_reduce_fusion.9
  652.2 6.9 bitcast_reduce_fusion.7
  659.1 7.2 bitcast_reduce_fusion.8
  666.3 7.0 bitcast_reduce_fusion.6
  673.3 7.0 bitcast_reduce_fusion.5
  680.3 7.0 bitcast_reduce_fusion.4
  736.1 11.1 maximum_bitcast_fusion.1
  747.2 20.8 %pad_maximum_fusion = f32[2,9,512,1024]{3,2,1,0:T(8,128)} fusion(f32[1,9,512,1024]{3,2,1,0:T(8,128)} %maximum_bitcast_fusion.1, f32[1,9,512,1024]{3,2,1,0:T(8,128)S(1)} %maximum_bitcast_fusion), kind=kLoop, calls=%fused_computation | loop fusion | flops 9437184 | bytes 75497472 | tf_op jit(solution)/shard_map/stack | solution.py:184
  768.1 47.8 %reshape.180 = f32[4,4,576,2,2,256]{5,4,3,2,1,0:T(2,128)} reshape(f32[2,9,512,1024]{3,2,1,0:T(8,128)} %pad_maximum_fusion) | data formatting | bytes 75497472 | tf_op jit(solution)/shard_map/reshape | solution.py:184
  815.8 52.2 %copy.54 = f32[4,2,4,576,2,256]{5,4,3,2,1,0:T(2,128)} copy(f32[4,2,4,576,2,256]{5,1,4,3,2,0:T(2,128)} %bitcast.366) | data formatting | bytes 75497472 | tf_op jit(solution)/shard_map/transpose | solution.py:185
  868.0 29.8 %copy.123 = f32[2304,8,2,256]{3,1,2,0:T(8,128)} copy(f32[2304,8,2,256]{3,2,1,0:T(2,128)} %bitcast.367) | data formatting | bytes 75497472
  897.9 348.9 %reduce-scatter.2.cloned.1.call-done = f32[576,512]{1,0:T(8,128)} async-done(((f32[18432,512]{1,0:T(8,128)}), f32[576,512]{1,0:T(8,128)}) %reduce-scatter.2.cloned.1.call-update) | async-done | bytes 1179664 | tf_op jit(solution)/shard_map/reduce_scatter | solution.py:186
  1261.3 70.4 %all-gather.5.cloned.1.call-done = bf16[18432,256]{1,0:T(8,128)(2,1)} async-done(((bf16[576,256]{1,0:T(8,128)(2,1)}), bf16[18432,256]{1,0:T(8,128)(2,1)}) %all-gather.5.cloned.1.call-update) | async-done | bytes 9437200 | tf_op jit(solution)/shard_map/all_gather | solution.py:191
  1331.7 18.3 %copy.157 = bf16[4,2,4,576,256]{4,1,3,2,0:T(2,128)(2,1)} copy(bf16[4,2,4,576,256]{4,3,2,1,0:T(8,128)(2,1)} %bitcast.370) | data formatting | bytes 18874368 | tf_op jit(solution)/shard_map/reshape | solution.py:192
  1350.1 15.7 %reshape.183 = bf16[18,512,512]{2,1,0:T(8,128)(2,1)} reshape(bf16[4,4,576,2,256]{4,3,2,1,0:T(2,128)(2,1)} %bitcast.368) | data formatting | bytes 18874368 | tf_op jit(solution)/shard_map/reshape | solution.py:193
  1365.8 16.2 %fusion.22 = bf16[10,512,512]{2,0,1:T(8,128)(2,1)} fusion(bf16[18,512,512]{2,1,0:T(8,128)(2,1)} %reshape.183, s32[18]{0:T(128)S(1)} %copy-done.83, s32[10]{0:T(128)S(1)} %iota_add_fusion), kind=kOutput, calls=%fused_computation.96 | convolution fusion | flops 96993456 | bytes 14680176 | tf_op jit(solution)/shard_map/qm,mij->qij/dot_general | solution.py:196
  1382.0 50.8 %multiply_subtract_fusion = (f32[10,256,512]{2,1,0:T(8,128)}, f32[10,256,512]{2,1,0:T(8,128)}, f32[10,256,512]{2,1,0:T(8,128)}) fusion(f32[10,256,512]{2,1,0:T(8,128)} %param.25, f32[10,256,512]{2,1,0:T(8,128)} %param.26, f32[10,256,512]{2,1,0:T(8,128)} %param.27, bf16[10,512,512]{2,0,1:T(8,128)(2,1)} %convolution_convert_fusion, ...), kind=kOutput, calls=%fused_computation.108 | convolution fusion | flops 2705326080 | bytes 44564480 | tf_op jit(solution)/shard_map/qcj,qoj->qco/dot_general | solution.py:213
  (320 shorter events, 208.4 us)
Async XLA Ops:
  7.2 6.0 copy-start.72
  7.2 192.8 %all-gather.3.cloned.1.call-start = ((), (), s32[]{:S(2)}) async-start(), calls=%async_computation.1 | async-start | bytes 23592960 | tf_op jit(solution)/shard_map/all_gather | solution.py:108
  11.7 1235.1 %reduce-scatter.2.cloned.1.call-start = ((), (), s32[]{:S(2)}) async-start(), calls=%async_computation.2 | async-start | bytes 38928384 | tf_op jit(solution)/shard_map/reduce_scatter | solution.py:186
  13.2 186.8 %copy-start.82 = (s32[18]{0:T(128)}, s32[18]{0:T(128)S(1)}, u32[]{:S(2)}) copy-start(s32[18]{0:T(128)S(1)} %multiply_add_fusion.3) | copy-start | bytes 220
  351.7 23.7 %copy-start.2 = (bf16[32,8,8,512]{3,2,1,0:T(8,128)(2,1)}, bf16[32,8,8,512]{3,2,1,0:T(8,128)(2,1)S(1)}, u32[]{:S(2)}) copy-start(bf16[32,8,8,512]{3,2,1,0:T(8,128)(2,1)S(1)} %multiply_convert_fusion.2) | copy-start | bytes 6291460
  474.6 9.9 copy-start.74
  474.7 9.9 copy-start.78
  481.1 26.7 %copy-start = (bf16[32,8,8,512]{3,2,1,0:T(8,128)(2,1)}, bf16[32,8,8,512]{3,2,1,0:T(8,128)(2,1)S(1)}, u32[]{:S(2)}) copy-start(bf16[32,8,8,512]{3,2,1,0:T(8,128)(2,1)S(1)} %multiply_convert_fusion.1) | copy-start | bytes 6291460
  512.5 12.4 copy-start.5
  512.5 12.4 copy-start.6
  524.9 55.8 %copy-start.32 = (bf16[2,512,512]{2,1,0:T(8,128)(2,1)S(1)}, bf16[2,512,512]{2,1,0:T(8,128)(2,1)}, u32[]{:S(2)}) copy-start(bf16[2,512,512]{2,1,0:T(8,128)(2,1)} %param.23) | copy-start | bytes 3145732
  580.0 6.8 copy-start.80
  580.0 6.8 copy-start.85
  580.7 6.2 copy-start.90
  642.2 6.9 copy-start.1
  642.2 6.9 copy-start.33
  706.0 6.7 copy-start.61
  706.0 6.8 copy-start.62
  897.8 349.0 %copy-start.63 = (f32[576,256]{1,0:T(8,128)S(1)}, f32[576,256]{1,0:T(8,128)}, u32[]{:S(2)}) copy-start(f32[576,256]{1,0:T(8,128)} %param.24) | copy-start | bytes 1769476
  897.8 352.1 %copy-start.83 = (s32[18]{0:T(128)S(1)}, s32[18]{0:T(128)}, u32[]{:S(2)}) copy-start(s32[18]{0:T(128)} %copy-done.82) | copy-start | bytes 220
  897.8 352.3 %copy-start.66 = (bf16[2,512,512]{2,1,0:T(8,128)(2,1)S(1)}, bf16[2,512,512]{2,1,0:T(8,128)(2,1)}, u32[]{:S(2)}) copy-start(bf16[2,512,512]{2,1,0:T(8,128)(2,1)} %param.22) | copy-start | bytes 3145732
  897.9 433.9 %all-gather.5.cloned.1.call-start = ((), (), s32[]{:S(2)}) async-start(), calls=%async_computation.3 | async-start | bytes 9732096 | tf_op jit(solution)/shard_map/all_gather | solution.py:191
  1246.8 6.6 copy-start.34
  1253.4 5.3 copy-start.75
  1253.4 5.3 copy-start.79
  1253.4 5.3 copy-start.73
  1253.4 5.3 copy-start.76
  1253.4 5.3 copy-start.77
  1253.5 6.6 copy-start.68
  1253.5 6.5 copy-start.69
  1253.5 6.5 copy-start.70
  1253.5 6.5 copy-start.71
  (62 other events, 179.4 us)
Sparse Core Ops, SparseCore 0:
  11.8 188.1 all-gather.2
  898.0 348.7 reduce-scatter.1
  1250.6 81.1 all-gather.4
where the time goes:
time: 1450 us; the launch traced here: 1440 us
  waiting for transfers between devices  601 us (41%)
  matrix products  331 us (23%)
  local copies, waits for them, and re-layouts  223 us (15%)
  blocking collectives  173 us (12%)
  other arithmetic  95.3 us (7%)
  between operations  15.9 us (1%)
    reduce_scatter x1, waiting for transfers between devices, shards(): lax.psum_scatter(whole, ('dp', 'side', 'blk'), scatter_dimension=0, tiled...  349 us
    all_gather x1, waiting for transfers between devices, shards(): lax.all_gather(master.astype(jnp.bfloat16), ('side', 'blk'), axis=0, tile...  182 us
    dot_general x18, matrix products, tap_sums(): jnp.einsum('npqi,npqj->nij', shifted, grad_proj, preferred_element_type=j...  123 us
    psum x2, blocking collectives, shards(): lax.psum((jnp.sum(masked, axis=(0, 1, 2)), jnp.sum(masked * conv_out, axi...  92.2 us
    all_gather x1, waiting for transfers between devices, shards(): spread = lax.all_gather(divided, ('dp', 'side', 'blk'), axis=0, tiled=True)  70.4 us
    dot_general x18, matrix products, conv_forward(): jnp.einsum('npqc,co->npqo', shifted, kernel[tap], preferred_element_type=...  65.9 us
    unnamed x231, local copies, waits for them, and re-layouts  53.2 us
    transpose x1, local copies, waits for them, and re-layouts, shards(): whole.transpose(0, 4, 1, 2, 3, 5)  52.2 us
  transfers between devices with their start and end apart: 3, of which 3 were waited for; matrix products, arithmetic and copies ran while one was open for 1% of the time, Pallas kernels for 0%

commit v1 on v0

--- a/solution.py
+++ b/solution.py
@@ -1,6 +1,10 @@
+import functools
+
 import jax
 import jax.numpy as jnp
 from jax import lax
+from jax.experimental import pallas as pl
+from jax.experimental.pallas import tpu as pltpu
 from jax.sharding import PartitionSpec as P
 
 L = 2
@@ -70,6 +74,384 @@
         firsts.append(jnp.sum(each, axis=0))
         seconds.append(jnp.sum(each * each, axis=0))
     return jnp.concatenate([jnp.stack(firsts), jnp.stack(seconds)], axis=-1)
+
+
+MESH = pl.DeviceIdType.MESH
+SUB = 64
+UNIT = 256
+
+
+def _id(dp, side, blk):
+    return (dp, side, blk)
+
+
+def statistics_kernel(
+    images,
+    at_hbm,
+    gr_hbm,
+    out_ref,
+    at_v,
+    gr_v,
+    side_send,
+    side_recv,
+    own,
+    x_send,
+    x_recv,
+    x_keep,
+    z1_send,
+    z1_recv,
+    z2_send,
+    z2_recv,
+    z2_keep,
+    y_send,
+    y_recv,
+    y_keep,
+    load_sem,
+    side_ss,
+    side_rs,
+    x_ss,
+    x_rs,
+    z1_ss,
+    z1_rs,
+    z2_ss,
+    z2_rs,
+    y_ss,
+    y_rs,
+):
+    dp, me_side, me_z = lax.axis_index("dp"), lax.axis_index("side"), lax.axis_index("blk")
+    me_y, me_x = dp // 2, lax.rem(dp, 2)
+    to_side = (dp, 1 - me_side, me_z)
+    to_x = (me_y * 2 + 1 - me_x, me_side, me_z)
+    to_y = ((1 - me_y) * 2 + me_x, me_side, me_z)
+    z_low, z_high = lax.rem(me_z, 2), me_z // 2
+    to_z1 = (dp, me_side, z_high * 2 + 1 - z_low)
+    to_z2 = (dp, me_side, (1 - z_high) * 2 + z_low)
+    steps = 2 * 9
+
+    def loads():
+        items = []
+        for li in range(2):
+            items.append((at_hbm.at[li], at_v.at[li], li * 4 + 3))
+            for b in range(3):
+                slot = b if li == 0 or b != 1 else 3
+                items.append(
+                    (
+                        gr_hbm.at[li, pl.ds(b * images, images)],
+                        gr_v.at[pl.ds(slot * images, images)],
+                        li * 4 + b,
+                    )
+                )
+        return {key: pltpu.make_async_copy(s, d, load_sem.at[key]) for s, d, key in items}
+
+    load = loads()
+    load[3].start()
+    load[0].start()
+    load[1].start()
+    load[2].start()
+    load[7].start()
+    load[5].start()
+
+    barrier = pltpu.get_barrier_semaphore()
+    for target in (to_side, to_x, to_y, to_z1, to_z2):
+        pl.semaphore_signal(barrier, inc=1, device_id=target, device_id_type=MESH)
+    pl.semaphore_wait(barrier, 5)
+
+    def remote(src, dst, ss, rs, target):
+        return pltpu.make_async_remote_copy(
+            src_ref=src, dst_ref=dst, send_sem=ss, recv_sem=rs, device_id=target,
+            device_id_type=MESH,
+        )
+
+    def side_copy(k, j):
+        ring = lax.rem(k, 2)
+        return remote(
+            side_send.at[ring, j], side_recv.at[ring, j], side_ss.at[ring, j],
+            side_rs.at[ring, j], to_side,
+        )
+
+    def x_copy(k):
+        ring = lax.rem(k, 4)
+        return remote(x_send.at[ring], x_recv.at[k], x_ss.at[ring], x_rs.at[k], to_x)
+
+    def z1_copy(k, w, slot):
+        ring = lax.rem(k, 4)
+        return remote(
+            z1_send.at[ring, w], z1_recv.at[slot], z1_ss.at[ring, w], z1_rs.at[slot], to_z1
+        )
+
+    def z2_copy(k, w, slot):
+        ring = lax.rem(k, 4)
+        return remote(
+            z2_send.at[ring, w], z2_recv.at[slot], z2_ss.at[ring, w], z2_rs.at[slot], to_z2
+        )
+
+    def y_copy(k, w, slot):
+        ring = lax.rem(k, 4)
+        return remote(
+            y_send.at[ring, w], y_recv.at[slot], y_ss.at[ring, w], y_rs.at[slot], to_y
+        )
+
+    def product(k, j, half, store):
+        li = k // 9
+        unit = 9 * j + lax.rem(k, 9)
+        tap = unit // 2
+        base = lax.rem(unit, 2) * UNIT
+        a, b = tap // 3, lax.rem(tap, 3)
+        slot = jnp.where((b == 1) & (li == 1), 3, b)
+        first_row = pl.multiple_of((2 - a) * 16, 16)
+        cols = pl.ds(pl.multiple_of(half * 256, 256), 256)
+
+        def tile(r, carry):
+            rows = pl.ds(pl.multiple_of(base + r * 128, 128), 128)
+            square = total = None
+            for n in range(images):
+                p = jnp.dot(
+                    at_v[li, rows, n * 128 : (n + 1) * 128],
+                    gr_v[slot * images + n, pl.ds(first_row, 128), cols],
+                    preferred_element_type=jnp.float32,
+                )
+                square = p * p if square is None else square + p * p
+                total = p if total is None else total + p
+            store(r, total, square)
+            return carry
+
+        lax.fori_loop(0, 2, tile, 0)
+
+    def subunits(k):
+        li = k // 9
+        i = lax.rem(k, 9)
+        for w in range(4):
+            v = 4 * i + w
+            owner = v // 9
+            yield w, li, owner, lax.rem(v, 9)
+
+    def step(k, carry):
+        @pl.when(k == 0)
+        def _():
+            load[3].wait()
+            load[0].wait()
+            load[1].wait()
+
+        @pl.when(k == 1)
+        def _():
+            load[2].wait()
+
+        @pl.when(k == 8)
+        def _():
+            load[4].start()
+
+        @pl.when(k == 9)
+        def _():
+            load[6].start()
+            load[7].wait()
+            load[4].wait()
+            load[5].wait()
+
+        @pl.when(k == 10)
+        def _():
+            load[6].wait()
+
+        @pl.when(k < steps)
+        def _():
+            ring = lax.rem(k, 2)
+            for j in range(2):
+                @pl.when(k >= 2)
+                def _():
+                    side_copy(k - 2, j).wait_send()
+
+                def store(r, total, square, j=j):
+                    rows = pl.ds(pl.multiple_of(r * 128, 128), 128)
+                    side_send[ring, j, 0, rows, :] = total.astype(jnp.bfloat16)
+                    side_send[ring, j, 1, rows, :] = square.astype(jnp.bfloat16)
+
+                product(k, j, 1 - me_side, store)
+                side_copy(k, j).start()
+            for j in range(2):
+                def store(r, total, square, j=j):
+                    rows = pl.ds(pl.multiple_of(r * 128, 128), 128)
+                    own[j, 0, rows, :] = total
+                    own[j, 1, rows, :] = square
+
+                product(k, j, me_side, store)
+            for j in range(2):
+                side_copy(k, j).wait_recv()
+            @pl.when(k >= 4)
+            def _():
+                x_copy(k - 4).wait_send()
+            mine = own[me_x] + side_recv[ring, me_x].astype(jnp.float32)
+            x_keep[lax.rem(k, 4)] = mine
+            other = own[1 - me_x] + side_recv[ring, 1 - me_x].astype(jnp.float32)
+            x_send[lax.rem(k, 4)] = other.astype(jnp.bfloat16)
+            x_copy(k).start()
+
+        kx = k - 2
+
+        @pl.when((kx >= 0) & (kx < steps))
+        def _():
+            ring = lax.rem(kx, 4)
+            x_copy(kx).wait_recv()
+            both = x_keep[ring] + x_recv[kx].astype(jnp.float32)
+            x_keep[ring] = both
+            for w, li, owner, q in subunits(kx):
+                leaves = lax.rem(owner, 2) != z_low
+                slot = li * 18 + (owner // 2) * 9 + q
+
+                @pl.when(leaves)
+                def _():
+                    z1_send[ring, w] = x_keep[ring, :, w * SUB : (w + 1) * SUB, :].astype(
+                        jnp.bfloat16
+                    )
+                    z1_copy(kx, w, slot).start()
+
+        kz = k - 3
+
+        @pl.when((kz >= 0) & (kz < steps))
+        def _():
+            ring = lax.rem(kz, 4)
+            for w, li, owner, q in subunits(kz):
+                slot = li * 18 + (owner // 2) * 9 + q
+                stays = lax.rem(owner, 2) == z_low
+
+                @pl.when(lax.rem(owner, 2) != z_low)
+                def _():
+                    z1_copy(kz, w, slot).wait_send()
+
+                @pl.when(stays & (owner // 2 == z_high))
+                def _():
+                    z1_copy(kz, w, slot).wait_recv()
+                    z2_keep[ring, w] = x_keep[ring, :, w * SUB : (w + 1) * SUB, :] + z1_recv[
+                        slot
+                    ].astype(jnp.float32)
+
+                @pl.when(stays & (owner // 2 != z_high))
+                def _():
+                    z1_copy(kz, w, slot).wait_recv()
+                    z2_send[ring, w] = (
+                        x_keep[ring, :, w * SUB : (w + 1) * SUB, :]
+                        + z1_recv[slot].astype(jnp.float32)
+                    ).astype(jnp.bfloat16)
+                    z2_copy(kz, w, li * 9 + q).start()
+
+        kt = k - 4
+
+        @pl.when((kt >= 0) & (kt < steps))
+        def _():
+            ring = lax.rem(kt, 4)
+            for w, li, owner, q in subunits(kt):
+                low_same = lax.rem(owner, 2) == z_low
+
+                @pl.when(low_same & (owner // 2 != z_high))
+                def _():
+                    z2_copy(kt, w, li * 9 + q).wait_send()
+
+                here = owner == me_z
+
+                @pl.when(here & (me_y == 1 - li))
+                def _():
+                    z2_copy(kt, w, li * 9 + q).wait_recv()
+                    y_keep[ring, w] = z2_keep[ring, w] + z2_recv[li * 9 + q].astype(jnp.float32)
+
+                @pl.when(here & (me_y != 1 - li))
+                def _():
+                    z2_copy(kt, w, li * 9 + q).wait_recv()
+                    y_send[ring, w] = (
+                        z2_keep[ring, w] + z2_recv[li * 9 + q].astype(jnp.float32)
+                    ).astype(jnp.bfloat16)
+                    y_copy(kt, w, q).start()
+
+        ky = k - 5
+
+        @pl.when(ky >= 0)
+        def _():
+            ring = lax.rem(ky, 4)
+            for w, li, owner, q in subunits(ky):
+                here = owner == me_z
+
+                @pl.when(here & (me_y == 1 - li))
+                def _():
+                    y_copy(ky, w, q).wait_recv()
+                    value = y_keep[ring, w] + y_recv[q].astype(jnp.float32)
+                    rows = pl.ds(pl.multiple_of(q * SUB, SUB), SUB)
+                    out_ref[0, rows, :] = value[0]
+                    out_ref[1, rows, :] = value[1]
+
+                @pl.when(here & (me_y != 1 - li))
+                def _():
+                    y_copy(ky, w, q).wait_send()
+
+        return carry
+
+    lax.fori_loop(0, steps + 5, step, 0)
+    for j in range(2):
+        side_copy(steps - 2, j).wait_send()
+        side_copy(steps - 1, j).wait_send()
+    for k in range(steps - 4, steps):
+        x_copy(k).wait_send()
+
+
+def statistics(act_turned, grad_turned):
+    images = act_turned.shape[2] // 128
+    dma = pltpu.SemaphoreType.DMA
+    low, full = jnp.bfloat16, jnp.float32
+    pair = (2, UNIT, 256)
+    small = (2, SUB, 256)
+    return pl.pallas_call(
+        functools.partial(statistics_kernel, images),
+        out_shape=jax.ShapeDtypeStruct((2, 576, 256), full),
+        in_specs=[pl.BlockSpec(memory_space=pl.ANY)] * 2,
+        out_specs=pl.BlockSpec(memory_space=pltpu.VMEM),
+        scratch_shapes=[
+            pltpu.VMEM((2, 512, images * 128), low),
+            pltpu.VMEM((4 * images, 160, 512), low),
+            pltpu.VMEM((2, 2) + pair, low),
+            pltpu.VMEM((2, 2) + pair, low),
+            pltpu.VMEM((2,) + pair, full),
+            pltpu.VMEM((4,) + pair, low),
+            pltpu.VMEM((18,) + pair, low),
+            pltpu.VMEM((4,) + pair, full),
+            pltpu.VMEM((4, 4) + small, low),
+            pltpu.VMEM((36,) + small, low),
+            pltpu.VMEM((4, 4) + small, low),
+            pltpu.VMEM((18,) + small, low),
+            pltpu.VMEM((4, 4) + small, full),
+            pltpu.VMEM((4, 4) + small, low),
+            pltpu.VMEM((9,) + small, low),
+            pltpu.VMEM((4, 4) + small, full),
+            dma((8,)),
+            dma((2, 2)),
+            dma((2, 2)),
+            dma((4,)),
+            dma((18,)),
+            dma((4, 4)),
+            dma((36,)),
+            dma((4, 4)),
+            dma((18,)),
+            dma((4, 4)),
+            dma((9,)),
+        ],
+        name="statistics",
+        compiler_params=pltpu.CompilerParams(
+            collective_id=0, has_side_effects=True, vmem_limit_bytes=62 * 2**20
+        ),
+    )(act_turned, grad_turned)
+
+
+def turned_operands(inputs, grad_low, basis_in, basis_out):
+    images, side_len, _, width = inputs.shape
+    wide = jnp.pad(inputs, ((0, 0), (0, 0), (0, 8), (0, 0))).reshape(images * 128, width)
+    act = lax.dot_general(
+        basis_in, wide, (((0,), (1,)), ((), ())), preferred_element_type=jnp.float32
+    ).astype(jnp.bfloat16)
+    grad = jnp.einsum(
+        "npqo,oj->npqj", grad_low, basis_out, preferred_element_type=jnp.float32
+    ).astype(jnp.bfloat16)
+    zero = ((0, 0), (1, 1))
+    shifts = [
+        jnp.pad(grad[:, :, 1:], zero + ((0, 9), (0, 0))),
+        jnp.pad(grad, zero + ((0, 8), (0, 0))),
+        jnp.pad(grad[:, :, :7], zero + ((1, 8), (0, 0))),
+    ]
+    return act, jnp.concatenate([s.reshape(images, 160, width) for s in shifts], axis=0)
 
 
 def shards(
@@ -150,6 +532,7 @@
     loss_all, head_all = lax.psum((loss_local, grad_head), ("dp", "side", "blk"))
     d_pooled = jnp.dot(d_logits, head_low.astype(jnp.float32).T, precision=lax.Precision.HIGHEST)
     d_act = d_pooled[:, None, None, :] / pixels[:, None, None, None] * mask_four
+    fast = (n_dp, n_side, n_blk) == (4, 2, 4) and block_rows == 576
     terms = [None] * L
     grad_norm = [None] * L
     for layer in reversed(range(L)):
@@ -174,6 +557,9 @@
         grad_low = d_conv.astype(jnp.bfloat16)
         if layer > 0:
             d_act = conv_backward(grad_low, kernels[layer])
+        if fast:
+            terms[layer] = turned_operands(inputs, grad_low, basis_in[layer], basis_out[layer])
+            continue
         act_proj = jnp.einsum(
             "npqc,ci->npqi", inputs, basis_in[layer], preferred_element_type=jnp.float32
         ).astype(jnp.bfloat16)
@@ -181,11 +567,16 @@
             "npqo,oj->npqj", grad_low, basis_out[layer], preferred_element_type=jnp.float32
         ).astype(jnp.bfloat16)
         terms[layer] = tap_sums(act_proj, grad_proj)
-    whole = jnp.stack(terms).reshape(n_dp, n_blk, block_rows, 2, 2, half)
-    whole = whole.transpose(0, 4, 1, 2, 3, 5).reshape(n_dp * 2 * n_blk * block_rows, 2 * half)
-    reduced = lax.psum_scatter(whole, ("dp", "side", "blk"), scatter_dimension=0, tiled=True)
-    proj_sum = reduced[:, :half]
-    proj_square = reduced[:, half:]
+    if fast:
+        proj_sum, proj_square = statistics(
+            jnp.stack([terms[1][0], terms[0][0]]), jnp.stack([terms[1][1], terms[0][1]])
+        )
+    else:
+        whole = jnp.stack(terms).reshape(n_dp, n_blk, block_rows, 2, 2, half)
+        whole = whole.transpose(0, 4, 1, 2, 3, 5).reshape(n_dp * 2 * n_blk * block_rows, 2 * half)
+        reduced = lax.psum_scatter(whole, ("dp", "side", "blk"), scatter_dimension=0, tiled=True)
+        proj_sum = reduced[:, :half]
+        proj_square = reduced[:, half:]
     new_scales = DECAY * scales + (1.0 - DECAY) * proj_square / images_all
     divided = (proj_sum / weight_all / (new_scales + DAMPING)).astype(jnp.bfloat16)
     spread = lax.all_gather(divided, ("dp", "side", "blk"), axis=0, tiled=True)

time: 1450 us -> 1040 us (0.72)
  waiting for transfers between devices: 601 us -> 263 us
  Pallas kernels: 0 us -> 167 us
  local copies, waits for them, and re-layouts: 223 us -> 98.5 us
  matrix products: 331 us -> 213 us
  other arithmetic: 95.3 us -> 110 us
    reduce_scatter x1 -> x0, waiting for transfers between devices: 349 us -> none  [shards(): lax.psum_scatter(whole, ('dp', 'side', 'blk'), scatter_dimension=0, tiled...]
    pallas_call x0 -> x1, Pallas kernels: none -> 167 us  [statistics(): pl.pallas_call(functools.partial(statistics_kernel, images), out_shape=ja...]
    dot_general x22 -> x4, matrix products: 134 us -> 16.2 us  [the longest x2 8.94 us: turned_operands(): lax.dot_general(basis_in, wide, (((0,), (1,)), ((), ())), preferred_eleme...]
    transpose x1 -> x0, local copies, waits for them, and re-layouts: 52.2 us -> none  [shards(): whole.transpose(0, 4, 1, 2, 3, 5)]
    unnamed x231 -> x116, local copies, waits for them, and re-layouts: 53.2 us -> 4.62 us
    reshape x1 -> x0, local copies, waits for them, and re-layouts: 47.8 us -> none  [shards(): whole = jnp.stack(terms).reshape(n_dp, n_blk, block_rows, 2, 2, half)]
    pad x0 -> x8, local copies, waits for them, and re-layouts: none -> 21.4 us  [the longest x2 7.86 us: turned_operands(): jnp.pad(grad[:, :, :7], zero + ((1, 8), (0, 0)))]
  transfers between devices with their start and end apart: 3 -> 2, of which waited for: 3 -> 2; matrix products, arithmetic and copies ran while one was open for 1% -> 2% of each run, Pallas kernels for 0% -> 0%
where the time goes in v1:
time: 1040 us; the launch traced here: 1030 us
  waiting for transfers between devices  263 us (25%)
  matrix products  213 us (20%)
  Pallas kernels  167 us (16%)
  blocking collectives  161 us (15%)
  other arithmetic  110 us (11%)
  local copies, waits for them, and re-layouts  98.5 us (9%)
  between operations  15.7 us (2%)
    all_gather x1, waiting for transfers between devices, shards(): lax.all_gather(master.astype(jnp.bfloat16), ('side', 'blk'), axis=0, tile...  179 us
    pallas_call x1, Pallas kernels, statistics(): pl.pallas_call(functools.partial(statistics_kernel, images), out_shape=ja...  167 us
    all_gather x1, waiting for transfers between devices, shards(): spread = lax.all_gather(divided, ('dp', 'side', 'blk'), axis=0, tiled=True)  83.8 us
    psum x2, blocking collectives, shards(): lax.psum((jnp.sum(masked, axis=(0, 1, 2)), jnp.sum(masked * conv_out, axi...  79.9 us
    dot_general x18, matrix products, conv_forward(): jnp.einsum('npqc,co->npqo', shifted, kernel[tap], preferred_element_type=...  66.7 us
    dot_general x1, matrix products, shards(): jnp.einsum('qcj,qoj->qco', turned, cols_slot, preferred_element_type=jnp....  50.7 us
    another operation x2, other arithmetic, shards(): jnp.stack([terms[1][1], terms[0][1]])  43.5 us
    psum x1, blocking collectives, shards(): lax.psum((loss_local, grad_head), ('dp', 'side', 'blk'))  41.5 us
  transfers between devices with their start and end apart: 2, of which 2 were waited for; matrix products, arithmetic and copies ran while one was open for 2% of the time, Pallas kernels for 0%

profile of v1, /device:TPU:0, one launch (start us, length us, event | category | flops | bytes accessed | tf_op | source)
XLA Modules:
  0.0 1028.9 jit_solution(17481977377799350424)
XLA Ops:
  7.3 4.3 convert_element_type.124
  16.2 4.5 fusion.11
  20.6 179.3 %all-gather.3.cloned.1.call-done = bf16[80,256,512]{2,1,0:T(8,128)(2,1)} async-done(((bf16[10,256,512]{2,1,0:T(8,128)(2,1)}), bf16[80,256,512]{2,1,0:T(8,128)(2,1)}) %all-gather.3.cloned.1.call-update) | async-done | bytes 20971536 | tf_op jit(solution)/shard_map/all_gather | solution.py:490
  200.0 25.0 %fusion.7 = bf16[18,2,256,512]{3,0,2,1:T(8,128)(2,1)} fusion(bf16[2,40,256,512]{3,2,1,0:T(8,128)(2,1)} %bitcast.175, s32[18]{0:T(128)S(1)} %multiply_add_fusion.3), kind=kOutput, calls=%fused_computation.29 | convolution fusion | flops 382206656 | bytes 30408776 | tf_op jit(solution)/shard_map/ms,hsrc->mhrc/dot_general | solution.py:493
  224.9 35.3 %fusion.100 = (bf16[1,2,256,512]{3,0,2,1:T(2,128)(2,1)}, bf16[1,2,256,512]{3,0,2,1:T(2,128)(2,1)}, bf16[1,2,256,512]{3,0,2,1:T(2,128)(2,1)}, bf16[1,2,256,512]{3...) fusion(bf16[18,2,256,512]{3,0,2,1:T(8,128)(2,1)} %fusion.7), kind=kLoop, calls=%fused_computation.187 | loop fusion | bytes 18874368 | tf_op jit(solution)/shard_map/slice | solution.py:48
  285.7 11.1 %multiply_reduce_fusion.1 = (f32[512]{0:T(512)S(1)}, f32[512]{0:T(512)S(1)}, f32[32,8,8,512]{3,2,1,0:T(8,128)}) fusion(f32[32,8,8]{2,1,0:T(8,128)S(1)} %select_convert_fusion, bf16[512,512,1,1]{1,0,3,2:T(8,128)(2,1)} %bitcast.211, bf16[32,8,8,512]{3,2,1,0:T(8,128)(2,1)S(1)} %multiply_convert_fusion.3, f32[32,8,8,512]{3,2,1,0:T(8,128)} %fusion.32, ...), kind=kOutput, calls=%fused_computation.33 | convolution fusion | flops 1086323712 | bytes 40382464 | tf_op jit(solution)/shard_map/npqc,co->npqo/dot_general | solution.py:48
  296.7 38.9 %all-reduce.22 = (f32[512]{0:T(512)S(1)}, f32[]{:T(128)}, f32[512]{0:T(512)S(1)}) all-reduce(f32[512]{0:T(512)S(1)} %get-tuple-element.17, f32[]{:T(128)} %get-tuple-element.23, f32[512]{0:T(512)S(1)} %get-tuple-element.16), channel_id=1, replica_groups=mesh['dp'=4,'side'=2,'blk'=4] {'dp','side','blk'}, use_global_device_ids=true, to_apply=%region_7.8 | all-reduce | flops 1025 | bytes 8200 | tf_op jit(solution)/shard_map/psum | solution.py:510
  362.3 11.8 %multiply_reduce_fusion = (f32[512]{0:T(512)S(1)}, f32[512]{0:T(512)S(1)}, f32[32,8,8,512]{3,2,1,0:T(8,128)}) fusion(f32[32,8,8]{2,1,0:T(8,128)S(1)} %select_convert_fusion, bf16[512,512,1,1]{1,0,3,2:T(8,128)(2,1)S(1)} %bitcast.199, bf16[32,8,8,512]{3,2,1,0:T(8,128)(2,1)S(1)} %multiply_convert_fusion.2, f32[32,8,8,512]{3,2,1,0:T(8,128)} %fusion.39, ...), kind=kOutput, calls=%fused_computation.31 | convolution fusion | flops 1086323712 | bytes 40382464 | tf_op jit(solution)/shard_map/npqc,co->npqo/dot_general | solution.py:48
  374.2 41.0 %all-reduce.21 = (f32[512]{0:T(512)S(1)}, f32[512]{0:T(512)S(1)}) all-reduce(f32[512]{0:T(512)S(1)} %get-tuple-element.15, f32[512]{0:T(512)S(1)} %get-tuple-element.14), channel_id=1, replica_groups=mesh['dp'=4,'side'=2,'blk'=4] {'dp','side','blk'}, use_global_device_ids=true, to_apply=%region_11.12 | all-reduce | flops 1024 | bytes 8192 | tf_op jit(solution)/shard_map/psum | solution.py:510
  416.0 3.5 multiply_reduce_fusion.4
  422.8 39.4 %all-reduce.20 = (f32[512]{0:T(512)S(1)}, f32[512]{0:T(512)S(1)}) all-reduce(f32[512]{0:T(512)S(1)} %get-tuple-element.13, f32[512]{0:T(512)S(1)} %get-tuple-element.12), channel_id=1, replica_groups=mesh['dp'=4,'side'=2,'blk'=4] {'dp','side','blk'}, use_global_device_ids=true, to_apply=%region_24.25 | all-reduce | flops 1024 | bytes 8192 | tf_op jit(solution)/shard_map/psum | solution.py:542
  462.9 5.8 multiply_convert_fusion.1
  472.0 3.4 fusion.112
  478.7 3.3 fusion.114
  482.1 3.4 fusion.115
  500.1 12.3 %pad_add_fusion = f32[32,10,10,512]{3,2,1,0:T(8,128)} fusion(f32[32,8,8,512]{3,2,1,0:T(8,128)} %fusion.113, f32[32,8,8,512]{3,2,1,0:T(8,128)} %fusion.112, f32[32,8,8,512]{3,2,1,0:T(8,128)} %fusion.111), kind=kLoop, calls=%fused_computation.23 | loop fusion | flops 3276800 | bytes 19136512 | tf_op jit(solution)/shard_map/add | solution.py:63
  512.4 14.7 %fusion.95 = (f32[512]{0:T(512)S(1)}, f32[512]{0:T(512)S(1)}, f32[32,8,8,512]{3,2,1,0:T(8,128)}) fusion(f32[512]{0:T(512)S(1)} %get-tuple-element.79, f32[32,8,8,512]{3,2,1,0:T(8,128)S(1)} %copy-done.3, f32[512]{0:T(512)S(1)} %get-tuple-element.78, f32[512]{0:T(512)S(1)} %bitcast.224, f32[512]{0:T(512)S(1)} %bitcast.220, ...), kind=kLoop, calls=%fused_computation.186 | loop fusion | flops 23067648 | bytes 37769216 | tf_op jit(solution)/shard_map/reduce_sum | solution.py:543
  527.1 41.5 %all-reduce.19 = (f32[]{:T(128)}, f32[]{:T(128)}, f32[512]{0:T(512)S(1)}, f32[512]{0:T(512)S(1)}, f32[513,10]{0,1:T(8,128)S(1)}) all-reduce(f32[]{:T(128)S(6)} %neg.14, f32[]{:T(128)} %get-tuple-element.24, f32[512]{0:T(512)S(1)} %get-tuple-element.19, ...), channel_id=1, replica_groups=mesh['dp'=4,'side'=2,'blk'=4] {'dp','side','blk'}, use_global_device_ids=true, to_apply=%region_18.19 | all-reduce | flops 6156 | bytes 49248 | tf_op jit(solution)/shard_map/psum | solution.py:532
  569.3 6.0 fusion.41
  588.2 3.9 pad.89
  595.4 3.9 pad.77
  599.3 4.5 fusion.10
  603.8 22.3 %maximum_bitcast_fusion = (bf16[1,96,160,512]{3,2,1,0:T(8,128)(2,1)}, bf16[1,96,160,512]{3,2,1,0:T(8,128)(2,1)}) fusion(bf16[32,160,512]{2,1,0:T(8,128)(2,1)} %bitcast.181, bf16[32,160,512]{2,1,0:T(8,128)(2,1)} %bitcast.177, bf16[32,160,512]{2,1,0:T(8,128)(2,1)} %bitcast.180, bf16[32,160,512]{2,1,0:T(8,128)(2,1)} %bitcast.179, ...), kind=kLoop, calls=%fused_computation.3 | loop fusion | flops 31457280 | bytes 62914560 | tf_op jit(solution)/shard_map/stack | solution.py:572
  626.1 21.3 %pad_maximum_fusion.gr_hbm = bf16[2,96,160,512]{3,2,1,0:T(8,128)(2,1)} fusion(bf16[1,96,160,512]{3,2,1,0:T(8,128)(2,1)} %get-tuple-element.85, bf16[1,96,160,512]{3,2,1,0:T(8,128)(2,1)} %get-tuple-element.84), kind=kLoop, calls=%fused_computation | loop fusion | flops 15728640 | bytes 62914560 | tf_op jit(solution)/shard_map/stack | solution.py:572
  647.3 7.5 pad_maximum_fusion.1.at_hbm
  654.8 167.2 %statistics.1 = f32[2,576,256]{2,1,0:T(8,128)} custom-call(bf16[2,512,4096]{2,1,0:T(8,128)(2,1)} %pad_maximum_fusion.1.at_hbm, bf16[2,96,160,512]{3,2,1,0:T(8,128)(2,1)} %pad_maximum_fusion.gr_hbm), custom_call_target="tpu_custom_call" | custom-call | tf_op jit(solution)/shard_map/statistics/pallas_call | solution.py:398
  829.4 5.1 convolution_convert_fusion
  837.2 83.8 %all-gather.5.cloned.1.call-done = bf16[18432,256]{1,0:T(8,128)(2,1)} async-done(((bf16[576,256]{1,0:T(8,128)(2,1)}), bf16[18432,256]{1,0:T(8,128)(2,1)}) %all-gather.5.cloned.1.call-update) | async-done | bytes 9437200 | tf_op jit(solution)/shard_map/all_gather | solution.py:582
  921.0 18.3 %copy.134 = bf16[4,2,4,576,256]{4,1,3,2,0:T(2,128)(2,1)} copy(bf16[4,2,4,576,256]{4,3,2,1,0:T(8,128)(2,1)} %bitcast.182) | data formatting | bytes 18874368 | tf_op jit(solution)/shard_map/reshape | solution.py:583
  939.4 15.7 %reshape.209 = bf16[18,512,512]{2,1,0:T(8,128)(2,1)} reshape(bf16[4,4,576,2,256]{4,3,2,1,0:T(2,128)(2,1)} %bitcast.174) | data formatting | bytes 18874368 | tf_op jit(solution)/shard_map/reshape | solution.py:584
  955.0 16.2 %fusion.4 = bf16[10,512,512]{2,0,1:T(8,128)(2,1)} fusion(bf16[18,512,512]{2,1,0:T(8,128)(2,1)} %reshape.209, s32[18]{0:T(128)S(1)} %copy-done.44, s32[10]{0:T(128)S(1)} %iota_add_fusion), kind=kOutput, calls=%fused_computation.27 | convolution fusion | flops 96993456 | bytes 14680176 | tf_op jit(solution)/shard_map/qm,mij->qij/dot_general | solution.py:587
  971.2 50.7 %multiply_subtract_fusion = (f32[10,256,512]{2,1,0:T(8,128)}, f32[10,256,512]{2,1,0:T(8,128)}, f32[10,256,512]{2,1,0:T(8,128)}) fusion(f32[10,256,512]{2,1,0:T(8,128)} %param.25, f32[10,256,512]{2,1,0:T(8,128)} %param.26, f32[10,256,512]{2,1,0:T(8,128)} %param.27, bf16[10,512,512]{2,0,1:T(8,128)(2,1)} %convolution_convert_fusion, ...), kind=kOutput, calls=%fused_computation.43 | convolution fusion | flops 2705326080 | bytes 44564480 | tf_op jit(solution)/shard_map/qcj,qoj->qco/dot_general | solution.py:604
  (189 shorter events, 108.5 us)
Async XLA Ops:
  7.2 4.5 copy-start.45
  7.2 4.5 copy-start.46
  7.2 4.6 copy-start.47
  7.2 192.8 %all-gather.3.cloned.1.call-start = ((), (), s32[]{:S(2)}) async-start(), calls=%async_computation | async-start | bytes 23592960 | tf_op jit(solution)/shard_map/all_gather | solution.py:490
  11.6 909.4 %all-gather.5.cloned.1.call-start = ((), (), s32[]{:S(2)}) async-start(), calls=%async_computation.1 | async-start | bytes 9732096 | tf_op jit(solution)/shard_map/all_gather | solution.py:582
  16.2 183.8 %copy-start.43 = (s32[18]{0:T(128)}, s32[18]{0:T(128)S(1)}, u32[]{:S(2)}) copy-start(s32[18]{0:T(128)S(1)} %multiply_add_fusion.3) | copy-start | bytes 220
  281.2 4.2 copy-start.25
  341.9 3.3 copy-start.23
  345.3 3.4 copy-start.22
  345.4 3.4 copy-start.6
  348.7 3.4 copy-start.21
  348.8 3.4 copy-start.8
  355.4 3.4 copy-start.19
  355.5 3.4 copy-start.12
  358.8 3.4 copy-start.18
  358.9 3.4 copy-start.14
  362.3 11.8 %copy-start.16 = (bf16[1,2,256,512]{3,2,0,1:T(8,128)(2,1)}, bf16[1,2,256,512]{3,2,0,1:T(8,128)(2,1)S(1)}, u32[]{:S(2)}) copy-start(bf16[1,2,256,512]{3,2,0,1:T(8,128)(2,1)S(1)} %copy.99) | copy-start | bytes 1572868
  415.2 5.1 copy-start.2
  468.7 26.7 %copy-start = (bf16[32,8,8,512]{3,2,1,0:T(8,128)(2,1)}, bf16[32,8,8,512]{3,2,1,0:T(8,128)(2,1)S(1)}, u32[]{:S(2)}) copy-start(bf16[32,8,8,512]{3,2,1,0:T(8,128)(2,1)S(1)} %multiply_convert_fusion.1) | copy-start | bytes 6291460
  472.0 3.4 copy-start.5
  478.7 3.4 copy-start.9
  482.1 3.4 copy-start.11
  500.1 12.3 %copy-start.3 = (f32[32,8,8,512]{3,2,1,0:T(8,128)S(1)}, f32[32,8,8,512]{3,2,1,0:T(8,128)}, u32[]{:S(2)}) copy-start(f32[32,8,8,512]{3,2,1,0:T(8,128)} %get-tuple-element.80) | copy-start | bytes 12582916
  512.4 56.8 %copy-start.32 = (bf16[2,512,512]{2,1,0:T(8,128)(2,1)S(1)}, bf16[2,512,512]{2,1,0:T(8,128)(2,1)}, u32[]{:S(2)}) copy-start(bf16[2,512,512]{2,1,0:T(8,128)(2,1)} %param.23) | copy-start | bytes 3145732
  595.4 3.9 copy-start.35
  654.8 167.2 %copy-start.33 = (f32[576,256]{1,0:T(8,128)S(1)}, f32[576,256]{1,0:T(8,128)}, u32[]{:S(2)}) copy-start(f32[576,256]{1,0:T(8,128)} %param.24) | copy-start | bytes 1769476
  654.8 170.3 %copy-start.44 = (s32[18]{0:T(128)S(1)}, s32[18]{0:T(128)}, u32[]{:S(2)}) copy-start(s32[18]{0:T(128)} %copy-done.43) | copy-start | bytes 220
  829.4 5.2 copy-start.40
  829.4 5.2 copy-start.41
  829.4 5.2 copy-start.42
  829.4 6.5 copy-start.37
  829.4 6.5 copy-start.38
  (19 other events, 50.8 us)
Sparse Core Ops, SparseCore 0:
  11.7 188.1 all-gather.2
  825.2 95.7 all-gather.4

commit v2 on v0

--- a/solution.py
+++ b/solution.py
@@ -1,6 +1,10 @@
+import functools
+
 import jax
 import jax.numpy as jnp
 from jax import lax
+from jax.experimental import pallas as pl
+from jax.experimental.pallas import tpu as pltpu
 from jax.sharding import PartitionSpec as P
 
 L = 2
@@ -70,6 +74,534 @@
         firsts.append(jnp.sum(each, axis=0))
         seconds.append(jnp.sum(each * each, axis=0))
     return jnp.concatenate([jnp.stack(firsts), jnp.stack(seconds)], axis=-1)
+
+
+MESH = pl.DeviceIdType.MESH
+
+
+def statistics_kernel(
+    images,
+    images_all,
+    at_hbm,
+    gr_hbm,
+    scales_hbm,
+    weight_ref,
+    out,
+    ns_out,
+    at_v,
+    gr_v,
+    sc_v,
+    ns_v,
+    div_v,
+    s_send,
+    s_recv,
+    x1_send,
+    x1_recv,
+    x1_keep,
+    y1_send,
+    y1_recv,
+    y1_keep,
+    x2_send,
+    x2_recv,
+    y2_send,
+    y2_recv,
+    two_keep,
+    z_send,
+    z_recv,
+    z_keep,
+    load_sem,
+    misc_sem,
+    local_sem,
+    ss,
+    s_rs,
+    rs,
+    z_ss,
+    z_rs,
+    gz_ss,
+    gz_rs,
+):
+    low, full = jnp.bfloat16, jnp.float32
+    dp, me_s, me_z = lax.axis_index("dp"), lax.axis_index("side"), lax.axis_index("blk")
+    me_y, me_x = dp // 2, lax.rem(dp, 2)
+    to_s = (dp, 1 - me_s, me_z)
+    to_x = (me_y * 2 + 1 - me_x, me_s, me_z)
+    to_y = ((1 - me_y) * 2 + me_x, me_s, me_z)
+    steps = 2 * 9
+
+    def remote(src, dst, send, recv, target):
+        return pltpu.make_async_remote_copy(
+            src_ref=src,
+            dst_ref=dst,
+            send_sem=send,
+            recv_sem=recv,
+            device_id=target,
+            device_id_type=MESH,
+        )
+
+    def load(li, what):
+        if what == 3:
+            return pltpu.make_async_copy(at_hbm.at[li], at_v.at[li], load_sem.at[li, 3])
+        at = pl.ds(what * images, images)
+        return pltpu.make_async_copy(gr_hbm.at[li, at], gr_v.at[li, at], load_sem.at[li, what])
+
+    for what in (3, 0, 1, 2):
+        load(0, what).start()
+
+    barrier = pltpu.get_barrier_semaphore()
+    away = [(dp, me_s, lax.rem(me_z + d, 4)) for d in (1, 2, 3)]
+    for target in [to_s, to_x, to_y] + away:
+        pl.semaphore_signal(barrier, inc=1, device_id=target, device_id_type=MESH)
+    pl.semaphore_wait(barrier, 6)
+
+    sc_local = pltpu.make_async_copy(scales_hbm.at[:, me_y], sc_v.at[1 - me_y], misc_sem.at[0])
+    sc_remote = remote(
+        scales_hbm.at[:, 1 - me_y], sc_v.at[1 - me_y], misc_sem.at[1], misc_sem.at[2], to_y
+    )
+    sc_local.start()
+    sc_remote.start()
+
+    def side_copy(k):
+        return remote(
+            s_send.at[lax.rem(k, 2)],
+            s_recv.at[lax.rem(k, 4)],
+            ss.at[0, lax.rem(k, 2)],
+            s_rs.at[lax.rem(k, 4)],
+            to_s,
+        )
+
+    def x1_copy(j):
+        ring = lax.rem(j, 2)
+        return remote(x1_send.at[ring], x1_recv.at[j], ss.at[1, ring], rs.at[0, j], to_x)
+
+    def y1_copy(j):
+        ring = lax.rem(j, 2)
+        return remote(
+            y1_send.at[ring, 1 - me_y], y1_recv.at[j], ss.at[2, ring], rs.at[1, j], to_y
+        )
+
+    def x2_copy(j):
+        ring = lax.rem(j, 2)
+        return remote(x2_send.at[ring], x2_recv.at[j], ss.at[3, ring], rs.at[2, j], to_x)
+
+    def y2_copy(j):
+        ring = lax.rem(j, 2)
+        return remote(y2_send.at[ring], y2_recv.at[j], ss.at[4, ring], rs.at[3, j], to_y)
+
+    def z_copy(j, d):
+        ring, other = lax.rem(j, 2), lax.rem(me_z + d, 4)
+        return remote(
+            z_send.at[ring, other],
+            z_recv.at[j, d - 1],
+            z_ss.at[ring, d - 1],
+            z_rs.at[j, d - 1],
+            (dp, me_s, other),
+        )
+
+    def place(j):
+        return 1 - j // 9, lax.rem(j, 9)
+
+    def local_copy(j):
+        layer, i = place(j)
+        ring = lax.rem(j, 2)
+        return pltpu.make_async_copy(
+            div_v.at[ring], out.at[me_s, layer, me_x, me_z, i, me_y], local_sem.at[ring]
+        )
+
+    def gz_copy(j, d):
+        layer, i = place(j)
+        ring, other = lax.rem(j, 2), lax.rem(me_z + d, 4)
+        return remote(
+            div_v.at[ring],
+            out.at[me_s, layer, me_x, me_z, i, me_y],
+            gz_ss.at[ring, d - 1],
+            gz_rs.at[j, d - 1],
+            (dp, me_s, other),
+        )
+
+    lower, upper = pl.ds(0, 2), pl.ds(2, 2)
+
+    def spread(j, which, kind, target):
+        part = out.at[which]
+        return remote(part, part, ss.at[kind, lax.rem(j, 2)], rs.at[kind - 1, j], target)
+
+    def g1y_copy(j):
+        layer, i = place(j)
+        return spread(j, (me_s, layer, me_x, lower, i, me_y), 5, to_y)
+
+    def g1x_copy(j):
+        layer, i = place(j)
+        return spread(j, (me_s, layer, me_x, upper, i, me_y), 6, to_x)
+
+    def g2x_copy(j):
+        layer, i = place(j)
+        return spread(j, (me_s, layer, me_x, lower, i), 7, to_x)
+
+    def g2y_copy(j):
+        layer, i = place(j)
+        return spread(j, (me_s, layer, pl.ds(0, 2), upper, i, me_y), 8, to_y)
+
+    def gs_copy(j):
+        layer, i = place(j)
+        return spread(j, (me_s, layer, pl.ds(0, 2), pl.ds(0, 4), i), 9, to_s)
+
+    def products(j, half, ahead, store):
+        li, i = j // 9, lax.rem(j, 9)
+        cols = pl.ds(pl.multiple_of(half * 256, 256), 256)
+        for u in range(8):
+            x_to = ahead if u < 4 else 1 - ahead
+            row = x_to * 2304 + (u % 4) * 576 + 64 * i
+            tap = row // 512
+            rows = pl.ds(pl.multiple_of(lax.rem(row, 512), 64), 64)
+            near = pl.ds(pl.multiple_of((2 - tap // 3) * 16, 16), 128)
+            shift = lax.rem(tap, 3) * images
+            square = total = None
+            for n in range(images):
+                p = jnp.dot(
+                    at_v[li, rows, n * 128 : (n + 1) * 128],
+                    gr_v[li, shift + n, near, cols],
+                    preferred_element_type=full,
+                )
+                square = p * p if square is None else square + p * p
+                total = p if total is None else total + p
+            store(u, x_to, u % 4, total, square)
+
+    def step(k, carry):
+        for at, needs in ((0, (0, 1, 2, 3)), (9, (0, 1, 2, 3))):
+            @pl.when(k == at)
+            def _():
+                for what in needs:
+                    load(at // 9, what).wait()
+
+        @pl.when(k == 1)
+        def _():
+            for what in range(4):
+                load(1, what).start()
+
+        @pl.when((k >= 2) & (k < steps))
+        def _():
+            side_copy(k - 2).wait_send()
+
+        @pl.when(k < steps)
+        def _():
+            ring = lax.rem(k, 2)
+
+            def store(u, x_to, z_to, total, square):
+                s_send[ring, u, 0] = total.astype(low)
+                s_send[ring, u, 1] = square.astype(low)
+
+            products(k, 1 - me_s, 0, store)
+            side_copy(k).start()
+
+        j = k - 1
+
+        @pl.when((j >= 2) & (j < steps))
+        def _():
+            x1_copy(j - 2).wait_send()
+            y1_copy(j - 2).wait_send()
+
+        @pl.when((j >= 0) & (j < steps))
+        def _():
+            ring, four = lax.rem(j, 2), lax.rem(j, 4)
+            side_copy(j).wait_recv()
+
+            def store(u, x_to, z_to, total, square):
+                got = s_recv[four, x_to * 4 + z_to].astype(full)
+                both = (total + got[0], square + got[1])
+                for c in range(2):
+                    if z_to < 2 and u < 4:
+                        x1_send[ring, z_to, c] = both[c].astype(low)
+                    elif z_to < 2:
+                        x1_keep[ring, z_to, c] = both[c]
+                    else:
+                        for y_to in range(2):
+                            piece = both[c][y_to * 32 : y_to * 32 + 32]
+                            y1_send[ring, y_to, x_to, z_to - 2, c] = piece.astype(low)
+                            y1_keep[ring, y_to, x_to, z_to - 2, c] = piece
+
+            products(j, me_s, 1 - me_x, store)
+            x1_copy(j).start()
+            y1_copy(j).start()
+
+        j2 = k - 2
+
+        @pl.when((j2 >= 0) & (j2 < steps))
+        def _():
+            ring = lax.rem(j2, 2)
+
+            @pl.when(j2 >= 2)
+            def _():
+                x2_copy(j2 - 2).wait_send()
+                y2_copy(j2 - 2).wait_send()
+
+            x1_copy(j2).wait_recv()
+            here = pl.ds(pl.multiple_of(me_y * 32, 32), 32)
+            there = pl.ds(pl.multiple_of((1 - me_y) * 32, 32), 32)
+            for z_to in range(2):
+                for c in range(2):
+                    two_keep[ring, z_to, c] = x1_keep[ring, z_to, c, here, :] + x1_recv[
+                        j2, z_to, c, here, :
+                    ].astype(full)
+                    y2_send[ring, z_to, c] = (
+                        x1_keep[ring, z_to, c, there, :]
+                        + x1_recv[j2, z_to, c, there, :].astype(full)
+                    ).astype(low)
+            y2_copy(j2).start()
+            y1_copy(j2).wait_recv()
+            for z_to in range(2):
+                two_keep[ring, 2 + z_to] = y1_keep[ring, me_y, me_x, z_to] + y1_recv[
+                    j2, me_x, z_to
+                ].astype(full)
+                x2_send[ring, z_to] = (
+                    y1_keep[ring, me_y, 1 - me_x, z_to]
+                    + y1_recv[j2, 1 - me_x, z_to].astype(full)
+                ).astype(low)
+            x2_copy(j2).start()
+
+        j3 = k - 3
+
+        @pl.when((j3 >= 0) & (j3 < steps))
+        def _():
+            ring = lax.rem(j3, 2)
+
+            @pl.when(j3 >= 2)
+            def _():
+                for d in (1, 2, 3):
+                    z_copy(j3 - 2, d).wait_send()
+
+            y2_copy(j3).wait_recv()
+            x2_copy(j3).wait_recv()
+            for z_to in range(4):
+                got = y2_recv[j3, z_to] if z_to < 2 else x2_recv[j3, z_to - 2]
+                both = two_keep[ring, z_to] + got.astype(full)
+                z_keep[ring, z_to] = both
+                z_send[ring, z_to] = both.astype(low)
+            for d in (1, 2, 3):
+                z_copy(j3, d).start()
+
+        j4 = k - 4
+
+        @pl.when(j4 == 0)
+        def _():
+            sc_local.wait()
+            sc_remote.wait_recv()
+
+        @pl.when((j4 >= 0) & (j4 < steps))
+        def _():
+            ring, li, i = lax.rem(j4, 2), j4 // 9, lax.rem(j4, 9)
+
+            @pl.when(j4 >= 2)
+            def _():
+                for d in (1, 2, 3):
+                    gz_copy(j4 - 2, d).wait_send()
+
+            for d in (1, 2, 3):
+                z_copy(j4, d).wait_recv()
+            got = z_recv[j4].astype(full)
+            both = z_keep[ring, me_z] + got[0] + got[1] + got[2]
+            scale = DECAY * sc_v[li, i] + (1.0 - DECAY) * both[1] / images_all
+            ns_v[li, i] = scale
+            div_v[ring] = (both[0] / weight_ref[...] / (scale + DAMPING)).astype(low)
+            local_copy(j4).start()
+            for d in (1, 2, 3):
+                gz_copy(j4, d).start()
+
+        for li in range(2):
+            @pl.when((j4 == 9 * li + 8) & (me_y == 1 - li))
+            def _():
+                pltpu.make_async_copy(ns_v.at[li], ns_out.at[:, me_y], misc_sem.at[3]).start()
+
+            @pl.when((j4 == 9 * li + 8) & (me_y == li))
+            def _():
+                remote(
+                    ns_v.at[li], ns_out.at[:, me_y], misc_sem.at[4], misc_sem.at[5], to_y
+                ).start()
+
+        j5 = k - 5
+
+        @pl.when((j5 >= 0) & (j5 < steps))
+        def _():
+            @pl.when(j5 >= 2)
+            def _():
+                g1y_copy(j5 - 2).wait_send()
+                g1x_copy(j5 - 2).wait_send()
+
+            local_copy(j5).wait()
+            for d in (1, 2, 3):
+                gz_copy(j5, d).wait_recv()
+            g1y_copy(j5).start()
+            g1x_copy(j5).start()
+
+        j6 = k - 6
+
+        @pl.when((j6 >= 0) & (j6 < steps))
+        def _():
+            @pl.when(j6 >= 2)
+            def _():
+                g2y_copy(j6 - 2).wait_send()
+                g2x_copy(j6 - 2).wait_send()
+
+            g1y_copy(j6).wait_recv()
+            g2x_copy(j6).start()
+            g1x_copy(j6).wait_recv()
+            g2y_copy(j6).start()
+
+        j7 = k - 7
+
+        @pl.when(j7 >= 0)
+        def _():
+            @pl.when(j7 >= 2)
+            def _():
+                gs_copy(j7 - 2).wait_send()
+
+            g2x_copy(j7).wait_recv()
+            g2y_copy(j7).wait_recv()
+            gs_copy(j7).start()
+
+        return carry
+
+    lax.fori_loop(0, steps + 7, step, 0)
+
+    def finish(j, carry):
+        gs_copy(j).wait_recv()
+        return carry
+
+    lax.fori_loop(0, steps, finish, 0)
+    sc_remote.wait_send()
+    li = 1 - me_y
+    pltpu.make_async_copy(ns_v.at[li], ns_out.at[:, me_y], misc_sem.at[3]).wait()
+    ns_remote = remote(ns_v.at[0], ns_out.at[:, 0], misc_sem.at[4], misc_sem.at[5], to_y)
+    ns_remote.wait_send()
+    ns_remote.wait_recv()
+    for j in (steps - 2, steps - 1):
+        for copy in (side_copy, x1_copy, y1_copy, x2_copy, y2_copy):
+            copy(j).wait_send()
+        for copy in (g1y_copy, g1x_copy, g2y_copy, g2x_copy, gs_copy):
+            copy(j).wait_send()
+        for d in (1, 2, 3):
+            z_copy(j, d).wait_send()
+            gz_copy(j, d).wait_send()
+
+
+def statistics(act_turned, grad_turned, scales, weight_all, images_all):
+    images = act_turned.shape[2] // 128
+    dma = pltpu.SemaphoreType.DMA
+    low, full = jnp.bfloat16, jnp.float32
+    tile, piece = (2, 64, 256), (2, 32, 256)
+    any_spec = pl.BlockSpec(memory_space=pl.ANY)
+    divided, new_scales = pl.pallas_call(
+        functools.partial(statistics_kernel, images, images_all),
+        out_shape=[
+            jax.ShapeDtypeStruct((2, 2, 2, 4, 9, 2, 32, 256), low),
+            jax.ShapeDtypeStruct((9, 2, 32, 256), full),
+        ],
+        in_specs=[any_spec, any_spec, any_spec, pl.BlockSpec(memory_space=pltpu.VMEM)],
+        out_specs=[any_spec, any_spec],
+        scratch_shapes=[
+            pltpu.VMEM((2, 512, images * 128), low),
+            pltpu.VMEM((2, 3 * images, 160, 512), low),
+            pltpu.VMEM((2, 9, 32, 256), full),
+            pltpu.VMEM((2, 9, 32, 256), full),
+            pltpu.VMEM((2, 32, 256), low),
+            pltpu.VMEM((2, 8) + tile, low),
+            pltpu.VMEM((4, 8) + tile, low),
+            pltpu.VMEM((2, 2) + tile, low),
+            pltpu.VMEM((18, 2) + tile, low),
+            pltpu.VMEM((2, 2) + tile, full),
+            pltpu.VMEM((2, 2, 2, 2) + piece, low),
+            pltpu.VMEM((18, 2, 2) + piece, low),
+            pltpu.VMEM((2, 2, 2, 2) + piece, full),
+            pltpu.VMEM((2, 2) + piece, low),
+            pltpu.VMEM((18, 2) + piece, low),
+            pltpu.VMEM((2, 2) + piece, low),
+            pltpu.VMEM((18, 2) + piece, low),
+            pltpu.VMEM((2, 4) + piece, full),
+            pltpu.VMEM((2, 4) + piece, low),
+            pltpu.VMEM((18, 3) + piece, low),
+            pltpu.VMEM((2, 4) + piece, full),
+            dma((2, 4)),
+            dma((6,)),
+            dma((2,)),
+            dma((10, 2)),
+            dma((4,)),
+            dma((9, 18)),
+            dma((2, 3)),
+            dma((18, 3)),
+            dma((2, 3)),
+            dma((18, 3)),
+        ],
+        name="statistics",
+        compiler_params=pltpu.CompilerParams(
+            collective_id=0, has_side_effects=True, vmem_limit_bytes=63 * 2**20
+        ),
+    )(
+        act_turned,
+        grad_turned,
+        scales.reshape(9, 2, 32, 256),
+        jnp.full((1, 256), weight_all, full),
+    )
+    return divided.reshape(2, 18, 512, 256), new_scales.reshape(576, 256)
+
+
+def turned_operands(inputs, grad_low, basis_in, basis_out):
+    images, side_len, _, width = inputs.shape
+    wide = jnp.pad(inputs, ((0, 0), (0, 0), (0, 8), (0, 0))).reshape(images * 128, width)
+    act = lax.dot_general(
+        basis_in, wide, (((0,), (1,)), ((), ())), preferred_element_type=jnp.float32
+    ).astype(jnp.bfloat16)
+    grad = jnp.einsum(
+        "npqo,oj->npqj", grad_low, basis_out, preferred_element_type=jnp.float32
+    ).astype(jnp.bfloat16)
+    zero = ((0, 0), (1, 1))
+    shifts = [
+        jnp.pad(grad[:, :, 1:], zero + ((0, 9), (0, 0))),
+        jnp.pad(grad, zero + ((0, 8), (0, 0))),
+        jnp.pad(grad[:, :, :7], zero + ((1, 8), (0, 0))),
+    ]
+    return act, jnp.concatenate([s.reshape(images, 160, width) for s in shifts], axis=0)
+
+
+def owned_kernel(
+    which, divided, rows_ref, cols_ref, w_ref, m_ref, v_ref, new_w, new_m, new_v
+):
+    low, full = jnp.bfloat16, jnp.float32
+    held = which[1, pl.program_id(0)].astype(full)
+    rows = rows_ref[0]
+    turned = [
+        jnp.dot(rows, divided[s, 0], preferred_element_type=full).astype(low) for s in range(2)
+    ]
+    gradient = lax.dot_general(
+        jnp.concatenate(turned, axis=1),
+        cols_ref[0],
+        (((1,), (1,)), ((), ())),
+        preferred_element_type=full,
+    )
+    new_w[0], new_m[0], new_v[0] = adamw(
+        w_ref[0], m_ref[0], v_ref[0], gradient * held, RATE_CONV
+    )
+
+
+def owned_update(divided, basis_in, basis_out, master, moment1, moment2, which):
+    slots, half, width = master.shape
+    block = pl.BlockSpec((1, half, width), lambda q, which: (q, 0, 0))
+    return pl.pallas_call(
+        owned_kernel,
+        grid_spec=pltpu.PrefetchScalarGridSpec(
+            num_scalar_prefetch=1,
+            grid=(slots,),
+            in_specs=[
+                pl.BlockSpec((2, 1, width, half), lambda q, which: (0, which[0, q], 0, 0)),
+                pl.BlockSpec((1, half, width), lambda q, which: (which[0, q] // TAPS, which[2, q], 0)),
+                pl.BlockSpec((1, width, width), lambda q, which: (which[0, q] // TAPS, 0, 0)),
+                block,
+                block,
+                block,
+            ],
+            out_specs=[block, block, block],
+        ),
+        out_shape=[jax.ShapeDtypeStruct(master.shape, jnp.float32)] * 3,
+        name="owned_update",
+        compiler_params=pltpu.CompilerParams(vmem_limit_bytes=32 * 2**20),
+    )(which, divided, basis_in, basis_out, master, moment1, moment2)
 
 
 def shards(
@@ -150,6 +682,7 @@
     loss_all, head_all = lax.psum((loss_local, grad_head), ("dp", "side", "blk"))
     d_pooled = jnp.dot(d_logits, head_low.astype(jnp.float32).T, precision=lax.Precision.HIGHEST)
     d_act = d_pooled[:, None, None, :] / pixels[:, None, None, None] * mask_four
+    fast = (n_dp, n_side, n_blk) == (4, 2, 4) and block_rows == 576
     terms = [None] * L
     grad_norm = [None] * L
     for layer in reversed(range(L)):
@@ -174,6 +707,9 @@
         grad_low = d_conv.astype(jnp.bfloat16)
         if layer > 0:
             d_act = conv_backward(grad_low, kernels[layer])
+        if fast:
+            terms[layer] = turned_operands(inputs, grad_low, basis_in[layer], basis_out[layer])
+            continue
         act_proj = jnp.einsum(
             "npqc,ci->npqi", inputs, basis_in[layer], preferred_element_type=jnp.float32
         ).astype(jnp.bfloat16)
@@ -181,37 +717,58 @@
             "npqo,oj->npqj", grad_low, basis_out[layer], preferred_element_type=jnp.float32
         ).astype(jnp.bfloat16)
         terms[layer] = tap_sums(act_proj, grad_proj)
-    whole = jnp.stack(terms).reshape(n_dp, n_blk, block_rows, 2, 2, half)
-    whole = whole.transpose(0, 4, 1, 2, 3, 5).reshape(n_dp * 2 * n_blk * block_rows, 2 * half)
-    reduced = lax.psum_scatter(whole, ("dp", "side", "blk"), scatter_dimension=0, tiled=True)
-    proj_sum = reduced[:, :half]
-    proj_square = reduced[:, half:]
-    new_scales = DECAY * scales + (1.0 - DECAY) * proj_square / images_all
-    divided = (proj_sum / weight_all / (new_scales + DAMPING)).astype(jnp.bfloat16)
-    spread = lax.all_gather(divided, ("dp", "side", "blk"), axis=0, tiled=True)
-    spread = spread.reshape(n_dp, 2, n_blk, block_rows, half).transpose(0, 2, 3, 1, 4)
-    precond_all = spread.reshape(matrices, width, width)
     slot_ids = lax.axis_index("blk") * slots_dev + jnp.arange(slots_dev)
-    owned = (slot[None, :] == slot_ids[:, None]).astype(jnp.bfloat16)
-    chosen = jnp.einsum(
-        "qm,mij->qij", owned, precond_all, preferred_element_type=jnp.float32
-    ).astype(jnp.bfloat16)
-    layer_hot = (index[:, None] // TAPS == jnp.arange(L)[None, :]).astype(jnp.bfloat16)
-    slot_layer = jnp.dot(owned, layer_hot, preferred_element_type=jnp.float32).astype(jnp.bfloat16)
-    half_rows = lax.dynamic_slice_in_dim(
-        basis_in, lax.axis_index("side") * master.shape[1], master.shape[1], 1
-    )
-    rows_slot = jnp.einsum(
-        "ql,lci->qci", slot_layer, half_rows, preferred_element_type=jnp.float32
-    ).astype(jnp.bfloat16)
-    cols_slot = jnp.einsum(
-        "ql,loj->qoj", slot_layer, basis_out, preferred_element_type=jnp.float32
-    ).astype(jnp.bfloat16)
-    turned = jnp.einsum(
-        "qci,qij->qcj", rows_slot, chosen, preferred_element_type=jnp.float32
-    ).astype(jnp.bfloat16)
-    slot_grad = jnp.einsum("qcj,qoj->qco", turned, cols_slot, preferred_element_type=jnp.float32)
-    new_master, new_moment1, new_moment2 = adamw(master, moment1, moment2, slot_grad, RATE_CONV)
+    hits = slot[None, :] == slot_ids[:, None]
+    which = jnp.stack(
+        [
+            jnp.sum(jnp.where(hits, index[None, :], 0), axis=1),
+            jnp.sum(hits.astype(jnp.int32), axis=1),
+            jnp.full((slots_dev,), lax.axis_index("side"), jnp.int32),
+        ]
+    ).astype(jnp.int32)
+    if fast:
+        divided, new_scales = statistics(
+            jnp.stack([terms[1][0], terms[0][0]]),
+            jnp.stack([terms[1][1], terms[0][1]]),
+            scales,
+            weight_all,
+            images_all,
+        )
+        new_master, new_moment1, new_moment2 = owned_update(
+            divided, basis_in, basis_out, master, moment1, moment2, which
+        )
+    else:
+        whole = jnp.stack(terms).reshape(n_dp, n_blk, block_rows, 2, 2, half)
+        whole = whole.transpose(0, 4, 1, 2, 3, 5).reshape(n_dp * 2 * n_blk * block_rows, 2 * half)
+        reduced = lax.psum_scatter(whole, ("dp", "side", "blk"), scatter_dimension=0, tiled=True)
+        proj_sum = reduced[:, :half]
+        proj_square = reduced[:, half:]
+        new_scales = DECAY * scales + (1.0 - DECAY) * proj_square / images_all
+        divided = (proj_sum / weight_all / (new_scales + DAMPING)).astype(jnp.bfloat16)
+        spread = lax.all_gather(divided, ("dp", "side", "blk"), axis=0, tiled=True)
+        spread = spread.reshape(n_dp, 2, n_blk, block_rows, half).transpose(0, 2, 3, 1, 4)
+        precond_all = spread.reshape(matrices, width, width)
+        slot_ids = lax.axis_index("blk") * slots_dev + jnp.arange(slots_dev)
+        owned = (slot[None, :] == slot_ids[:, None]).astype(jnp.bfloat16)
+        chosen = jnp.einsum(
+            "qm,mij->qij", owned, precond_all, preferred_element_type=jnp.float32
+        ).astype(jnp.bfloat16)
+        layer_hot = (index[:, None] // TAPS == jnp.arange(L)[None, :]).astype(jnp.bfloat16)
+        slot_layer = jnp.dot(owned, layer_hot, preferred_element_type=jnp.float32).astype(jnp.bfloat16)
+        half_rows = lax.dynamic_slice_in_dim(
+            basis_in, lax.axis_index("side") * master.shape[1], master.shape[1], 1
+        )
+        rows_slot = jnp.einsum(
+            "ql,lci->qci", slot_layer, half_rows, preferred_element_type=jnp.float32
+        ).astype(jnp.bfloat16)
+        cols_slot = jnp.einsum(
+            "ql,loj->qoj", slot_layer, basis_out, preferred_element_type=jnp.float32
+        ).astype(jnp.bfloat16)
+        turned = jnp.einsum(
+            "qci,qij->qcj", rows_slot, chosen, preferred_element_type=jnp.float32
+        ).astype(jnp.bfloat16)
+        slot_grad = jnp.einsum("qcj,qoj->qco", turned, cols_slot, preferred_element_type=jnp.float32)
+        new_master, new_moment1, new_moment2 = adamw(master, moment1, moment2, slot_grad, RATE_CONV)
     new_norm, new_norm_m, new_norm_v = adamw(
         norm_params, norm_m, norm_v, jnp.stack(grad_norm) / weight_all, RATE_NORM
     )

time: 1450 us -> 853 us (0.59)
  waiting for transfers between devices: 601 us -> 175 us
  matrix products: 331 us -> 150 us
  Pallas kernels: 0 us -> 172 us
  local copies, waits for them, and re-layouts: 223 us -> 77.5 us
    reduce_scatter x1 -> x0, waiting for transfers between devices: 349 us -> none  [shards(): lax.psum_scatter(whole, ('dp', 'side', 'blk'), scatter_dimension=0, tiled...]
    dot_general x27 -> x4, matrix products: 210 us -> 20.8 us  [the longest x2 13.4 us: turned_operands(): lax.dot_general(basis_in, wide, (((0,), (1,)), ((), ())), preferred_eleme...]
    pallas_call x0 -> x2, Pallas kernels: none -> 172 us  [the longest x1 159 us: statistics(): pl.pallas_call(functools.partial(statistics_kernel, images, images_all),...]
    reshape x3 -> x0, local copies, waits for them, and re-layouts: 81.8 us -> none  [the longest x1 47.8 us: shards(): whole = jnp.stack(terms).reshape(n_dp, n_blk, block_rows, 2, 2, half)]
    all_gather x1 -> x0, waiting for transfers between devices: 70.4 us -> none  [shards(): spread = lax.all_gather(divided, ('dp', 'side', 'blk'), axis=0, tiled=True)]
    transpose x1 -> x0, local copies, waits for them, and re-layouts: 52.2 us -> none  [shards(): whole.transpose(0, 4, 1, 2, 3, 5)]
    unnamed x231 -> x137, local copies, waits for them, and re-layouts: 53.2 us -> 17.2 us
    pad x0 -> x8, local copies, waits for them, and re-layouts: none -> 17.9 us  [the longest x2 7.23 us: turned_operands(): jnp.pad(grad[:, :, :7], zero + ((1, 8), (0, 0)))]
  transfers between devices with their start and end apart: 3 -> 1, of which waited for: 3 -> 1; matrix products, arithmetic and copies ran while one was open for 1% -> 1% of each run, Pallas kernels for 0% -> 0%
where the time goes in v2:
time: 853 us; the launch traced here: 849 us
  waiting for transfers between devices  175 us (21%)
  Pallas kernels  172 us (20%)
  blocking collectives  161 us (19%)
  matrix products  150 us (18%)
  other arithmetic  97.9 us (11%)
  local copies, waits for them, and re-layouts  77.5 us (9%)
  between operations  15.7 us (2%)
    all_gather x1, waiting for transfers between devices, shards(): lax.all_gather(master.astype(jnp.bfloat16), ('side', 'blk'), axis=0, tile...  175 us
    pallas_call x1, Pallas kernels, statistics(): pl.pallas_call(functools.partial(statistics_kernel, images, images_all),...  159 us
    psum x2, blocking collectives, shards(): lax.psum((jnp.sum(masked, axis=(0, 1, 2)), jnp.sum(masked * conv_out, axi...  79.9 us
    dot_general x18, matrix products, conv_forward(): jnp.einsum('npqc,co->npqo', shifted, kernel[tap], preferred_element_type=...  73.5 us
    psum x1, blocking collectives, shards(): lax.psum((loss_local, grad_head), ('dp', 'side', 'blk'))  41.5 us
    psum x1, blocking collectives, shards(): lax.psum((jnp.sum(d_pre * normed, axis=(0, 1, 2)), jnp.sum(d_pre, axis=(0...  39.4 us
    another operation x3, other arithmetic, shards(): jnp.stack([terms[1][1], terms[0][1]])  35.8 us
    slice x1, local copies, waits for them, and re-layouts, conv_forward(): kernel[tap]  35.3 us
  transfers between devices with their start and end apart: 1, of which 1 were waited for; matrix products, arithmetic and copies ran while one was open for 1% of the time, Pallas kernels for 0%

profile of v2, /device:TPU:0, one launch (start us, length us, event | category | flops | bytes accessed | tf_op | source)
XLA Modules:
  0.0 849.1 jit_solution(15622913888769565609)
XLA Ops:
  7.3 4.5 convert_element_type.107
  18.2 6.7 fusion.6
  24.9 175.2 %all-gather.2.cloned.1.call-done = bf16[80,256,512]{2,1,0:T(8,128)(2,1)} async-done(((bf16[10,256,512]{2,1,0:T(8,128)(2,1)}), bf16[80,256,512]{2,1,0:T(8,128)(2,1)}) %all-gather.2.cloned.1.call-update) | async-done | bytes 20971536 | tf_op jit(solution)/shard_map/all_gather | solution.py:640
  200.1 25.0 %fusion.2 = bf16[18,2,256,512]{3,0,2,1:T(8,128)(2,1)} fusion(bf16[2,40,256,512]{3,2,1,0:T(8,128)(2,1)} %bitcast.162, s32[18]{0:T(128)S(1)} %multiply_add_fusion.2), kind=kOutput, calls=%fused_computation.23 | convolution fusion | flops 382206656 | bytes 30408776 | tf_op jit(solution)/shard_map/ms,hsrc->mhrc/dot_general | solution.py:643
  225.1 35.3 %fusion.71 = (bf16[1,2,256,512]{3,0,2,1:T(2,128)(2,1)}, bf16[1,2,256,512]{3,0,2,1:T(2,128)(2,1)}, bf16[1,2,256,512]{3,0,2,1:T(2,128)(2,1)}, bf16[1,2,256,512]{3,...) fusion(bf16[18,2,256,512]{3,0,2,1:T(8,128)(2,1)} %fusion.2), kind=kLoop, calls=%fused_computation.156 | loop fusion | bytes 18874368 | tf_op jit(solution)/shard_map/slice | solution.py:48
  287.1 12.8 %multiply_reduce_fusion.1 = (f32[512]{0:T(512)S(1)}, f32[512]{0:T(512)S(1)}, f32[32,8,8,512]{3,2,1,0:T(8,128)}) fusion(f32[32,8,8]{2,1,0:T(8,128)S(1)} %select_convert_fusion, bf16[512,512,1,1]{1,0,3,2:T(8,128)(2,1)S(1)} %bitcast.200, bf16[32,8,8,512]{3,2,1,0:T(8,128)(2,1)S(1)} %copy-done.10, f32[32,8,8,512]{3,2,1,0:T(8,128)} %fusion.20, ...), kind=kOutput, calls=%fused_computation.27 | convolution fusion | flops 1086323712 | bytes 40382464 | tf_op jit(solution)/shard_map/npqc,co->npqo/dot_general | solution.py:48
  299.9 38.8 %all-reduce.22 = (f32[512]{0:T(512)S(1)}, f32[]{:T(128)}, f32[512]{0:T(512)S(1)}) all-reduce(f32[512]{0:T(512)S(1)} %get-tuple-element.27, f32[]{:T(128)} %get-tuple-element.33, f32[512]{0:T(512)S(1)} %get-tuple-element.26), channel_id=1, replica_groups=mesh['dp'=4,'side'=2,'blk'=4] {'dp','side','blk'}, use_global_device_ids=true, to_apply=%region_7.8 | all-reduce | flops 1025 | bytes 8200 | tf_op jit(solution)/shard_map/psum | solution.py:660
  367.4 13.0 %multiply_reduce_fusion = (f32[512]{0:T(512)S(1)}, f32[512]{0:T(512)S(1)}, f32[32,8,8,512]{3,2,1,0:T(8,128)}) fusion(f32[32,8,8]{2,1,0:T(8,128)S(1)} %select_convert_fusion, bf16[512,512,1,1]{1,0,3,2:T(8,128)(2,1)S(1)} %bitcast.188, bf16[32,8,8,512]{3,2,1,0:T(8,128)(2,1)S(1)} %multiply_convert_fusion.2, f32[32,8,8,512]{3,2,1,0:T(8,128)} %fusion.27, ...), kind=kOutput, calls=%fused_computation.25 | convolution fusion | flops 1086323712 | bytes 40382464 | tf_op jit(solution)/shard_map/npqc,co->npqo/dot_general | solution.py:48
  380.4 41.0 %all-reduce.21 = (f32[512]{0:T(512)S(1)}, f32[512]{0:T(512)S(1)}) all-reduce(f32[512]{0:T(512)S(1)} %get-tuple-element.25, f32[512]{0:T(512)S(1)} %get-tuple-element.24), channel_id=1, replica_groups=mesh['dp'=4,'side'=2,'blk'=4] {'dp','side','blk'}, use_global_device_ids=true, to_apply=%region_11.12 | all-reduce | flops 1024 | bytes 8192 | tf_op jit(solution)/shard_map/psum | solution.py:660
  422.2 3.5 multiply_reduce_fusion.4
  429.2 39.4 %all-reduce.20 = (f32[512]{0:T(512)S(1)}, f32[512]{0:T(512)S(1)}) all-reduce(f32[512]{0:T(512)S(1)} %get-tuple-element.23, f32[512]{0:T(512)S(1)} %get-tuple-element.22), channel_id=1, replica_groups=mesh['dp'=4,'side'=2,'blk'=4] {'dp','side','blk'}, use_global_device_ids=true, to_apply=%region_24.25 | all-reduce | flops 1024 | bytes 8192 | tf_op jit(solution)/shard_map/psum | solution.py:692
  469.2 5.8 multiply_convert_fusion.1
  475.0 3.4 fusion.78
  478.4 3.4 fusion.79
  485.0 3.4 fusion.81
  488.4 3.4 fusion.82
  491.8 3.3 fusion.83
  495.1 3.3 fusion.84
  498.4 3.3 fusion.85
  501.7 3.3 fusion.86
  513.7 12.1 %pad_add_fusion = f32[32,10,10,512]{3,2,1,0:T(8,128)} fusion(f32[32,8,8,512]{3,2,1,0:T(8,128)} %fusion.80, f32[32,8,8,512]{3,2,1,0:T(8,128)} %fusion.79, f32[32,8,8,512]{3,2,1,0:T(8,128)} %fusion.78), kind=kLoop, calls=%fused_computation.21 | loop fusion | flops 3276800 | bytes 19136512 | tf_op jit(solution)/shard_map/add | solution.py:63
  525.9 14.6 %fusion.67 = (f32[512]{0:T(512)S(1)}, f32[512]{0:T(512)S(1)}, f32[32,8,8,512]{3,2,1,0:T(8,128)}) fusion(f32[512]{0:T(512)S(1)} %get-tuple-element.86, f32[32,8,8,512]{3,2,1,0:T(8,128)S(1)} %copy-done.12, f32[512]{0:T(512)S(1)} %get-tuple-element.85, f32[512]{0:T(512)S(1)} %bitcast.215, f32[512]{0:T(512)S(1)} %bitcast.211, ...), kind=kLoop, calls=%fused_computation.155 | loop fusion | flops 23067648 | bytes 37769216 | tf_op jit(solution)/shard_map/reduce_sum | solution.py:693
  540.4 41.5 %all-reduce.19 = (f32[]{:T(128)}, f32[]{:T(128)}, f32[512]{0:T(512)S(1)}, f32[512]{0:T(512)S(1)}, f32[513,10]{0,1:T(8,128)S(1)}) all-reduce(f32[]{:T(128)S(6)} %neg.14, f32[]{:T(128)} %get-tuple-element.36, f32[512]{0:T(512)S(1)} %get-tuple-element.29, ...), channel_id=1, replica_groups=mesh['dp'=4,'side'=2,'blk'=4] {'dp','side','blk'}, use_global_device_ids=true, to_apply=%region_18.19 | all-reduce | flops 6156 | bytes 49248 | tf_op jit(solution)/shard_map/psum | solution.py:682
  582.6 6.0 fusion.29
  599.7 5.6 pad.89
  605.3 6.6 fusion.5
  612.0 7.3 maximum_bitcast_fusion
  619.3 6.9 maximum_bitcast_fusion.1
  626.2 21.6 %pad_maximum_fusion.gr_hbm = bf16[2,96,160,512]{3,2,1,0:T(8,128)(2,1)} fusion(bf16[1,96,160,512]{3,2,1,0:T(8,128)(2,1)} %maximum_bitcast_fusion.1, bf16[1,96,160,512]{3,2,1,0:T(8,128)(2,1)} %maximum_bitcast_fusion), kind=kLoop, calls=%fused_computation | loop fusion | flops 15728640 | bytes 62914560 | tf_op jit(solution)/shard_map/stack | solution.py:732
  647.8 7.5 pad_maximum_fusion.1.at_hbm
  656.6 158.7 %statistics.1 = (bf16[2,2,2,4,9,2,32,256]{7,6,5,4,3,2,1,0:T(8,128)(2,1)}, f32[9,2,32,256]{3,2,1,0:T(8,128)}) custom-call(bf16[2,512,4096]{2,1,0:T(8,128)(2,1)} %pad_maximum_fusion.1.at_hbm, bf16[2,96,160,512]{3,2,1,0:T(8,128)(2,1)} %pad_maximum_fusion.gr_hbm, f32[9,2,32,256]{3,2,1,0:T(8,128)} %bitcast.202, f32[1,256]{1,0:T(1,128)} %broadcast_in_dim.53.weight_ref), custom_call_target="tpu_custom_call" | custom-call | tf_op jit(solution)/shard_map/statistics/pallas_call | solution.py:491
  827.8 13.3 %owned_update.1 = (f32[10,256,512]{2,1,0:T(8,128)}, f32[10,256,512]{2,1,0:T(8,128)}, f32[10,256,512]{2,1,0:T(8,128)}) custom-call(s32[3,10]{1,0:T(4,128)S(1)} %add_add_fusion.2.which, bf16[2,18,512,256]{3,2,1,0:T(8,128)(2,1)} %bitcast.171, bf16[2,512,512]{2,1,0:T(8,128)(2,1)S(1)} %copy-done.4, bf16[2,512,512]{2,1,0:T(8,128)(2,1)S(1)} %copy-done.6, ...), custom_call_target="tpu_custom_call" | custom-call | tf_op jit(solution)/shard_map/owned_update/pallas_call | solution.py:586
  (204 shorter events, 103.6 us)
Async XLA Ops:
  7.2 4.6 copy-start.53
  7.2 4.6 copy-start.54
  7.2 4.7 copy-start.55
  7.2 4.9 copy-start.44
  7.2 192.9 %all-gather.2.cloned.1.call-start = ((), (), s32[]{:S(2)}) async-start(), calls=%async_computation | async-start | bytes 23592960 | tf_op jit(solution)/shard_map/all_gather | solution.py:640
  13.9 4.2 copy-start.49
  13.9 4.2 copy-start.3
  225.1 36.7 %copy-start.10 = (bf16[32,8,8,512]{3,2,1,0:T(8,128)(2,1)S(1)}, bf16[32,8,8,512]{3,2,1,0:T(8,128)(2,1)}, u32[]{:S(2)}) copy-start(bf16[32,8,8,512]{3,2,1,0:T(8,128)(2,1)} %copy-done.9) | copy-start | bytes 6291460
  283.5 3.3 copy-start.36
  342.5 24.8 %copy-start.7 = (bf16[32,8,8,512]{3,2,1,0:T(8,128)(2,1)}, bf16[32,8,8,512]{3,2,1,0:T(8,128)(2,1)S(1)}, u32[]{:S(2)}) copy-start(bf16[32,8,8,512]{3,2,1,0:T(8,128)(2,1)S(1)} %multiply_convert_fusion.2) | copy-start | bytes 6291460
  347.0 3.4 copy-start.34
  350.4 3.4 copy-start.33
  350.5 3.4 copy-start.17
  360.4 3.4 copy-start.30
  360.5 3.4 copy-start.23
  363.8 3.4 copy-start.29
  363.9 3.4 copy-start.25
  367.4 13.0 %copy-start.27 = (bf16[1,2,256,512]{3,2,0,1:T(8,128)(2,1)}, bf16[1,2,256,512]{3,2,0,1:T(8,128)(2,1)S(1)}, u32[]{:S(2)}) copy-start(bf16[1,2,256,512]{3,2,0,1:T(8,128)(2,1)S(1)} %copy.84) | copy-start | bytes 1572868
  421.4 5.2 copy-start.11
  485.0 3.4 copy-start.20
  488.4 3.4 copy-start.22
  501.7 3.3 copy-start.5
  513.7 12.2 %copy-start.12 = (f32[32,8,8,512]{3,2,1,0:T(8,128)S(1)}, f32[32,8,8,512]{3,2,1,0:T(8,128)}, u32[]{:S(2)}) copy-start(f32[32,8,8,512]{3,2,1,0:T(8,128)} %get-tuple-element.87) | copy-start | bytes 12582916
  599.7 12.3 %slice-start = ((s8[5242880]{0:T(1024)(128)(4,1)}), s8[4194304]{0:T(1024)(128)(4,1)S(1)}, s32[]{:S(2)}) async-start(s8[5242880]{0:T(1024)(128)(4,1)} %bitcast.163), calls=%async_computation.1 | async-start | bytes 8388608
  605.3 6.7 slice-start.1
  612.0 7.3 copy-start.13
  656.5 158.8 %copy-start.47 = (f32[513,10]{0,1:T(8,128)S(1)}, f32[513,10]{0,1:T(8,128)}, u32[]{:S(2)}) copy-start(f32[513,10]{0,1:T(8,128)} %param.32) | copy-start | bytes 61564
  656.5 158.8 %copy-start.48 = (f32[513,10]{0,1:T(8,128)S(1)}, f32[513,10]{0,1:T(8,128)}, u32[]{:S(2)}) copy-start(f32[513,10]{0,1:T(8,128)} %param.33) | copy-start | bytes 61564
  656.5 160.1 %copy-start.50 = (f32[2,2,512]{2,1,0:T(2,128)S(1)}, f32[2,2,512]{2,1,0:T(2,128)}, u32[]{:S(2)}) copy-start(f32[2,2,512]{2,1,0:T(2,128)} %param.28) | copy-start | bytes 24580
  656.5 160.1 %copy-start.51 = (f32[2,2,512]{2,1,0:T(2,128)S(1)}, f32[2,2,512]{2,1,0:T(2,128)}, u32[]{:S(2)}) copy-start(f32[2,2,512]{2,1,0:T(2,128)} %param.29) | copy-start | bytes 24580
  656.5 160.1 %copy-start.52 = (f32[2,2,512]{2,1,0:T(2,128)S(1)}, f32[2,2,512]{2,1,0:T(2,128)}, u32[]{:S(2)}) copy-start(f32[2,2,512]{2,1,0:T(2,128)} %param.30) | copy-start | bytes 24580
  827.8 13.3 %copy-start.45 = (f32[9,2,32,256]{3,2,1,0:T(8,128)S(1)}, f32[9,2,32,256]{3,2,1,0:T(8,128)}, u32[]{:S(2)}) copy-start(f32[9,2,32,256]{3,2,1,0:T(8,128)} %get-tuple-element.17) | copy-start | bytes 1769476
  (28 other events, 75.2 us)
Sparse Core Ops, SparseCore 0:
  11.9 188.1 all-gather.1

commit v3 on v2

--- a/solution.py
+++ b/solution.py
@@ -77,6 +77,675 @@
 
 
 MESH = pl.DeviceIdType.MESH
+
+
+def sweep_kernel(
+    classes,
+    feats_ref,
+    group_ref,
+    own_slot,
+    own_flag,
+    master_hbm,
+    params_ref,
+    head_ref,
+    bias_ref,
+    hot_ref,
+    weight_ref,
+    image_group,
+    basis_in_ref,
+    basis_out_ref,
+    at_out,
+    gr_out,
+    total_out,
+    norm_out,
+    head_out,
+    w_full,
+    xpad,
+    conv_a,
+    conv_b,
+    d_buf,
+    at_v,
+    n_pad,
+    gr_v,
+    piece,
+    w_own,
+    w_left,
+    w_right,
+    w_back,
+    basis_t,
+    small_one,
+    small_two,
+    head_one,
+    head_two,
+    out_sem,
+    g_ss,
+    g_rs,
+    one_ss,
+    one_rs,
+    two_ss,
+    two_rs,
+):
+    low, full = jnp.bfloat16, jnp.float32
+    highest = lax.Precision.HIGHEST
+    dp, me_s, me_z = lax.axis_index("dp"), lax.axis_index("side"), lax.axis_index("blk")
+    me_y, me_x = dp // 2, lax.rem(dp, 2)
+    to_s = (dp, 1 - me_s, me_z)
+    to_x = (me_y * 2 + 1 - me_x, me_s, me_z)
+    to_y = ((1 - me_y) * 2 + me_x, me_s, me_z)
+    dp_x, dp_y = me_y * 2 + 1 - me_x, (1 - me_y) * 2 + me_x
+    dp_xy = (1 - me_y) * 2 + 1 - me_x
+    to_right = (dp, me_s, lax.rem(me_z + 1, 4))
+    to_left = (dp, me_s, lax.rem(me_z + 3, 4))
+    images, width = 32, 512
+    matrices = 2 * TAPS
+
+    def remote(src, dst, send, recv, target):
+        return pltpu.make_async_remote_copy(
+            src_ref=src,
+            dst_ref=dst,
+            send_sem=send,
+            recv_sem=recv,
+            device_id=target,
+            device_id_type=MESH,
+        )
+
+    piece_copy = pltpu.make_async_copy(
+        master_hbm.at[:, pl.ds(pl.multiple_of(dp * 64, 64), 64)], piece, out_sem.at[0]
+    )
+    piece_copy.start()
+
+    near = [(a, b) for a in range(4) for b in range(2) if a or b]
+    barrier = pltpu.get_barrier_semaphore()
+
+    def near_id(a, b):
+        return lax.rem(dp + a, 4), lax.rem(me_s + b, 2)
+
+    for a, b in near:
+        other, core = near_id(a, b)
+        pl.semaphore_signal(barrier, inc=1, device_id=(other, core, me_z), device_id_type=MESH)
+    for d in (1, 2, 3):
+        pl.semaphore_signal(
+            barrier, inc=1, device_id=(dp, me_s, lax.rem(me_z + d, 4)), device_id_type=MESH
+        )
+
+    piece_copy.wait()
+
+    def own(m, carry):
+        value = piece[own_slot[m]] * own_flag[m].astype(full)
+        w_own[m] = value.astype(low)
+        return carry
+
+    lax.fori_loop(0, matrices, own, 0)
+
+    @pl.when(me_z == 0)
+    def _():
+        w_left[...] = jnp.zeros_like(w_left)
+
+    @pl.when(me_z == 3)
+    def _():
+        w_right[...] = jnp.zeros_like(w_right)
+
+    pl.semaphore_wait(barrier, 10)
+
+    def right_copy(m):
+        return remote(w_left.at[m], w_left.at[m], g_ss.at[0, m], g_rs.at[0, m], to_right)
+
+    def left_copy(m):
+        return remote(w_back.at[m], w_right.at[m], g_ss.at[1, m], g_rs.at[1, m], to_left)
+
+    def x_copy(m):
+        part = w_full.at[m, me_s, dp]
+        return remote(part, part, g_ss.at[2, m], g_rs.at[2, m], to_x)
+
+    def y_copy(m):
+        part = w_full.at[m, me_s, dp]
+        return remote(part, part, g_ss.at[3, m], g_rs.at[3, m], to_y)
+
+    def even_copy(m):
+        part = w_full.at[m, me_s, dp_x]
+        return remote(part, part, g_ss.at[4, m], g_rs.at[4, m], to_y)
+
+    def odd_copy(m):
+        part = w_full.at[m, me_s, dp_y]
+        return remote(part, part, g_ss.at[4, m], g_rs.at[4, m], to_x)
+
+    def core_copy(m):
+        part = w_full.at[m, me_s]
+        return remote(part, part, g_ss.at[5, m], g_rs.at[5, m], to_s)
+
+    def flow_right(m):
+        @pl.when((m >= 0) & (m < matrices))
+        def _():
+            @pl.when(me_z > 0)
+            def _():
+                right_copy(m).wait_recv()
+
+            w_left[m] = w_left[m] + w_own[m]
+
+            @pl.when(me_z < 3)
+            def _():
+                right_copy(m).start()
+
+    def flow_left(m):
+        @pl.when((m >= 0) & (m < matrices))
+        def _():
+            @pl.when(me_z < 3)
+            def _():
+                left_copy(m).wait_recv()
+
+            w_back[m] = w_right[m] + w_own[m]
+
+            @pl.when(me_z > 0)
+            def _():
+                left_copy(m).start()
+
+    early_right = me_z < 2
+
+    def gather(t):
+        flow_right(jnp.where(early_right, t, t - 2))
+        flow_left(jnp.where(early_right, t - 2, t))
+        m = t - 2
+
+        @pl.when((m >= 0) & (m < matrices))
+        def _():
+            w_full[m, me_s, dp] = w_left[m] + w_right[m]
+            x_copy(m).start()
+            y_copy(m).start()
+
+        m4 = t - 4
+
+        @pl.when((m4 >= 0) & (m4 < matrices))
+        def _():
+            x_copy(m4).wait_recv()
+            y_copy(m4).wait_recv()
+
+            @pl.when(lax.rem(m4, 2) == 0)
+            def _():
+                even_copy(m4).start()
+
+            @pl.when(lax.rem(m4, 2) == 1)
+            def _():
+                odd_copy(m4).start()
+
+        m6 = t - 6
+
+        @pl.when((m6 >= 0) & (m6 < matrices))
+        def _():
+            even_copy(m6).wait_recv()
+            core_copy(m6).start()
+
+    def weights(m):
+        return w_full[m].reshape(width, width)
+
+    def inner(p, q):
+        return jnp.where((p < 4) & (q < 4), 1.0, 0.0).astype(full)
+
+    def mask_of(p, q, rows=slice(None)):
+        return jnp.maximum(group_ref[rows, :], inner(p, q))
+
+    def cell(i):
+        return pl.ds(pl.multiple_of(i * images, images), images)
+
+    def half_cell(i, g):
+        return pl.ds(pl.multiple_of(i * images + g * 16, 16), 16)
+
+    def prepare(t):
+        for g in range(2):
+            block = feats_ref[g * 16 : g * 16 + 16, t].astype(full)
+            turned = jnp.swapaxes(block, 0, 1)
+            for q in range(8):
+                value = turned[q] * mask_of(t, q, slice(g * 16, g * 16 + 16))
+                xpad[t + 1, q + 1, g * 16 : g * 16 + 16, :] = value.astype(low)
+        line = lax.broadcasted_iota(jnp.int32, (8, 8, width), 0)
+        column = lax.broadcasted_iota(jnp.int32, (8, 8, width), 1)
+        core = jnp.where((line < 4) & (column < 4), 1.0, 0.0).astype(full)
+        wide = []
+        for k in range(4):
+            n = t * 4 + k
+            value = feats_ref[n].astype(full) * jnp.maximum(core, image_group[n].astype(full))
+            value = jnp.concatenate([value, jnp.zeros_like(value)], axis=1)
+            wide.append(value.reshape(128, width).astype(low))
+        project(0, t, jnp.concatenate(wide, axis=0))
+
+    def project(layer, t, rows):
+        at_v[:, pl.ds(pl.multiple_of(t * 512, 512), 512)] = lax.dot_general(
+            basis_t[layer], rows, (((1,), (1,)), ((), ())), preferred_element_type=full
+        ).astype(low)
+
+    def at_copy(li):
+        return pltpu.make_async_copy(at_v, at_out.at[li], out_sem.at[1 + li])
+
+    def gr_copy(li):
+        return pltpu.make_async_copy(gr_v, gr_out.at[li], out_sem.at[3 + li])
+
+    def conv_tap(tap, m, acc):
+        a, b = tap // 3, lax.rem(tap, 3)
+        kernel = weights(m)
+        for p in range(8):
+            rows = xpad[p + a, pl.ds(b, 8)].reshape(8 * images, width)
+            acc[p * 256 : p * 256 + 256, :] += jnp.dot(rows, kernel, preferred_element_type=full)
+
+    xpad[...] = jnp.zeros_like(xpad)
+    conv_a[...] = jnp.zeros_like(conv_a)
+    conv_b[...] = jnp.zeros_like(conv_b)
+    for layer in range(2):
+        basis_t[layer] = basis_in_ref[layer].T
+
+    def first(t, carry):
+        gather(t)
+
+        @pl.when(t < 8)
+        def _():
+            prepare(t)
+
+        tap = t - 8
+
+        @pl.when(tap >= 0)
+        def _():
+            core_copy(tap).wait_recv()
+            conv_tap(tap, tap, conv_a)
+
+        return carry
+
+    lax.fori_loop(0, 17, first, 0)
+    at_copy(1).start()
+
+    mine = dp * 2 + me_s
+
+    def sum_one(buf, sems, n, a, b):
+        other, core = near_id(a, b)
+        return remote(
+            buf.at[mine], buf.at[mine], sems[0].at[n, a * 2 + b], sems[1].at[n, mine],
+            (other, core, me_z),
+        )
+
+    def sum_one_wait(buf, n, a, b):
+        other, core = near_id(a, b)
+        slot = other * 2 + core
+        remote(
+            buf.at[slot], buf.at[slot], one_ss.at[n, a * 2 + b], one_rs.at[n, slot],
+            (other, core, me_z),
+        ).wait_recv()
+
+    def sum_two(buf, n, d):
+        other = lax.rem(me_z + d, 4)
+        return remote(
+            buf.at[me_z], buf.at[me_z], two_ss.at[n, d], two_rs.at[n, me_z], (dp, me_s, other)
+        )
+
+    def sum_start(n, buf):
+        for a, b in near:
+            sum_one(buf, (one_ss, one_rs), n, a, b).start()
+
+    def sum_middle(n, buf, buf_two):
+        for a, b in near:
+            sum_one_wait(buf, n, a, b)
+        total = buf[0]
+        for slot in range(1, 8):
+            total = total + buf[slot]
+        buf_two[me_z] = total
+        for d in (1, 2, 3):
+            sum_two(buf_two, n, d).start()
+
+    def sum_end(n, buf_two):
+        for d in (1, 2, 3):
+            other = lax.rem(me_z + d, 4)
+            remote(
+                buf_two.at[other], buf_two.at[other], two_ss.at[n, d], two_rs.at[n, other],
+                (dp, me_s, other),
+            ).wait_recv()
+        return buf_two[0] + buf_two[1] + buf_two[2] + buf_two[3]
+
+    def sum_sent(n, buf, buf_two):
+        for a, b in near:
+            sum_one(buf, (one_ss, one_rs), n, a, b).wait_send()
+        for d in (1, 2, 3):
+            sum_two(buf_two, n, d).wait_send()
+
+    def column(value):
+        return jnp.sum(value, axis=0, keepdims=True)
+
+    zero = jnp.zeros((images, width), full)
+
+    def channel_sums(acc):
+        def line(p, carry):
+            sums, squares = carry
+            for q in range(8):
+                value = acc[cell(p * 8 + q), :]
+                masked = value * mask_of(p, q)
+                sums = sums + masked
+                squares = squares + masked * value
+            return sums, squares
+
+        sums, squares = lax.fori_loop(0, 8, line, (zero, zero))
+        return column(sums), column(squares)
+
+    sums, squares = channel_sums(conv_a)
+    group = group_ref[...]
+    pixels = 16.0 + 48.0 * group
+    small_one[0, mine, 0:1, :] = sums
+    small_one[0, mine, 1:2, :] = squares
+    small_one[0, mine, 2:3, :] = column(pixels)
+    small_one[0, mine, 3:4, :] = jnp.broadcast_to(column(weight_ref[...])[:, 0:1], (1, width))
+    sum_start(0, small_one.at[0])
+
+    def later(t, carry):
+        gather(t)
+        return carry
+
+    lax.fori_loop(17, 20, later, 0)
+    sum_middle(0, small_one.at[0], small_two.at[0])
+    lax.fori_loop(20, 22, later, 0)
+    total = sum_end(0, small_two.at[0])
+    total_out[...] = total
+    count = total[2:3]
+
+    def moments(total):
+        average = total[0:1] / count
+        return average, lax.rsqrt(total[1:2] / count - average * average + EPS_NORM)
+
+    average_a, inv_a = moments(total)
+
+    def activation(value, layer, average, inv):
+        normed = (value - average) * inv
+        pre = params_ref[layer, 0:1, :] * normed + params_ref[layer, 1:2, :]
+        return normed, pre, jax.nn.sigmoid(pre)
+
+    def images_first(values):
+        return jnp.swapaxes(jnp.stack(values), 0, 1)
+
+    def act_line(p, carry):
+        for g in range(2):
+            acts = []
+            for q in range(8):
+                value = conv_a[half_cell(p * 8 + q, g), :]
+                normed, pre, sigma = activation(value, 0, average_a, inv_a)
+                act = pre * sigma * mask_of(p, q, slice(g * 16, g * 16 + 16))
+                xpad[p + 1, q + 1, g * 16 : g * 16 + 16, :] = act.astype(low)
+                acts.append(act)
+            turned = images_first(acts)
+            turned = jnp.concatenate([turned, jnp.zeros_like(turned)], axis=1).astype(low)
+            n_pad[g * 16 : g * 16 + 16, pl.ds(pl.multiple_of(p * 16, 16), 16), :] = turned
+        return carry
+
+    lax.fori_loop(0, 8, act_line, 0)
+    lax.fori_loop(22, 24, later, 0)
+
+    def second(tap, carry):
+        core_copy(TAPS + tap).wait_recv()
+        conv_tap(tap, TAPS + tap, conv_b)
+        return carry
+
+    lax.fori_loop(0, TAPS, second, 0)
+    sums, squares = channel_sums(conv_b)
+    small_one[1, mine, 0:1, :] = sums
+    small_one[1, mine, 1:2, :] = squares
+    small_one[1, mine, 2:4, :] = jnp.zeros((2, width), full)
+    sum_start(1, small_one.at[1])
+    at_copy(1).wait()
+
+    def project_one(t, carry):
+        project(1, t, n_pad[pl.ds(t * 4, 4)].reshape(512, width))
+        return carry
+
+    lax.fori_loop(0, 4, project_one, 0)
+    sum_middle(1, small_one.at[1], small_two.at[1])
+    lax.fori_loop(4, 8, project_one, 0)
+    at_copy(0).start()
+    total = sum_end(1, small_two.at[1])
+    average_b, inv_b = moments(total)
+
+    def pool_line(p, carry):
+        for q in range(8):
+            normed, pre, sigma = activation(conv_b[cell(p * 8 + q), :], 1, average_b, inv_b)
+            carry = carry + pre * sigma * mask_of(p, q)
+        return carry
+
+    pooled = lax.fori_loop(0, 8, pool_line, zero) / pixels
+    pooled_low = pooled.astype(low)
+    head_low = head_ref[...].astype(low)
+    logits = jnp.dot(pooled_low, head_low, preferred_element_type=full) + bias_ref[...]
+    valid = lax.broadcasted_iota(jnp.int32, logits.shape, 1) < classes
+    top = jnp.max(jnp.where(valid, logits, -1e30), axis=1, keepdims=True)
+    shifted = logits - top
+    spread = jnp.sum(jnp.where(valid, jnp.exp(shifted), 0.0), axis=1, keepdims=True)
+    log_prob = jnp.where(valid, shifted - jnp.log(spread), 0.0)
+    hot = hot_ref[...]
+    image_weight = weight_ref[...]
+    picked = jnp.sum(hot * log_prob, axis=1, keepdims=True)
+    loss = -column(image_weight * picked)[:, 0:1]
+    d_logits = jnp.where(valid, image_weight * (jnp.exp(log_prob) - hot), 0.0)
+    grad_head = lax.dot_general(
+        d_logits,
+        pooled_low.astype(full),
+        (((0,), (0,)), ((), ())),
+        precision=highest,
+        preferred_element_type=full,
+    )
+    head_one[mine, 0:16, :] = grad_head[0:16]
+    head_one[mine, 16:24, :] = jnp.zeros((8, width), full)
+    head_one[mine, 16:17, 0:128] = column(d_logits)
+    head_one[mine, 17:18, :] = jnp.broadcast_to(loss, (1, width))
+    d_pooled = (
+        lax.dot_general(
+            d_logits,
+            head_low.astype(full),
+            (((1,), (1,)), ((), ())),
+            precision=highest,
+            preferred_element_type=full,
+        )
+        / pixels
+    )
+
+    def d_line_top(p, carry):
+        gammas, betas = carry
+        for q in range(8):
+            at = cell(p * 8 + q)
+            normed, pre, sigma = activation(conv_b[at, :], 1, average_b, inv_b)
+            d_pre = d_pooled * mask_of(p, q) * sigma * (1.0 + pre * (1.0 - sigma))
+            d_buf[at, :] = d_pre
+            gammas = gammas + d_pre * normed
+            betas = betas + d_pre
+        return gammas, betas
+
+    gammas, betas = lax.fori_loop(0, 8, d_line_top, (zero, zero))
+
+    def put_sums(n, gammas, betas):
+        small_one[n, mine, 0:1, :] = column(gammas)
+        small_one[n, mine, 1:2, :] = column(betas)
+        small_one[n, mine, 2:4, :] = jnp.zeros((2, width), full)
+        sum_start(n, small_one.at[n])
+
+    put_sums(2, gammas, betas)
+    sum_start(4, head_one)
+
+    def clear(n, carry):
+        gr_v[n, 0:16, :] = jnp.zeros((16, width), low)
+        gr_v[n, 144:160, :] = jnp.zeros((16, width), low)
+        return carry
+
+    lax.fori_loop(0, 3 * images, clear, 0)
+    sum_middle(2, small_one.at[2], small_two.at[2])
+    total_b = sum_end(2, small_two.at[2])
+    norm_out[1] = total_b
+
+    def grad_lines(layer, acc, average, inv, total):
+        gamma = params_ref[layer, 0:1, :]
+        beta_part = gamma * total[1:2] / count
+        gamma_part = gamma * total[0:1] / count
+
+        def line(p, carry):
+            for q in range(8):
+                at = cell(p * 8 + q)
+                normed = (acc[at, :] - average) * inv
+                value = mask_of(p, q) * (
+                    inv * (gamma * d_buf[at, :] - beta_part - normed * gamma_part)
+                )
+                xpad[p + 1, q + 1, :, :] = value.astype(low)
+            return carry
+
+        lax.fori_loop(0, 8, line, 0)
+
+    grad_lines(1, conv_b, average_b, inv_b, total_b)
+    d_buf[...] = jnp.zeros_like(d_buf)
+
+    def back(tap, carry):
+        a, b = tap // 3, lax.rem(tap, 3)
+        kernel = weights(TAPS + tap)
+        for p in range(8):
+            rows = xpad[p + 2 - a, pl.ds(2 - b, 8)].reshape(8 * images, width)
+            d_buf[p * 256 : p * 256 + 256, :] += lax.dot_general(
+                rows, kernel, (((1,), (1,)), ((), ())), preferred_element_type=full
+            )
+        return carry
+
+    lax.fori_loop(0, TAPS, back, 0)
+    sum_middle(4, head_one, head_two)
+
+    def d_line(p, carry):
+        gammas, betas = carry
+        for q in range(8):
+            at = cell(p * 8 + q)
+            normed, pre, sigma = activation(conv_a[at, :], 0, average_a, inv_a)
+            d_pre = d_buf[at, :] * mask_of(p, q) * sigma * (1.0 + pre * (1.0 - sigma))
+            d_buf[at, :] = d_pre
+            gammas = gammas + d_pre * normed
+            betas = betas + d_pre
+        return gammas, betas
+
+    gammas, betas = lax.fori_loop(0, 8, d_line, (zero, zero))
+    put_sums(3, gammas, betas)
+
+    def turn_grads(layer):
+        def line(p, carry):
+            rows = xpad[p + 1, 1:9].reshape(8 * images, width)
+            value = jnp.dot(rows, basis_out_ref[layer], preferred_element_type=full)
+            value = value.reshape(8, images, width)
+            lines = pl.ds(pl.multiple_of(p * 16 + 16, 16), 16)
+            for g in range(4):
+                turned = jnp.swapaxes(value[:, g * 8 : g * 8 + 8], 0, 1)
+                gap = jnp.zeros((8, 1, width), full)
+                rest = jnp.zeros((8, 8, width), full)
+                shifts = (
+                    jnp.concatenate([turned[:, 1:], gap], axis=1),
+                    turned,
+                    jnp.concatenate([gap, turned[:, :7]], axis=1),
+                )
+                for b in range(3):
+                    wide = jnp.concatenate([shifts[b], rest], axis=1).astype(low)
+                    gr_v[b * images + g * 8 : b * images + g * 8 + 8, lines, :] = wide
+            return carry
+
+        return line
+
+    lax.fori_loop(0, 4, turn_grads(1), 0)
+    sum_middle(3, small_one.at[3], small_two.at[3])
+    lax.fori_loop(4, 8, turn_grads(1), 0)
+    gr_copy(0).start()
+    total_a = sum_end(3, small_two.at[3])
+    norm_out[0] = total_a
+    grad_lines(0, conv_a, average_a, inv_a, total_a)
+    head_out[...] = sum_end(4, head_two)
+    gr_copy(0).wait()
+    lax.fori_loop(0, 8, turn_grads(0), 0)
+    gr_copy(1).start()
+    at_copy(0).wait()
+
+    def sent(m, carry):
+        @pl.when(me_z < 3)
+        def _():
+            right_copy(m).wait_send()
+
+        @pl.when(me_z > 0)
+        def _():
+            left_copy(m).wait_send()
+
+        x_copy(m).wait_send()
+        y_copy(m).wait_send()
+        even_copy(m).wait_send()
+        core_copy(m).wait_send()
+        return carry
+
+    lax.fori_loop(0, matrices, sent, 0)
+    for n in range(4):
+        sum_sent(n, small_one.at[n], small_two.at[n])
+    sum_sent(4, head_one, head_two)
+    gr_copy(1).wait()
+
+
+def sweep(
+    feats, size_group, labels, class_wt, slot, owners, basis_in, basis_out, master, norm_params, head
+):
+    count_img, side_len, _, width = feats.shape
+    classes = class_wt.shape[0]
+    low, full, dma = jnp.bfloat16, jnp.float32, pltpu.SemaphoreType.DMA
+    held = owners == lax.axis_index("blk")
+    own_slot = jnp.where(held, slot - lax.axis_index("blk") * master.shape[0], 0)
+    hot = (labels[:, None] == jnp.arange(128)[None, :]).astype(full)
+    weight = jnp.sum(
+        jnp.where(labels[:, None] == jnp.arange(classes)[None, :], class_wt[None, :], 0), axis=1
+    ).astype(full)
+    group = jnp.broadcast_to((size_group == 1).astype(full)[:, None], (count_img, width))
+    vmem, any_spec = pl.BlockSpec(memory_space=pltpu.VMEM), pl.BlockSpec(memory_space=pl.ANY)
+    smem = pl.BlockSpec(memory_space=pltpu.SMEM)
+    rows = count_img * side_len * side_len
+    return pl.pallas_call(
+        functools.partial(sweep_kernel, classes),
+        out_shape=[
+            jax.ShapeDtypeStruct((2, width, count_img * 128), low),
+            jax.ShapeDtypeStruct((2, 3 * count_img, 160, width), low),
+            jax.ShapeDtypeStruct((4, width), full),
+            jax.ShapeDtypeStruct((2, 4, width), full),
+            jax.ShapeDtypeStruct((24, width), full),
+        ],
+        in_specs=[vmem, vmem, smem, smem, any_spec, vmem, vmem, vmem, vmem, vmem, smem, vmem, vmem],
+        out_specs=[any_spec, any_spec, vmem, vmem, vmem],
+        scratch_shapes=[
+            pltpu.VMEM((18, 2, 4, 64, 512), low),
+            pltpu.VMEM((10, 10, 32, 512), low),
+            pltpu.VMEM((rows, 512), full),
+            pltpu.VMEM((rows, 512), full),
+            pltpu.VMEM((rows, 512), full),
+            pltpu.VMEM((512, 4096), low),
+            pltpu.VMEM((32, 128, 512), low),
+            pltpu.VMEM((96, 160, 512), low),
+            pltpu.VMEM((10, 64, 512), full),
+            pltpu.VMEM((18, 64, 512), low),
+            pltpu.VMEM((18, 64, 512), low),
+            pltpu.VMEM((18, 64, 512), low),
+            pltpu.VMEM((18, 64, 512), low),
+            pltpu.VMEM((2, 512, 512), low),
+            pltpu.VMEM((4, 8, 4, 512), full),
+            pltpu.VMEM((4, 4, 4, 512), full),
+            pltpu.VMEM((8, 24, 512), full),
+            pltpu.VMEM((4, 24, 512), full),
+            dma((5,)),
+            dma((6, 18)),
+            dma((6, 18)),
+            dma((5, 8)),
+            dma((5, 8)),
+            dma((5, 4)),
+            dma((5, 4)),
+        ],
+        name="sweep",
+        compiler_params=pltpu.CompilerParams(
+            collective_id=1, has_side_effects=True, vmem_limit_bytes=63 * 2**20
+        ),
+    )(
+        feats,
+        group,
+        own_slot.astype(jnp.int32),
+        held.astype(jnp.int32),
+        master,
+        norm_params,
+        jnp.pad(head[:width], ((0, 0), (0, 128 - classes))),
+        jnp.pad(head[width:], ((0, 0), (0, 128 - classes))),
+        hot,
+        jnp.broadcast_to(weight[:, None], (count_img, 128)),
+        (size_group == 1).astype(jnp.int32),
+        basis_in,
+        basis_out,
+    )
 
 
 def statistics_kernel(
@@ -542,24 +1211,6 @@
     return divided.reshape(2, 18, 512, 256), new_scales.reshape(576, 256)
 
 
-def turned_operands(inputs, grad_low, basis_in, basis_out):
-    images, side_len, _, width = inputs.shape
-    wide = jnp.pad(inputs, ((0, 0), (0, 0), (0, 8), (0, 0))).reshape(images * 128, width)
-    act = lax.dot_general(
-        basis_in, wide, (((0,), (1,)), ((), ())), preferred_element_type=jnp.float32
-    ).astype(jnp.bfloat16)
-    grad = jnp.einsum(
-        "npqo,oj->npqj", grad_low, basis_out, preferred_element_type=jnp.float32
-    ).astype(jnp.bfloat16)
-    zero = ((0, 0), (1, 1))
-    shifts = [
-        jnp.pad(grad[:, :, 1:], zero + ((0, 9), (0, 0))),
-        jnp.pad(grad, zero + ((0, 8), (0, 0))),
-        jnp.pad(grad[:, :, :7], zero + ((1, 8), (0, 0))),
-    ]
-    return act, jnp.concatenate([s.reshape(images, 160, width) for s in shifts], axis=0)
-
-
 def owned_kernel(
     which, divided, rows_ref, cols_ref, w_ref, m_ref, v_ref, new_w, new_m, new_v
 ):
@@ -604,7 +1255,7 @@
     )(which, divided, basis_in, basis_out, master, moment1, moment2)
 
 
-def shards(
+def shards_general(
     feats,
     size_group,
     labels,
@@ -682,7 +1333,6 @@
     loss_all, head_all = lax.psum((loss_local, grad_head), ("dp", "side", "blk"))
     d_pooled = jnp.dot(d_logits, head_low.astype(jnp.float32).T, precision=lax.Precision.HIGHEST)
     d_act = d_pooled[:, None, None, :] / pixels[:, None, None, None] * mask_four
-    fast = (n_dp, n_side, n_blk) == (4, 2, 4) and block_rows == 576
     terms = [None] * L
     grad_norm = [None] * L
     for layer in reversed(range(L)):
@@ -707,9 +1357,6 @@
         grad_low = d_conv.astype(jnp.bfloat16)
         if layer > 0:
             d_act = conv_backward(grad_low, kernels[layer])
-        if fast:
-            terms[layer] = turned_operands(inputs, grad_low, basis_in[layer], basis_out[layer])
-            continue
         act_proj = jnp.einsum(
             "npqc,ci->npqi", inputs, basis_in[layer], preferred_element_type=jnp.float32
         ).astype(jnp.bfloat16)
@@ -717,58 +1364,37 @@
             "npqo,oj->npqj", grad_low, basis_out[layer], preferred_element_type=jnp.float32
         ).astype(jnp.bfloat16)
         terms[layer] = tap_sums(act_proj, grad_proj)
+    whole = jnp.stack(terms).reshape(n_dp, n_blk, block_rows, 2, 2, half)
+    whole = whole.transpose(0, 4, 1, 2, 3, 5).reshape(n_dp * 2 * n_blk * block_rows, 2 * half)
+    reduced = lax.psum_scatter(whole, ("dp", "side", "blk"), scatter_dimension=0, tiled=True)
+    proj_sum = reduced[:, :half]
+    proj_square = reduced[:, half:]
+    new_scales = DECAY * scales + (1.0 - DECAY) * proj_square / images_all
+    divided = (proj_sum / weight_all / (new_scales + DAMPING)).astype(jnp.bfloat16)
+    spread = lax.all_gather(divided, ("dp", "side", "blk"), axis=0, tiled=True)
+    spread = spread.reshape(n_dp, 2, n_blk, block_rows, half).transpose(0, 2, 3, 1, 4)
+    precond_all = spread.reshape(matrices, width, width)
     slot_ids = lax.axis_index("blk") * slots_dev + jnp.arange(slots_dev)
-    hits = slot[None, :] == slot_ids[:, None]
-    which = jnp.stack(
-        [
-            jnp.sum(jnp.where(hits, index[None, :], 0), axis=1),
-            jnp.sum(hits.astype(jnp.int32), axis=1),
-            jnp.full((slots_dev,), lax.axis_index("side"), jnp.int32),
-        ]
-    ).astype(jnp.int32)
-    if fast:
-        divided, new_scales = statistics(
-            jnp.stack([terms[1][0], terms[0][0]]),
-            jnp.stack([terms[1][1], terms[0][1]]),
-            scales,
-            weight_all,
-            images_all,
-        )
-        new_master, new_moment1, new_moment2 = owned_update(
-            divided, basis_in, basis_out, master, moment1, moment2, which
-        )
-    else:
-        whole = jnp.stack(terms).reshape(n_dp, n_blk, block_rows, 2, 2, half)
-        whole = whole.transpose(0, 4, 1, 2, 3, 5).reshape(n_dp * 2 * n_blk * block_rows, 2 * half)
-        reduced = lax.psum_scatter(whole, ("dp", "side", "blk"), scatter_dimension=0, tiled=True)
-        proj_sum = reduced[:, :half]
-        proj_square = reduced[:, half:]
-        new_scales = DECAY * scales + (1.0 - DECAY) * proj_square / images_all
-        divided = (proj_sum / weight_all / (new_scales + DAMPING)).astype(jnp.bfloat16)
-        spread = lax.all_gather(divided, ("dp", "side", "blk"), axis=0, tiled=True)
-        spread = spread.reshape(n_dp, 2, n_blk, block_rows, half).transpose(0, 2, 3, 1, 4)
-        precond_all = spread.reshape(matrices, width, width)
-        slot_ids = lax.axis_index("blk") * slots_dev + jnp.arange(slots_dev)
-        owned = (slot[None, :] == slot_ids[:, None]).astype(jnp.bfloat16)
-        chosen = jnp.einsum(
-            "qm,mij->qij", owned, precond_all, preferred_element_type=jnp.float32
-        ).astype(jnp.bfloat16)
-        layer_hot = (index[:, None] // TAPS == jnp.arange(L)[None, :]).astype(jnp.bfloat16)
-        slot_layer = jnp.dot(owned, layer_hot, preferred_element_type=jnp.float32).astype(jnp.bfloat16)
-        half_rows = lax.dynamic_slice_in_dim(
-            basis_in, lax.axis_index("side") * master.shape[1], master.shape[1], 1
-        )
-        rows_slot = jnp.einsum(
-            "ql,lci->qci", slot_layer, half_rows, preferred_element_type=jnp.float32
-        ).astype(jnp.bfloat16)
-        cols_slot = jnp.einsum(
-            "ql,loj->qoj", slot_layer, basis_out, preferred_element_type=jnp.float32
-        ).astype(jnp.bfloat16)
-        turned = jnp.einsum(
-            "qci,qij->qcj", rows_slot, chosen, preferred_element_type=jnp.float32
-        ).astype(jnp.bfloat16)
-        slot_grad = jnp.einsum("qcj,qoj->qco", turned, cols_slot, preferred_element_type=jnp.float32)
-        new_master, new_moment1, new_moment2 = adamw(master, moment1, moment2, slot_grad, RATE_CONV)
+    owned = (slot[None, :] == slot_ids[:, None]).astype(jnp.bfloat16)
+    chosen = jnp.einsum(
+        "qm,mij->qij", owned, precond_all, preferred_element_type=jnp.float32
+    ).astype(jnp.bfloat16)
+    layer_hot = (index[:, None] // TAPS == jnp.arange(L)[None, :]).astype(jnp.bfloat16)
+    slot_layer = jnp.dot(owned, layer_hot, preferred_element_type=jnp.float32).astype(jnp.bfloat16)
+    half_rows = lax.dynamic_slice_in_dim(
+        basis_in, lax.axis_index("side") * master.shape[1], master.shape[1], 1
+    )
+    rows_slot = jnp.einsum(
+        "ql,lci->qci", slot_layer, half_rows, preferred_element_type=jnp.float32
+    ).astype(jnp.bfloat16)
+    cols_slot = jnp.einsum(
+        "ql,loj->qoj", slot_layer, basis_out, preferred_element_type=jnp.float32
+    ).astype(jnp.bfloat16)
+    turned = jnp.einsum(
+        "qci,qij->qcj", rows_slot, chosen, preferred_element_type=jnp.float32
+    ).astype(jnp.bfloat16)
+    slot_grad = jnp.einsum("qcj,qoj->qco", turned, cols_slot, preferred_element_type=jnp.float32)
+    new_master, new_moment1, new_moment2 = adamw(master, moment1, moment2, slot_grad, RATE_CONV)
     new_norm, new_norm_m, new_norm_v = adamw(
         norm_params, norm_m, norm_v, jnp.stack(grad_norm) / weight_all, RATE_NORM
     )
@@ -789,6 +1415,93 @@
     )
 
 
+def shards_fast(
+    feats,
+    size_group,
+    labels,
+    class_wt,
+    owners,
+    basis_in,
+    basis_out,
+    scales,
+    master,
+    moment1,
+    moment2,
+    norm_params,
+    norm_m,
+    norm_v,
+    head,
+    head_m,
+    head_v,
+):
+    classes = class_wt.shape[0]
+    width = feats.shape[3]
+    slots_dev = master.shape[0]
+    index = jnp.arange(owners.shape[0])
+    earlier = (owners[:, None] == owners[None, :]) & (index[None, :] < index[:, None])
+    slot = owners * slots_dev + jnp.sum(earlier.astype(jnp.int32), axis=1)
+    act_turned, grad_turned, total, norm_sums, head_sums = sweep(
+        feats,
+        size_group,
+        labels,
+        class_wt,
+        slot,
+        owners,
+        basis_in,
+        basis_out,
+        master,
+        norm_params,
+        head,
+    )
+    weight_all = total[3, 0]
+    images_all = feats.shape[0] * lax.axis_size("dp") * lax.axis_size("side") * lax.axis_size("blk")
+    slot_ids = lax.axis_index("blk") * slots_dev + jnp.arange(slots_dev)
+    hits = slot[None, :] == slot_ids[:, None]
+    which = jnp.stack(
+        [
+            jnp.sum(jnp.where(hits, index[None, :], 0), axis=1),
+            jnp.sum(hits.astype(jnp.int32), axis=1),
+            jnp.full((slots_dev,), lax.axis_index("side"), jnp.int32),
+        ]
+    ).astype(jnp.int32)
+    divided, new_scales = statistics(act_turned, grad_turned, scales, weight_all, images_all)
+    new_master, new_moment1, new_moment2 = owned_update(
+        divided, basis_in, basis_out, master, moment1, moment2, which
+    )
+    new_norm, new_norm_m, new_norm_v = adamw(
+        norm_params, norm_m, norm_v, norm_sums[:, :2] / weight_all, RATE_NORM
+    )
+    head_all = jnp.concatenate([head_sums[:classes].T, head_sums[16:17, :classes]], axis=0)
+    new_head, new_head_m, new_head_v = adamw(head, head_m, head_v, head_all / weight_all, RATE_HEAD)
+    return (
+        head_sums[17, 0],
+        weight_all,
+        new_scales,
+        new_master,
+        new_moment1,
+        new_moment2,
+        new_norm,
+        new_norm_m,
+        new_norm_v,
+        new_head,
+        new_head_m,
+        new_head_v,
+    )
+
+
+def shards(*args):
+    feats, class_wt, scales, master = args[0], args[3], args[7], args[8]
+    mesh_shape = tuple(lax.axis_size(name) for name in ("dp", "side", "blk"))
+    fits = (
+        mesh_shape == (4, 2, 4)
+        and scales.shape == (576, 256)
+        and feats.shape == (32, 8, 8, 512)
+        and master.shape == (10, 256, 512)
+        and class_wt.shape[0] <= 16
+    )
+    return shards_fast(*args) if fits else shards_general(*args)
+
+
 def solution(mesh):
     return jax.shard_map(
         shards,

time: 853 us -> 431 us (0.51)
  Pallas kernels: 172 us -> 400 us
  waiting for transfers between devices: 175 us -> 0 us
  blocking collectives: 161 us -> 0 us
  matrix products: 150 us -> 0 us
  other arithmetic: 97.9 us -> 9.38 us
  local copies, waits for them, and re-layouts: 77.5 us -> 20.3 us
  between operations: 15.7 us -> 0.73 us
    pallas_call x0 -> x1, Pallas kernels: none -> 228 us  [sweep(): pl.pallas_call(functools.partial(sweep_kernel, classes), out_shape=[jax.S...]
    all_gather x1 -> x0, waiting for transfers between devices: 175 us -> none  [shards(): lax.all_gather(master.astype(jnp.bfloat16), ('side', 'blk'), axis=0, tile...]
    psum x4 -> x0, blocking collectives: 161 us -> none  [the longest x2 79.9 us: shards(): lax.psum((jnp.sum(masked, axis=(0, 1, 2)), jnp.sum(masked * conv_out, axi...]
    dot_general x35 -> x0, matrix products: 150 us -> none  [the longest x18 73.5 us: conv_forward(): jnp.einsum('npqc,co->npqo', shifted, kernel[tap], preferred_element_type=...]
    another operation x7 -> x1, other arithmetic: 43.4 us -> 0.07 us  [shards_fast(): jnp.stack([jnp.sum(jnp.where(hits, index[None, :], 0), axis=1), jnp.sum(h...]
    slice x5 -> x6, local copies, waits for them, and re-layouts: 41 us -> 4.63 us  [the longest x1 1.2 us: shards_fast(): weight_all = total[3, 0]]
    reduce_sum x10 -> x3, other arithmetic: 22.9 us -> 1.85 us  [the longest x1 0.91 us: shards_fast(): slot = owners * slots_dev + jnp.sum(earlier.astype(jnp.int32), axis=1)]
    pad x8 -> x2, local copies, waits for them, and re-layouts: 17.9 us -> 1.25 us  [the longest x1 0.73 us: sweep(): jnp.pad(head[:width], ((0, 0), (0, 128 - classes)))]
  transfers between devices with their start and end apart: 1 -> 0, of which waited for: 1 -> 0; matrix products, arithmetic and copies ran while one was open for 1% -> 0% of each run, Pallas kernels for 0% -> 0%
where the time goes in v3:
time: 431 us
  Pallas kernels  400 us (93%)
  local copies, waits for them, and re-layouts  20.3 us (5%)
  other arithmetic  9.38 us (2%)
    pallas_call x1, Pallas kernels, sweep(): pl.pallas_call(functools.partial(sweep_kernel, classes), out_shape=[jax.S...  228 us
    pallas_call x1, Pallas kernels, statistics(): pl.pallas_call(functools.partial(statistics_kernel, images, images_all),...  158 us
    pallas_call x1, Pallas kernels, owned_update(): pl.pallas_call(owned_kernel, grid_spec=pltpu.PrefetchScalarGridSpec(num_s...  14.2 us
    unnamed x29, local copies, waits for them, and re-layouts  11 us

profile of v3, /device:TPU:0, one launch (start us, length us, event | category | flops | bytes accessed | tf_op | source)
XLA Modules:
  0.0 430.6 jit_solution(14807596034297574372)
XLA Ops:
  0.7 0.8 select_reduce_fusion
  1.5 1.2 compare_convert_fusion.1.own_flag
  2.7 0.9 convert_reduce_fusion
  3.6 1.2 multiply_add_fusion.2
  4.7 0.2 fusion.3
  5.0 1.2 compare_convert_fusion.2
  6.2 0.7 slice.22
  6.9 0.1 copy.36
  7.0 0.5 pad.9.bias_ref
  7.5 0.7 broadcast_in_dim.38.weight_ref
  8.2 1.3 fusion.1.hot_ref
  9.5 0.8 slice.21
  10.2 0.7 broadcast_in_dim.30.group_ref
  11.0 0.1 copy.35
  11.1 0.7 pad.8.head_ref
  11.8 227.7 %sweep.1 = (bf16[2,512,4096]{2,1,0:T(8,128)(2,1)}, bf16[2,96,160,512]{3,2,1,0:T(8,128)(2,1)}, f32[4,512]{1,0:T(4,128)}, f32[2,4,512]{2,1,0:T(4,128)}, f32[24,512]{1,0:T(8,128)}) custom-call(bf16[32,8,8,512]{3,2,1,0:T(8,128)(2,1)} %feats_ref.1, f32[32,512]{1,0:T(8,128)} %broadcast_in_dim.30.group_ref, s32[18]{0:T(128)} %get-tuple-element.41.own_slot, ...), custom_call_target="tpu_custom_call" | custom-call | tf_op jit(solution)/shard_map/sweep/pallas_call | solution.py:692
  239.6 1.2 slice.23
  240.8 1.2 slice.24
  242.0 0.7 slice.27
  242.6 0.8 slice_bitcast_fusion
  243.4 1.2 broadcast_in_dim.60.weight_ref
  244.7 158.3 %statistics.1 = (bf16[2,2,2,4,9,2,32,256]{7,6,5,4,3,2,1,0:T(8,128)(2,1)}, f32[9,2,32,256]{3,2,1,0:T(8,128)}) custom-call(bf16[2,512,4096]{2,1,0:T(8,128)(2,1)} %get-tuple-element.24.at_hbm, bf16[2,96,160,512]{3,2,1,0:T(8,128)(2,1)} %get-tuple-element.25.gr_hbm, f32[9,2,32,256]{3,2,1,0:T(8,128)} %bitcast.12, f32[1,256]{1,0:T(1,128)} %broadcast_in_dim.60.weight_ref), custom_call_target="tpu_custom_call" | custom-call | tf_op jit(solution)/shard_map/statistics/pallas_call | solution.py:1160
  402.9 0.1 copy.34
  403.1 1.3 multiply_subtract_fusion.1
  404.4 1.3 multiply_subtract_fusion
  405.7 2.5 copy-done
  408.2 2.5 copy-done.1
  410.6 2.5 copy-done.2
  413.1 1.2 copy-done.3
  414.4 1.2 copy-done.4
  415.6 14.2 %owned_update.1 = (f32[10,256,512]{2,1,0:T(8,128)}, f32[10,256,512]{2,1,0:T(8,128)}, f32[10,256,512]{2,1,0:T(8,128)}) custom-call(s32[3,10]{1,0:T(4,128)S(1)} %add_add_fusion.which, bf16[2,18,512,256]{3,2,1,0:T(8,128)(2,1)} %bitcast.10, bf16[2,512,512]{2,1,0:T(8,128)(2,1)S(1)} %copy-done.3, bf16[2,512,512]{2,1,0:T(8,128)(2,1)S(1)} %copy-done.4, ...), custom_call_target="tpu_custom_call" | custom-call | tf_op jit(solution)/shard_map/owned_update/pallas_call | solution.py:1237
  429.8 0.8 copy.38
  (25 shorter events, 0.2 us)
Async XLA Ops:
  244.6 158.4 %copy-start.9 = (f32[2,2,512]{2,1,0:T(2,128)S(1)}, f32[2,2,512]{2,1,0:T(2,128)}, u32[]{:S(2)}) copy-start(f32[2,2,512]{2,1,0:T(2,128)} %params_ref.1) | copy-start | bytes 24580
  244.6 158.4 %copy-start.10 = (f32[2,2,512]{2,1,0:T(2,128)S(1)}, f32[2,2,512]{2,1,0:T(2,128)}, u32[]{:S(2)}) copy-start(f32[2,2,512]{2,1,0:T(2,128)} %param.29) | copy-start | bytes 24580
  244.6 158.4 %copy-start.11 = (f32[2,2,512]{2,1,0:T(2,128)S(1)}, f32[2,2,512]{2,1,0:T(2,128)}, u32[]{:S(2)}) copy-start(f32[2,2,512]{2,1,0:T(2,128)} %param.30) | copy-start | bytes 24580
  244.6 158.4 %copy-start.12 = (f32[2,4,512]{2,1,0:T(4,128)S(1)}, f32[2,4,512]{2,1,0:T(4,128)}, u32[]{:S(2)}) copy-start(f32[2,4,512]{2,1,0:T(4,128)} %get-tuple-element.31) | copy-start | bytes 49156
  244.6 159.7 %copy-start.6 = (f32[513,10]{0,1:T(8,128)S(1)}, f32[513,10]{0,1:T(8,128)}, u32[]{:S(2)}) copy-start(f32[513,10]{0,1:T(8,128)} %param.31) | copy-start | bytes 61564
  244.6 159.7 %copy-start.7 = (f32[513,10]{0,1:T(8,128)S(1)}, f32[513,10]{0,1:T(8,128)}, u32[]{:S(2)}) copy-start(f32[513,10]{0,1:T(8,128)} %param.32) | copy-start | bytes 61564
  244.6 159.7 %copy-start.8 = (f32[513,10]{0,1:T(8,128)S(1)}, f32[513,10]{0,1:T(8,128)}, u32[]{:S(2)}) copy-start(f32[513,10]{0,1:T(8,128)} %param.33) | copy-start | bytes 61564
  405.7 2.5 copy-start
  408.2 2.5 copy-start.1
  410.6 2.5 copy-start.2
  413.1 1.2 copy-start.3
  414.4 1.2 copy-start.4
  415.6 14.2 %copy-start.5 = (f32[9,2,32,256]{3,2,1,0:T(8,128)S(1)}, f32[9,2,32,256]{3,2,1,0:T(8,128)}, u32[]{:S(2)}) copy-start(f32[9,2,32,256]{3,2,1,0:T(8,128)} %get-tuple-element.26) | copy-start | bytes 1769476

commit v4 on v3

--- a/solution.py
+++ b/solution.py
@@ -80,18 +80,14 @@
 
 
 def sweep_kernel(
-    classes,
     feats_ref,
-    group_ref,
-    own_slot,
-    own_flag,
+    image_group,
+    labels_ref,
+    class_ref,
+    owners_ref,
     master_hbm,
     params_ref,
     head_ref,
-    bias_ref,
-    hot_ref,
-    weight_ref,
-    image_group,
     basis_in_ref,
     basis_out_ref,
     at_out,
@@ -107,6 +103,9 @@
     at_v,
     n_pad,
     gr_v,
+    group_ref,
+    hot_ref,
+    weight_ref,
     piece,
     w_own,
     w_left,
@@ -170,12 +169,12 @@
 
     piece_copy.wait()
 
-    def own(m, carry):
-        value = piece[own_slot[m]] * own_flag[m].astype(full)
+    mine_is = [jnp.where(owners_ref[m] == me_z, 1, 0) for m in range(matrices)]
+    before = jnp.zeros((), jnp.int32)
+    for m in range(matrices):
+        value = piece[jnp.minimum(before, piece.shape[0] - 1)] * mine_is[m].astype(full)
         w_own[m] = value.astype(low)
-        return carry
-
-    lax.fori_loop(0, matrices, own, 0)
+        before = before + mine_is[m]
 
     @pl.when(me_z == 0)
     def _():
@@ -239,12 +238,10 @@
             def _():
                 left_copy(m).start()
 
-    early_right = me_z < 2
-
     def gather(t):
-        flow_right(jnp.where(early_right, t, t - 2))
-        flow_left(jnp.where(early_right, t - 2, t))
-        m = t - 2
+        flow_right(t - 2 * me_z)
+        flow_left(t - 2 * (3 - me_z))
+        m = t - 6
 
         @pl.when((m >= 0) & (m < matrices))
         def _():
@@ -252,7 +249,7 @@
             x_copy(m).start()
             y_copy(m).start()
 
-        m4 = t - 4
+        m4 = t - 8
 
         @pl.when((m4 >= 0) & (m4 < matrices))
         def _():
@@ -267,7 +264,7 @@
             def _():
                 odd_copy(m4).start()
 
-        m6 = t - 6
+        m6 = t - 10
 
         @pl.when((m6 >= 0) & (m6 < matrices))
         def _():
@@ -288,6 +285,9 @@
 
     def half_cell(i, g):
         return pl.ds(pl.multiple_of(i * images + g * 16, 16), 16)
+
+    def full_map(n):
+        return jnp.where(image_group[n] == 1, 1.0, 0.0).astype(full)
 
     def prepare(t):
         for g in range(2):
@@ -302,7 +302,7 @@
         wide = []
         for k in range(4):
             n = t * 4 + k
-            value = feats_ref[n].astype(full) * jnp.maximum(core, image_group[n].astype(full))
+            value = feats_ref[n].astype(full) * jnp.maximum(core, full_map(n))
             value = jnp.concatenate([value, jnp.zeros_like(value)], axis=1)
             wide.append(value.reshape(128, width).astype(low))
         project(0, t, jnp.concatenate(wide, axis=0))
@@ -325,20 +325,30 @@
             rows = xpad[p + a, pl.ds(b, 8)].reshape(8 * images, width)
             acc[p * 256 : p * 256 + 256, :] += jnp.dot(rows, kernel, preferred_element_type=full)
 
+    for t in range(3):
+        gather(t)
     xpad[...] = jnp.zeros_like(xpad)
-    conv_a[...] = jnp.zeros_like(conv_a)
-    conv_b[...] = jnp.zeros_like(conv_b)
-    for layer in range(2):
-        basis_t[layer] = basis_in_ref[layer].T
+    basis_t[0] = basis_in_ref[0].T
+    place = lax.broadcasted_iota(jnp.int32, (1, 128), 1)
+    for n in range(images):
+        group_ref[n : n + 1, :] = jnp.full((1, width), full_map(n), full)
+        hot_ref[n : n + 1, :] = jnp.where(place == labels_ref[n], 1.0, 0.0).astype(full)
+        weight_ref[n : n + 1, :] = jnp.full((1, 128), class_ref[labels_ref[n]].astype(full), full)
 
     def first(t, carry):
         gather(t)
 
-        @pl.when(t < 8)
-        def _():
-            prepare(t)
-
-        tap = t - 8
+        @pl.when(t < 11)
+        def _():
+            prepare(t - 3)
+
+        @pl.when(t == 11)
+        def _():
+            conv_a[...] = jnp.zeros_like(conv_a)
+            conv_b[...] = jnp.zeros_like(conv_b)
+            basis_t[1] = basis_in_ref[1].T
+
+        tap = t - 12
 
         @pl.when(tap >= 0)
         def _():
@@ -347,7 +357,7 @@
 
         return carry
 
-    lax.fori_loop(0, 17, first, 0)
+    lax.fori_loop(3, 21, first, 0)
     at_copy(1).start()
 
     mine = dp * 2 + me_s
@@ -433,9 +443,9 @@
         gather(t)
         return carry
 
-    lax.fori_loop(17, 20, later, 0)
+    lax.fori_loop(21, 23, later, 0)
     sum_middle(0, small_one.at[0], small_two.at[0])
-    lax.fori_loop(20, 22, later, 0)
+    lax.fori_loop(23, 24, later, 0)
     total = sum_end(0, small_two.at[0])
     total_out[...] = total
     count = total[2:3]
@@ -469,11 +479,15 @@
         return carry
 
     lax.fori_loop(0, 8, act_line, 0)
-    lax.fori_loop(22, 24, later, 0)
 
     def second(tap, carry):
         core_copy(TAPS + tap).wait_recv()
         conv_tap(tap, TAPS + tap, conv_b)
+
+        @pl.when(tap < 4)
+        def _():
+            gather(24 + tap)
+
         return carry
 
     lax.fori_loop(0, TAPS, second, 0)
@@ -503,18 +517,16 @@
 
     pooled = lax.fori_loop(0, 8, pool_line, zero) / pixels
     pooled_low = pooled.astype(low)
-    head_low = head_ref[...].astype(low)
-    logits = jnp.dot(pooled_low, head_low, preferred_element_type=full) + bias_ref[...]
-    valid = lax.broadcasted_iota(jnp.int32, logits.shape, 1) < classes
-    top = jnp.max(jnp.where(valid, logits, -1e30), axis=1, keepdims=True)
-    shifted = logits - top
-    spread = jnp.sum(jnp.where(valid, jnp.exp(shifted), 0.0), axis=1, keepdims=True)
-    log_prob = jnp.where(valid, shifted - jnp.log(spread), 0.0)
-    hot = hot_ref[...]
-    image_weight = weight_ref[...]
+    classes = head_ref.shape[1]
+    head_low = head_ref[0:width, :].astype(low)
+    logits = jnp.dot(pooled_low, head_low, preferred_element_type=full) + head_ref[width:, :]
+    shifted = logits - jnp.max(logits, axis=1, keepdims=True)
+    log_prob = shifted - jnp.log(jnp.sum(jnp.exp(shifted), axis=1, keepdims=True))
+    hot = hot_ref[:, 0:classes]
+    image_weight = weight_ref[:, 0:classes]
     picked = jnp.sum(hot * log_prob, axis=1, keepdims=True)
-    loss = -column(image_weight * picked)[:, 0:1]
-    d_logits = jnp.where(valid, image_weight * (jnp.exp(log_prob) - hot), 0.0)
+    loss = -column(weight_ref[:, 0:1] * picked)
+    d_logits = image_weight * (jnp.exp(log_prob) - hot)
     grad_head = lax.dot_general(
         d_logits,
         pooled_low.astype(full),
@@ -522,9 +534,9 @@
         precision=highest,
         preferred_element_type=full,
     )
-    head_one[mine, 0:16, :] = grad_head[0:16]
-    head_one[mine, 16:24, :] = jnp.zeros((8, width), full)
-    head_one[mine, 16:17, 0:128] = column(d_logits)
+    head_one[mine, :, :] = jnp.zeros((24, width), full)
+    head_one[mine, 0:classes, :] = grad_head
+    head_one[mine, 16:17, 0:classes] = column(d_logits)
     head_one[mine, 17:18, :] = jnp.broadcast_to(loss, (1, width))
     d_pooled = (
         lax.dot_general(
@@ -557,17 +569,11 @@
         sum_start(n, small_one.at[n])
 
     put_sums(2, gammas, betas)
-    sum_start(4, head_one)
-
-    def clear(n, carry):
-        gr_v[n, 0:16, :] = jnp.zeros((16, width), low)
-        gr_v[n, 144:160, :] = jnp.zeros((16, width), low)
-        return carry
-
-    lax.fori_loop(0, 3 * images, clear, 0)
+
     sum_middle(2, small_one.at[2], small_two.at[2])
     total_b = sum_end(2, small_two.at[2])
     norm_out[1] = total_b
+    sum_start(4, head_one)
 
     def grad_lines(layer, acc, average, inv, total):
         gamma = params_ref[layer, 0:1, :]
@@ -621,19 +627,11 @@
             rows = xpad[p + 1, 1:9].reshape(8 * images, width)
             value = jnp.dot(rows, basis_out_ref[layer], preferred_element_type=full)
             value = value.reshape(8, images, width)
-            lines = pl.ds(pl.multiple_of(p * 16 + 16, 16), 16)
+            lines = pl.ds(pl.multiple_of(p * 16, 16), 16)
             for g in range(4):
                 turned = jnp.swapaxes(value[:, g * 8 : g * 8 + 8], 0, 1)
-                gap = jnp.zeros((8, 1, width), full)
-                rest = jnp.zeros((8, 8, width), full)
-                shifts = (
-                    jnp.concatenate([turned[:, 1:], gap], axis=1),
-                    turned,
-                    jnp.concatenate([gap, turned[:, :7]], axis=1),
-                )
-                for b in range(3):
-                    wide = jnp.concatenate([shifts[b], rest], axis=1).astype(low)
-                    gr_v[b * images + g * 8 : b * images + g * 8 + 8, lines, :] = wide
+                turned = jnp.concatenate([turned, jnp.zeros_like(turned)], axis=1).astype(low)
+                gr_v[g * 8 : g * 8 + 8, lines, :] = turned
             return carry
 
         return line
@@ -674,31 +672,23 @@
 
 
 def sweep(
-    feats, size_group, labels, class_wt, slot, owners, basis_in, basis_out, master, norm_params, head
+    feats, size_group, labels, class_wt, owners, basis_in, basis_out, master, norm_params, head
 ):
     count_img, side_len, _, width = feats.shape
-    classes = class_wt.shape[0]
     low, full, dma = jnp.bfloat16, jnp.float32, pltpu.SemaphoreType.DMA
-    held = owners == lax.axis_index("blk")
-    own_slot = jnp.where(held, slot - lax.axis_index("blk") * master.shape[0], 0)
-    hot = (labels[:, None] == jnp.arange(128)[None, :]).astype(full)
-    weight = jnp.sum(
-        jnp.where(labels[:, None] == jnp.arange(classes)[None, :], class_wt[None, :], 0), axis=1
-    ).astype(full)
-    group = jnp.broadcast_to((size_group == 1).astype(full)[:, None], (count_img, width))
     vmem, any_spec = pl.BlockSpec(memory_space=pltpu.VMEM), pl.BlockSpec(memory_space=pl.ANY)
     smem = pl.BlockSpec(memory_space=pltpu.SMEM)
     rows = count_img * side_len * side_len
     return pl.pallas_call(
-        functools.partial(sweep_kernel, classes),
+        sweep_kernel,
         out_shape=[
             jax.ShapeDtypeStruct((2, width, count_img * 128), low),
-            jax.ShapeDtypeStruct((2, 3 * count_img, 160, width), low),
+            jax.ShapeDtypeStruct((2, count_img, 128, width), low),
             jax.ShapeDtypeStruct((4, width), full),
             jax.ShapeDtypeStruct((2, 4, width), full),
             jax.ShapeDtypeStruct((24, width), full),
         ],
-        in_specs=[vmem, vmem, smem, smem, any_spec, vmem, vmem, vmem, vmem, vmem, smem, vmem, vmem],
+        in_specs=[vmem, smem, smem, smem, smem, any_spec, vmem, vmem, vmem, vmem],
         out_specs=[any_spec, any_spec, vmem, vmem, vmem],
         scratch_shapes=[
             pltpu.VMEM((18, 2, 4, 64, 512), low),
@@ -708,7 +698,10 @@
             pltpu.VMEM((rows, 512), full),
             pltpu.VMEM((512, 4096), low),
             pltpu.VMEM((32, 128, 512), low),
-            pltpu.VMEM((96, 160, 512), low),
+            pltpu.VMEM((32, 128, 512), low),
+            pltpu.VMEM((32, 512), full),
+            pltpu.VMEM((32, 128), full),
+            pltpu.VMEM((32, 128), full),
             pltpu.VMEM((10, 64, 512), full),
             pltpu.VMEM((18, 64, 512), low),
             pltpu.VMEM((18, 64, 512), low),
@@ -733,16 +726,13 @@
         ),
     )(
         feats,
-        group,
-        own_slot.astype(jnp.int32),
-        held.astype(jnp.int32),
+        size_group,
+        labels,
+        class_wt,
+        owners,
         master,
         norm_params,
-        jnp.pad(head[:width], ((0, 0), (0, 128 - classes))),
-        jnp.pad(head[width:], ((0, 0), (0, 128 - classes))),
-        hot,
-        jnp.broadcast_to(weight[:, None], (count_img, 128)),
-        (size_group == 1).astype(jnp.int32),
+        head,
         basis_in,
         basis_out,
     )
@@ -758,6 +748,7 @@
     out,
     ns_out,
     at_v,
+    gc_v,
     gr_v,
     sc_v,
     ns_v,
@@ -807,14 +798,30 @@
             device_id_type=MESH,
         )
 
-    def load(li, what):
-        if what == 3:
-            return pltpu.make_async_copy(at_hbm.at[li], at_v.at[li], load_sem.at[li, 3])
-        at = pl.ds(what * images, images)
-        return pltpu.make_async_copy(gr_hbm.at[li, at], gr_v.at[li, at], load_sem.at[li, what])
-
-    for what in (3, 0, 1, 2):
-        load(0, what).start()
+    def load_act(li):
+        return pltpu.make_async_copy(at_hbm.at[li], at_v.at[li], load_sem.at[li])
+
+    def load_grad(li):
+        return pltpu.make_async_copy(gr_hbm.at[li], gc_v, load_sem.at[2 + li])
+
+    load_grad(0).start()
+    load_act(0).start()
+
+    def shifted(li, n):
+        lines = gc_v[n].astype(full).reshape(8, 16, 512)[:, 0:8]
+        gap, rest = jnp.zeros((8, 1, 512), full), jnp.zeros((8, 8, 512), full)
+        for b, value in enumerate(
+            (
+                jnp.concatenate([lines[:, 1:], gap], axis=1),
+                lines,
+                jnp.concatenate([gap, lines[:, :7]], axis=1),
+            )
+        ):
+            wide = jnp.concatenate([value, rest], axis=1).reshape(128, 512).astype(low)
+            at = b * images + n
+            gr_v[li, at, 0:16, :] = jnp.zeros((16, 512), low)
+            gr_v[li, at, 16:144, :] = wide
+            gr_v[li, at, 144:160, :] = jnp.zeros((16, 512), low)
 
     barrier = pltpu.get_barrier_semaphore()
     away = [(dp, me_s, lax.rem(me_z + d, 4)) for d in (1, 2, 3)]
@@ -935,16 +942,21 @@
             store(u, x_to, u % 4, total, square)
 
     def step(k, carry):
-        for at, needs in ((0, (0, 1, 2, 3)), (9, (0, 1, 2, 3))):
-            @pl.when(k == at)
-            def _():
-                for what in needs:
-                    load(at // 9, what).wait()
-
         @pl.when(k == 1)
         def _():
-            for what in range(4):
-                load(1, what).start()
+            load_grad(1).wait()
+
+        @pl.when((k >= 1) & (k < 9))
+        def _():
+            def few(n, carry):
+                shifted(1, (k - 1) * 4 + n)
+                return carry
+
+            lax.fori_loop(0, 4, few, 0)
+
+        @pl.when(k == 9)
+        def _():
+            load_act(1).wait()
 
         @pl.when((k >= 2) & (k < steps))
         def _():
@@ -1069,7 +1081,7 @@
             both = z_keep[ring, me_z] + got[0] + got[1] + got[2]
             scale = DECAY * sc_v[li, i] + (1.0 - DECAY) * both[1] / images_all
             ns_v[li, i] = scale
-            div_v[ring] = (both[0] / weight_ref[...] / (scale + DAMPING)).astype(low)
+            div_v[ring] = (both[0] / weight_ref[3:4, 0:256] / (scale + DAMPING)).astype(low)
             local_copy(j4).start()
             for d in (1, 2, 3):
                 gz_copy(j4, d).start()
@@ -1128,6 +1140,16 @@
 
         return carry
 
+    load_grad(0).wait()
+
+    def build(n, carry):
+        shifted(0, n)
+        return carry
+
+    lax.fori_loop(0, images, build, 0)
+    load_grad(1).start()
+    load_act(0).wait()
+    load_act(1).start()
     lax.fori_loop(0, steps + 7, step, 0)
 
     def finish(j, carry):
@@ -1151,7 +1173,7 @@
             gz_copy(j, d).wait_send()
 
 
-def statistics(act_turned, grad_turned, scales, weight_all, images_all):
+def statistics(act_turned, grad_turned, scales, total, images_all):
     images = act_turned.shape[2] // 128
     dma = pltpu.SemaphoreType.DMA
     low, full = jnp.bfloat16, jnp.float32
@@ -1167,6 +1189,7 @@
         out_specs=[any_spec, any_spec],
         scratch_shapes=[
             pltpu.VMEM((2, 512, images * 128), low),
+            pltpu.VMEM((images, 128, 512), low),
             pltpu.VMEM((2, 3 * images, 160, 512), low),
             pltpu.VMEM((2, 9, 32, 256), full),
             pltpu.VMEM((2, 9, 32, 256), full),
@@ -1187,7 +1210,7 @@
             pltpu.VMEM((2, 4) + piece, low),
             pltpu.VMEM((18, 3) + piece, low),
             pltpu.VMEM((2, 4) + piece, full),
-            dma((2, 4)),
+            dma((4,)),
             dma((6,)),
             dma((2,)),
             dma((10, 2)),
@@ -1206,7 +1229,7 @@
         act_turned,
         grad_turned,
         scales.reshape(9, 2, 32, 256),
-        jnp.full((1, 256), weight_all, full),
+        total,
     )
     return divided.reshape(2, 18, 512, 256), new_scales.reshape(576, 256)
 
@@ -1251,7 +1274,7 @@
         ),
         out_shape=[jax.ShapeDtypeStruct(master.shape, jnp.float32)] * 3,
         name="owned_update",
-        compiler_params=pltpu.CompilerParams(vmem_limit_bytes=32 * 2**20),
+        compiler_params=pltpu.CompilerParams(vmem_limit_bytes=63 * 2**20),
     )(which, divided, basis_in, basis_out, master, moment1, moment2)
 
 
@@ -1445,7 +1468,6 @@
         size_group,
         labels,
         class_wt,
-        slot,
         owners,
         basis_in,
         basis_out,
@@ -1464,7 +1486,7 @@
             jnp.full((slots_dev,), lax.axis_index("side"), jnp.int32),
         ]
     ).astype(jnp.int32)
-    divided, new_scales = statistics(act_turned, grad_turned, scales, weight_all, images_all)
+    divided, new_scales = statistics(act_turned, grad_turned, scales, total, images_all)
     new_master, new_moment1, new_moment2 = owned_update(
         divided, basis_in, basis_out, master, moment1, moment2, which
     )

time: 431 us -> 308 us (0.71)
  Pallas kernels: 400 us -> 296 us
  local copies, waits for them, and re-layouts: 20.3 us -> 4.99 us
  other arithmetic: 9.38 us -> 3.63 us
    pallas_call x1, Pallas kernels: 228 us -> 124 us  [sweep(): pl.pallas_call(sweep_kernel, out_shape=[jax.ShapeDtypeStruct((2, width, c...]
    unnamed x29 -> x22, local copies, waits for them, and re-layouts: 11 us -> 2.49 us
where the time goes in v4:
time: 308 us; the launch traced here: 305 us
  Pallas kernels  296 us (96%)
  local copies, waits for them, and re-layouts  4.99 us (2%)
  other arithmetic  3.63 us (1%)
    pallas_call x1, Pallas kernels, statistics(): pl.pallas_call(functools.partial(statistics_kernel, images, images_all),...  155 us
    pallas_call x1, Pallas kernels, sweep(): pl.pallas_call(sweep_kernel, out_shape=[jax.ShapeDtypeStruct((2, width, c...  124 us
    pallas_call x1, Pallas kernels, owned_update(): pl.pallas_call(owned_kernel, grid_spec=pltpu.PrefetchScalarGridSpec(num_s...  17.3 us

profile of v4, /device:TPU:0, one launch (start us, length us, event | category | flops | bytes accessed | tf_op | source)
XLA Modules:
  0.0 305.3 jit_solution(7134488565258681963)
XLA Ops:
  0.6 1.6 copy.31.head_ref
  2.3 123.5 %sweep.1 = (bf16[2,512,4096]{2,1,0:T(8,128)(2,1)}, bf16[2,32,128,512]{3,2,1,0:T(8,128)(2,1)}, f32[4,512]{1,0:T(4,128)}, f32[2,4,512]{2,1,0:T(4,128)}, f32[24,512]{1,0:T(8,128)}) custom-call(bf16[32,8,8,512]{3,2,1,0:T(8,128)(2,1)} %feats_ref.1, s32[32]{0:T(128)} %image_group.1, s32[32]{0:T(128)} %labels_ref.1, s32[10]{0:T(128)} %class_ref.1, s32[18]{0:T(128)} %owners_ref.1, ...), custom_call_target="tpu_custom_call" | custom-call | tf_op jit(solution)/shard_map/sweep/pallas_call | solution.py:682
  125.8 1.2 slice.15
  127.0 1.1 slice.16
  128.1 0.0 copy-start.9
  128.1 155.1 %statistics.1 = (bf16[2,2,2,4,9,2,32,256]{7,6,5,4,3,2,1,0:T(8,128)(2,1)}, f32[9,2,32,256]{3,2,1,0:T(8,128)}) custom-call(bf16[2,512,4096]{2,1,0:T(8,128)(2,1)} %get-tuple-element.24.at_hbm, bf16[2,32,128,512]{3,2,1,0:T(8,128)(2,1)} %get-tuple-element.25.gr_hbm, f32[9,2,32,256]{3,2,1,0:T(8,128)} %bitcast.11, f32[4,512]{1,0:T(4,128)} %get-tuple-element.23.weight_ref), custom_call_target="tpu_custom_call" | custom-call | tf_op jit(solution)/shard_map/statistics/pallas_call | solution.py:1182
  283.2 0.0 copy-done.9
  283.2 0.2 convert_reduce_fusion
  283.4 0.2 fusion.2
  283.6 0.1 pad.4.clone
  283.7 0.7 add_add_fusion.which
  284.4 0.0 copy-start.4
  284.4 0.0 copy-start.6
  284.4 0.0 copy-start.5
  284.4 0.0 copy-start.1
  284.4 0.0 copy-start.2
  284.4 0.0 copy-start.3
  284.4 0.0 copy-start
  284.4 17.3 %owned_update.1 = (f32[10,256,512]{2,1,0:T(8,128)}, f32[10,256,512]{2,1,0:T(8,128)}, f32[10,256,512]{2,1,0:T(8,128)}) custom-call(s32[3,10]{1,0:T(4,128)} %add_add_fusion.which, bf16[2,18,512,256]{3,2,1,0:T(8,128)(2,1)} %bitcast.10, bf16[2,512,512]{2,1,0:T(8,128)(2,1)} %rows_ref.1, bf16[2,512,512]{2,1,0:T(8,128)(2,1)} %cols_ref.1, f32[10,256,512]{2,1,0:T(8,128)} %w_ref.1, ...), custom_call_target="tpu_custom_call" | custom-call | tf_op jit(solution)/shard_map/owned_update/pallas_call | solution.py:1260
  301.7 0.0 copy-done.4
  301.7 0.0 copy-done.6
  301.8 0.0 copy-done.7
  301.8 0.0 copy-done.8
  301.8 1.3 multiply_subtract_fusion.1
  303.1 0.0 copy-done.5
  303.1 0.1 copy.32
  303.2 0.0 copy-done.1
  303.2 0.0 copy-done.2
  303.2 0.0 copy-done.3
  303.2 1.3 multiply_subtract_fusion
  304.5 0.0 copy-done
  304.5 0.8 copy.34
  (6 shorter events, 0.0 us)
Async XLA Ops:
  128.1 155.1 %copy-start.9 = (s32[18]{0:T(128)S(1)}, s32[18]{0:T(128)}, u32[]{:S(2)}) copy-start(s32[18]{0:T(128)} %owners_ref.1) | copy-start | bytes 220
  284.4 17.4 %copy-start.4 = (f32[2,2,512]{2,1,0:T(2,128)S(1)}, f32[2,2,512]{2,1,0:T(2,128)}, u32[]{:S(2)}) copy-start(f32[2,2,512]{2,1,0:T(2,128)} %params_ref.1) | copy-start | bytes 24580
  284.4 17.4 %copy-start.6 = (f32[2,2,512]{2,1,0:T(2,128)S(1)}, f32[2,2,512]{2,1,0:T(2,128)}, u32[]{:S(2)}) copy-start(f32[2,2,512]{2,1,0:T(2,128)} %param.29) | copy-start | bytes 24580
  284.4 17.4 %copy-start.7 = (f32[2,2,512]{2,1,0:T(2,128)S(1)}, f32[2,2,512]{2,1,0:T(2,128)}, u32[]{:S(2)}) copy-start(f32[2,2,512]{2,1,0:T(2,128)} %param.30) | copy-start | bytes 24580
  284.4 17.4 %copy-start.8 = (f32[2,4,512]{2,1,0:T(4,128)S(1)}, f32[2,4,512]{2,1,0:T(4,128)}, u32[]{:S(2)}) copy-start(f32[2,4,512]{2,1,0:T(4,128)} %get-tuple-element.31) | copy-start | bytes 49156
  284.4 18.7 %copy-start.5 = (f32[24,512]{1,0:T(8,128)S(1)}, f32[24,512]{1,0:T(8,128)}, u32[]{:S(2)}) copy-start(f32[24,512]{1,0:T(8,128)} %get-tuple-element.22) | copy-start | bytes 147460
  284.4 18.8 %copy-start.1 = (f32[513,10]{0,1:T(8,128)S(1)}, f32[513,10]{0,1:T(8,128)}, u32[]{:S(2)}) copy-start(f32[513,10]{0,1:T(8,128)} %param.31) | copy-start | bytes 61564
  284.4 18.8 %copy-start.2 = (f32[513,10]{0,1:T(8,128)S(1)}, f32[513,10]{0,1:T(8,128)}, u32[]{:S(2)}) copy-start(f32[513,10]{0,1:T(8,128)} %param.32) | copy-start | bytes 61564
  284.4 18.8 %copy-start.3 = (f32[513,10]{0,1:T(8,128)S(1)}, f32[513,10]{0,1:T(8,128)}, u32[]{:S(2)}) copy-start(f32[513,10]{0,1:T(8,128)} %param.33) | copy-start | bytes 61564
  284.4 20.1 %copy-start = (f32[9,2,32,256]{3,2,1,0:T(8,128)S(1)}, f32[9,2,32,256]{3,2,1,0:T(8,128)}, u32[]{:S(2)}) copy-start(f32[9,2,32,256]{3,2,1,0:T(8,128)} %get-tuple-element.26) | copy-start | bytes 1769476

commit v5 on v4

--- a/solution.py
+++ b/solution.py
@@ -27,8 +27,8 @@
 def adamw(weight_now, first_now, second_now, gradient, rate):
     first_new = BETA_ONE * first_now + (1.0 - BETA_ONE) * gradient
     second_new = BETA_TWO * second_now + (1.0 - BETA_TWO) * gradient * gradient
-    first_hat = first_new / (1.0 - BETA_ONE**STEP)
-    second_hat = second_new / (1.0 - BETA_TWO**STEP)
+    first_hat = first_new * (1.0 / (1.0 - BETA_ONE**STEP))
+    second_hat = second_new * (1.0 / (1.0 - BETA_TWO**STEP))
     weight_new = weight_now - rate * (
         first_hat / (jnp.sqrt(second_hat) + ADAM_EPS) + WEIGHT_DECAY * weight_now
     )
@@ -79,7 +79,8 @@
 MESH = pl.DeviceIdType.MESH
 
 
-def sweep_kernel(
+def step_kernel(
+    images_all,
     feats_ref,
     image_group,
     labels_ref,
@@ -90,8 +91,9 @@
     head_ref,
     basis_in_ref,
     basis_out_ref,
-    at_out,
-    gr_out,
+    scales_hbm,
+    out,
+    ns_out,
     total_out,
     norm_out,
     head_out,
@@ -99,23 +101,31 @@
     xpad,
     conv_a,
     conv_b,
-    d_buf,
     at_v,
-    n_pad,
     gr_v,
     group_ref,
     hot_ref,
     weight_ref,
     piece,
-    w_own,
-    w_left,
-    w_right,
-    w_back,
     basis_t,
     small_one,
     small_two,
     head_one,
     head_two,
+    sc_v,
+    ns_v,
+    div_v,
+    s_send,
+    s_recv,
+    x1_send,
+    x1_keep,
+    y1_send,
+    y1_keep,
+    x2_send,
+    y2_send,
+    two_keep,
+    z_send,
+    z_keep,
     out_sem,
     g_ss,
     g_rs,
@@ -123,6 +133,16 @@
     one_rs,
     two_ss,
     two_rs,
+    misc_sem,
+    local_sem,
+    ss,
+    s_ss,
+    s_rs,
+    rs,
+    z_ss,
+    z_rs,
+    gz_ss,
+    gz_rs,
 ):
     low, full = jnp.bfloat16, jnp.float32
     highest = lax.Precision.HIGHEST
@@ -137,6 +157,21 @@
     to_left = (dp, me_s, lax.rem(me_z + 3, 4))
     images, width = 32, 512
     matrices = 2 * TAPS
+    steps = 2 * 9
+
+    def w_left(m):
+        return gr_v.at[m, 0:64]
+
+    def w_right(m):
+        return gr_v.at[m, 64:128]
+
+    def w_own(m):
+        return gr_v.at[18 + m, 0:64]
+
+    def w_back(m):
+        return gr_v.at[18 + m, 64:128]
+
+    first_map = 40
 
     def remote(src, dst, send, recv, target):
         return pltpu.make_async_remote_copy(
@@ -173,24 +208,31 @@
     before = jnp.zeros((), jnp.int32)
     for m in range(matrices):
         value = piece[jnp.minimum(before, piece.shape[0] - 1)] * mine_is[m].astype(full)
-        w_own[m] = value.astype(low)
+        w_own(m)[...] = value.astype(low)
         before = before + mine_is[m]
 
     @pl.when(me_z == 0)
     def _():
-        w_left[...] = jnp.zeros_like(w_left)
+        gr_v[0:18, 0:64, :] = jnp.zeros((18, 64, width), low)
 
     @pl.when(me_z == 3)
     def _():
-        w_right[...] = jnp.zeros_like(w_right)
+        gr_v[0:18, 64:128, :] = jnp.zeros((18, 64, width), low)
 
     pl.semaphore_wait(barrier, 10)
 
+    sc_local = pltpu.make_async_copy(scales_hbm.at[:, me_y], sc_v.at[1 - me_y], misc_sem.at[0])
+    sc_remote = remote(
+        scales_hbm.at[:, 1 - me_y], sc_v.at[1 - me_y], misc_sem.at[1], misc_sem.at[2], to_y
+    )
+    sc_local.start()
+    sc_remote.start()
+
     def right_copy(m):
-        return remote(w_left.at[m], w_left.at[m], g_ss.at[0, m], g_rs.at[0, m], to_right)
+        return remote(w_left(m), w_left(m), g_ss.at[0, m], g_rs.at[0, m], to_right)
 
     def left_copy(m):
-        return remote(w_back.at[m], w_right.at[m], g_ss.at[1, m], g_rs.at[1, m], to_left)
+        return remote(w_back(m), w_right(m), g_ss.at[1, m], g_rs.at[1, m], to_left)
 
     def x_copy(m):
         part = w_full.at[m, me_s, dp]
@@ -219,7 +261,7 @@
             def _():
                 right_copy(m).wait_recv()
 
-            w_left[m] = w_left[m] + w_own[m]
+            w_left(m)[...] = w_left(m)[...] + w_own(m)[...]
 
             @pl.when(me_z < 3)
             def _():
@@ -232,7 +274,7 @@
             def _():
                 left_copy(m).wait_recv()
 
-            w_back[m] = w_right[m] + w_own[m]
+            w_back(m)[...] = w_right(m)[...] + w_own(m)[...]
 
             @pl.when(me_z > 0)
             def _():
@@ -245,7 +287,7 @@
 
         @pl.when((m >= 0) & (m < matrices))
         def _():
-            w_full[m, me_s, dp] = w_left[m] + w_right[m]
+            w_full[m, me_s, dp] = w_left(m)[...] + w_right(m)[...]
             x_copy(m).start()
             y_copy(m).start()
 
@@ -308,15 +350,9 @@
         project(0, t, jnp.concatenate(wide, axis=0))
 
     def project(layer, t, rows):
-        at_v[:, pl.ds(pl.multiple_of(t * 512, 512), 512)] = lax.dot_general(
+        at_v[1 - layer, :, pl.ds(pl.multiple_of(t * 512, 512), 512)] = lax.dot_general(
             basis_t[layer], rows, (((1,), (1,)), ((), ())), preferred_element_type=full
         ).astype(low)
-
-    def at_copy(li):
-        return pltpu.make_async_copy(at_v, at_out.at[li], out_sem.at[1 + li])
-
-    def gr_copy(li):
-        return pltpu.make_async_copy(gr_v, gr_out.at[li], out_sem.at[3 + li])
 
     def conv_tap(tap, m, acc):
         a, b = tap // 3, lax.rem(tap, 3)
@@ -358,7 +394,6 @@
         return carry
 
     lax.fori_loop(3, 21, first, 0)
-    at_copy(1).start()
 
     mine = dp * 2 + me_s
 
@@ -397,14 +432,20 @@
         for d in (1, 2, 3):
             sum_two(buf_two, n, d).start()
 
-    def sum_end(n, buf_two):
+    def sum_arrived(n, buf_two):
         for d in (1, 2, 3):
             other = lax.rem(me_z + d, 4)
             remote(
                 buf_two.at[other], buf_two.at[other], two_ss.at[n, d], two_rs.at[n, other],
                 (dp, me_s, other),
             ).wait_recv()
+
+    def sum_total(buf_two):
         return buf_two[0] + buf_two[1] + buf_two[2] + buf_two[3]
+
+    def sum_end(n, buf_two):
+        sum_arrived(n, buf_two)
+        return sum_total(buf_two)
 
     def sum_sent(n, buf, buf_two):
         for a, b in near:
@@ -475,7 +516,7 @@
                 acts.append(act)
             turned = images_first(acts)
             turned = jnp.concatenate([turned, jnp.zeros_like(turned)], axis=1).astype(low)
-            n_pad[g * 16 : g * 16 + 16, pl.ds(pl.multiple_of(p * 16, 16), 16), :] = turned
+            gr_v[first_map + g * 16 : first_map + g * 16 + 16, pl.ds(pl.multiple_of(p * 16, 16), 16), :] = turned
         return carry
 
     lax.fori_loop(0, 8, act_line, 0)
@@ -496,16 +537,14 @@
     small_one[1, mine, 1:2, :] = squares
     small_one[1, mine, 2:4, :] = jnp.zeros((2, width), full)
     sum_start(1, small_one.at[1])
-    at_copy(1).wait()
 
     def project_one(t, carry):
-        project(1, t, n_pad[pl.ds(t * 4, 4)].reshape(512, width))
+        project(1, t, gr_v[pl.ds(first_map + t * 4, 4), 0:128, :].reshape(512, width))
         return carry
 
     lax.fori_loop(0, 4, project_one, 0)
     sum_middle(1, small_one.at[1], small_two.at[1])
     lax.fori_loop(4, 8, project_one, 0)
-    at_copy(0).start()
     total = sum_end(1, small_two.at[1])
     average_b, inv_b = moments(total)
 
@@ -517,9 +556,14 @@
 
     pooled = lax.fori_loop(0, 8, pool_line, zero) / pixels
     pooled_low = pooled.astype(low)
-    classes = head_ref.shape[1]
-    head_low = head_ref[0:width, :].astype(low)
-    logits = jnp.dot(pooled_low, head_low, preferred_element_type=full) + head_ref[width:, :]
+    classes = head_ref.shape[0]
+    head_low = head_ref[:, 0:width].astype(low)
+    bias = jnp.broadcast_to(head_ref[:, width : width + 1], (classes, classes))
+    across = lax.broadcasted_iota(jnp.int32, (classes, classes), 0)
+    along = lax.broadcasted_iota(jnp.int32, (classes, classes), 1)
+    logits = lax.dot_general(
+        pooled_low, head_low, (((1,), (1,)), ((), ())), preferred_element_type=full
+    ) + column(jnp.where(across == along, bias, 0.0))
     shifted = logits - jnp.max(logits, axis=1, keepdims=True)
     log_prob = shifted - jnp.log(jnp.sum(jnp.exp(shifted), axis=1, keepdims=True))
     hot = hot_ref[:, 0:classes]
@@ -542,7 +586,7 @@
         lax.dot_general(
             d_logits,
             head_low.astype(full),
-            (((1,), (1,)), ((), ())),
+            (((1,), (0,)), ((), ())),
             precision=highest,
             preferred_element_type=full,
         )
@@ -555,7 +599,6 @@
             at = cell(p * 8 + q)
             normed, pre, sigma = activation(conv_b[at, :], 1, average_b, inv_b)
             d_pre = d_pooled * mask_of(p, q) * sigma * (1.0 + pre * (1.0 - sigma))
-            d_buf[at, :] = d_pre
             gammas = gammas + d_pre * normed
             betas = betas + d_pre
         return gammas, betas
@@ -568,6 +611,22 @@
         small_one[n, mine, 2:4, :] = jnp.zeros((2, width), full)
         sum_start(n, small_one.at[n])
 
+    def sent(m, carry):
+        @pl.when(me_z < 3)
+        def _():
+            right_copy(m).wait_send()
+
+        @pl.when(me_z > 0)
+        def _():
+            left_copy(m).wait_send()
+
+        x_copy(m).wait_send()
+        y_copy(m).wait_send()
+        even_copy(m).wait_send()
+        core_copy(m).wait_send()
+        return carry
+
+    lax.fori_loop(0, matrices, sent, 0)
     put_sums(2, gammas, betas)
 
     sum_middle(2, small_one.at[2], small_two.at[2])
@@ -575,299 +634,133 @@
     norm_out[1] = total_b
     sum_start(4, head_one)
 
-    def grad_lines(layer, acc, average, inv, total):
+    def grad_of(layer, normed, d_pre, inv, total):
         gamma = params_ref[layer, 0:1, :]
-        beta_part = gamma * total[1:2] / count
-        gamma_part = gamma * total[0:1] / count
-
-        def line(p, carry):
-            for q in range(8):
-                at = cell(p * 8 + q)
-                normed = (acc[at, :] - average) * inv
-                value = mask_of(p, q) * (
-                    inv * (gamma * d_buf[at, :] - beta_part - normed * gamma_part)
-                )
-                xpad[p + 1, q + 1, :, :] = value.astype(low)
-            return carry
-
-        lax.fori_loop(0, 8, line, 0)
-
-    grad_lines(1, conv_b, average_b, inv_b, total_b)
-    d_buf[...] = jnp.zeros_like(d_buf)
+        return inv * (
+            gamma * d_pre
+            - gamma * total[1:2] / count
+            - normed * (gamma * total[0:1] / count)
+        )
+
+    def grad_top(p, carry):
+        for q in range(8):
+            normed, pre, sigma = activation(conv_b[cell(p * 8 + q), :], 1, average_b, inv_b)
+            mask = mask_of(p, q)
+            d_pre = d_pooled * mask * sigma * (1.0 + pre * (1.0 - sigma))
+            value = mask * grad_of(1, normed, d_pre, inv_b, total_b)
+            xpad[p + 1, q + 1, :, :] = value.astype(low)
+        return carry
+
+    lax.fori_loop(0, 8, grad_top, 0)
+    conv_b[...] = jnp.zeros_like(conv_b)
 
     def back(tap, carry):
         a, b = tap // 3, lax.rem(tap, 3)
         kernel = weights(TAPS + tap)
         for p in range(8):
             rows = xpad[p + 2 - a, pl.ds(2 - b, 8)].reshape(8 * images, width)
-            d_buf[p * 256 : p * 256 + 256, :] += lax.dot_general(
+            conv_b[p * 256 : p * 256 + 256, :] += lax.dot_general(
                 rows, kernel, (((1,), (1,)), ((), ())), preferred_element_type=full
             )
         return carry
-
-    lax.fori_loop(0, TAPS, back, 0)
-    sum_middle(4, head_one, head_two)
 
     def d_line(p, carry):
         gammas, betas = carry
         for q in range(8):
             at = cell(p * 8 + q)
             normed, pre, sigma = activation(conv_a[at, :], 0, average_a, inv_a)
-            d_pre = d_buf[at, :] * mask_of(p, q) * sigma * (1.0 + pre * (1.0 - sigma))
-            d_buf[at, :] = d_pre
+            d_pre = conv_b[at, :] * mask_of(p, q) * sigma * (1.0 + pre * (1.0 - sigma))
+            conv_b[at, :] = d_pre
             gammas = gammas + d_pre * normed
             betas = betas + d_pre
         return gammas, betas
-
-    gammas, betas = lax.fori_loop(0, 8, d_line, (zero, zero))
-    put_sums(3, gammas, betas)
 
     def turn_grads(layer):
         def line(p, carry):
             rows = xpad[p + 1, 1:9].reshape(8 * images, width)
             value = jnp.dot(rows, basis_out_ref[layer], preferred_element_type=full)
             value = value.reshape(8, images, width)
-            lines = pl.ds(pl.multiple_of(p * 16, 16), 16)
+            lines = pl.ds(pl.multiple_of(p * 16 + 16, 16), 16)
+            gap = jnp.zeros((8, 1, width), full)
+            rest = jnp.zeros((8, 8, width), full)
             for g in range(4):
                 turned = jnp.swapaxes(value[:, g * 8 : g * 8 + 8], 0, 1)
-                turned = jnp.concatenate([turned, jnp.zeros_like(turned)], axis=1).astype(low)
-                gr_v[g * 8 : g * 8 + 8, lines, :] = turned
+                shifts = (
+                    jnp.concatenate([turned[:, 1:], gap], axis=1),
+                    turned,
+                    jnp.concatenate([gap, turned[:, :7]], axis=1),
+                )
+                for b in range(3):
+                    wide = jnp.concatenate([shifts[b], rest], axis=1).astype(low)
+                    gr_v[b * images + g * 8 : b * images + g * 8 + 8, lines, :] = wide
             return carry
 
         return line
 
-    lax.fori_loop(0, 4, turn_grads(1), 0)
-    sum_middle(3, small_one.at[3], small_two.at[3])
-    lax.fori_loop(4, 8, turn_grads(1), 0)
-    gr_copy(0).start()
-    total_a = sum_end(3, small_two.at[3])
-    norm_out[0] = total_a
-    grad_lines(0, conv_a, average_a, inv_a, total_a)
-    head_out[...] = sum_end(4, head_two)
-    gr_copy(0).wait()
-    lax.fori_loop(0, 8, turn_grads(0), 0)
-    gr_copy(1).start()
-    at_copy(0).wait()
-
-    def sent(m, carry):
-        @pl.when(me_z < 3)
-        def _():
-            right_copy(m).wait_send()
-
-        @pl.when(me_z > 0)
-        def _():
-            left_copy(m).wait_send()
-
-        x_copy(m).wait_send()
-        y_copy(m).wait_send()
-        even_copy(m).wait_send()
-        core_copy(m).wait_send()
+    def clear(n, carry):
+        gr_v[n, 0:16, :] = jnp.zeros((16, width), low)
+        gr_v[n, 144:160, :] = jnp.zeros((16, width), low)
         return carry
 
-    lax.fori_loop(0, matrices, sent, 0)
-    for n in range(4):
-        sum_sent(n, small_one.at[n], small_two.at[n])
-    sum_sent(4, head_one, head_two)
-    gr_copy(1).wait()
-
-
-def sweep(
-    feats, size_group, labels, class_wt, owners, basis_in, basis_out, master, norm_params, head
-):
-    count_img, side_len, _, width = feats.shape
-    low, full, dma = jnp.bfloat16, jnp.float32, pltpu.SemaphoreType.DMA
-    vmem, any_spec = pl.BlockSpec(memory_space=pltpu.VMEM), pl.BlockSpec(memory_space=pl.ANY)
-    smem = pl.BlockSpec(memory_space=pltpu.SMEM)
-    rows = count_img * side_len * side_len
-    return pl.pallas_call(
-        sweep_kernel,
-        out_shape=[
-            jax.ShapeDtypeStruct((2, width, count_img * 128), low),
-            jax.ShapeDtypeStruct((2, count_img, 128, width), low),
-            jax.ShapeDtypeStruct((4, width), full),
-            jax.ShapeDtypeStruct((2, 4, width), full),
-            jax.ShapeDtypeStruct((24, width), full),
-        ],
-        in_specs=[vmem, smem, smem, smem, smem, any_spec, vmem, vmem, vmem, vmem],
-        out_specs=[any_spec, any_spec, vmem, vmem, vmem],
-        scratch_shapes=[
-            pltpu.VMEM((18, 2, 4, 64, 512), low),
-            pltpu.VMEM((10, 10, 32, 512), low),
-            pltpu.VMEM((rows, 512), full),
-            pltpu.VMEM((rows, 512), full),
-            pltpu.VMEM((rows, 512), full),
-            pltpu.VMEM((512, 4096), low),
-            pltpu.VMEM((32, 128, 512), low),
-            pltpu.VMEM((32, 128, 512), low),
-            pltpu.VMEM((32, 512), full),
-            pltpu.VMEM((32, 128), full),
-            pltpu.VMEM((32, 128), full),
-            pltpu.VMEM((10, 64, 512), full),
-            pltpu.VMEM((18, 64, 512), low),
-            pltpu.VMEM((18, 64, 512), low),
-            pltpu.VMEM((18, 64, 512), low),
-            pltpu.VMEM((18, 64, 512), low),
-            pltpu.VMEM((2, 512, 512), low),
-            pltpu.VMEM((4, 8, 4, 512), full),
-            pltpu.VMEM((4, 4, 4, 512), full),
-            pltpu.VMEM((8, 24, 512), full),
-            pltpu.VMEM((4, 24, 512), full),
-            dma((5,)),
-            dma((6, 18)),
-            dma((6, 18)),
-            dma((5, 8)),
-            dma((5, 8)),
-            dma((5, 4)),
-            dma((5, 4)),
-        ],
-        name="sweep",
-        compiler_params=pltpu.CompilerParams(
-            collective_id=1, has_side_effects=True, vmem_limit_bytes=63 * 2**20
-        ),
-    )(
-        feats,
-        size_group,
-        labels,
-        class_wt,
-        owners,
-        master,
-        norm_params,
-        head,
-        basis_in,
-        basis_out,
-    )
-
-
-def statistics_kernel(
-    images,
-    images_all,
-    at_hbm,
-    gr_hbm,
-    scales_hbm,
-    weight_ref,
-    out,
-    ns_out,
-    at_v,
-    gc_v,
-    gr_v,
-    sc_v,
-    ns_v,
-    div_v,
-    s_send,
-    s_recv,
-    x1_send,
-    x1_recv,
-    x1_keep,
-    y1_send,
-    y1_recv,
-    y1_keep,
-    x2_send,
-    x2_recv,
-    y2_send,
-    y2_recv,
-    two_keep,
-    z_send,
-    z_recv,
-    z_keep,
-    load_sem,
-    misc_sem,
-    local_sem,
-    ss,
-    s_rs,
-    rs,
-    z_ss,
-    z_rs,
-    gz_ss,
-    gz_rs,
-):
-    low, full = jnp.bfloat16, jnp.float32
-    dp, me_s, me_z = lax.axis_index("dp"), lax.axis_index("side"), lax.axis_index("blk")
-    me_y, me_x = dp // 2, lax.rem(dp, 2)
-    to_s = (dp, 1 - me_s, me_z)
-    to_x = (me_y * 2 + 1 - me_x, me_s, me_z)
-    to_y = ((1 - me_y) * 2 + me_x, me_s, me_z)
-    steps = 2 * 9
-
-    def remote(src, dst, send, recv, target):
-        return pltpu.make_async_remote_copy(
-            src_ref=src,
-            dst_ref=dst,
-            send_sem=send,
-            recv_sem=recv,
-            device_id=target,
-            device_id_type=MESH,
-        )
-
-    def load_act(li):
-        return pltpu.make_async_copy(at_hbm.at[li], at_v.at[li], load_sem.at[li])
-
-    def load_grad(li):
-        return pltpu.make_async_copy(gr_hbm.at[li], gc_v, load_sem.at[2 + li])
-
-    load_grad(0).start()
-    load_act(0).start()
-
-    def shifted(li, n):
-        lines = gc_v[n].astype(full).reshape(8, 16, 512)[:, 0:8]
-        gap, rest = jnp.zeros((8, 1, 512), full), jnp.zeros((8, 8, 512), full)
-        for b, value in enumerate(
-            (
-                jnp.concatenate([lines[:, 1:], gap], axis=1),
-                lines,
-                jnp.concatenate([gap, lines[:, :7]], axis=1),
-            )
-        ):
-            wide = jnp.concatenate([value, rest], axis=1).reshape(128, 512).astype(low)
-            at = b * images + n
-            gr_v[li, at, 0:16, :] = jnp.zeros((16, 512), low)
-            gr_v[li, at, 16:144, :] = wide
-            gr_v[li, at, 144:160, :] = jnp.zeros((16, 512), low)
-
-    barrier = pltpu.get_barrier_semaphore()
-    away = [(dp, me_s, lax.rem(me_z + d, 4)) for d in (1, 2, 3)]
-    for target in [to_s, to_x, to_y] + away:
-        pl.semaphore_signal(barrier, inc=1, device_id=target, device_id_type=MESH)
-    pl.semaphore_wait(barrier, 6)
-
-    sc_local = pltpu.make_async_copy(scales_hbm.at[:, me_y], sc_v.at[1 - me_y], misc_sem.at[0])
-    sc_remote = remote(
-        scales_hbm.at[:, 1 - me_y], sc_v.at[1 - me_y], misc_sem.at[1], misc_sem.at[2], to_y
-    )
-    sc_local.start()
-    sc_remote.start()
-
-    def side_copy(k):
-        return remote(
-            s_send.at[lax.rem(k, 2)],
-            s_recv.at[lax.rem(k, 4)],
-            ss.at[0, lax.rem(k, 2)],
-            s_rs.at[lax.rem(k, 4)],
-            to_s,
-        )
+    lax.fori_loop(0, 3 * images, clear, 0)
+    lax.fori_loop(0, 8, turn_grads(1), 0)
+
+    def bottom():
+        total_a = sum_total(small_two.at[3])
+        norm_out[0] = total_a
+
+        def line(p, carry):
+            for q in range(8):
+                at = cell(p * 8 + q)
+                normed = (conv_a[at, :] - average_a) * inv_a
+                value = mask_of(p, q) * grad_of(0, normed, conv_b[at, :], inv_a, total_a)
+                xpad[p + 1, q + 1, :, :] = value.astype(low)
+            return carry
+
+        lax.fori_loop(0, 8, line, 0)
+        lax.fori_loop(0, 8, turn_grads(0), 0)
+        head_out[...] = sum_end(4, head_two)
+
+    def x1_recv(j):
+        return w_full.at[j, 0, :, :, 0:256]
+
+    def y1_recv(j):
+        return w_full.at[j, 0, :, :, 256:512]
+
+    def x2_recv(j):
+        return w_full.at[j, 1, 0:2, :, 0:256]
+
+    def y2_recv(j):
+        return w_full.at[j, 1, 2:4, :, 0:256]
+
+    def z_recv(j, d):
+        return w_full.at[j, 1, d - 1, :, 256:512]
+
+    def side_copy(j):
+        ring, four = lax.rem(j, 2), lax.rem(j, 4)
+        return remote(s_send.at[ring], s_recv.at[four], s_ss.at[ring], s_rs.at[four], to_s)
 
     def x1_copy(j):
         ring = lax.rem(j, 2)
-        return remote(x1_send.at[ring], x1_recv.at[j], ss.at[1, ring], rs.at[0, j], to_x)
+        return remote(x1_send.at[ring], x1_recv(j), ss.at[1, ring], rs.at[0, j], to_x)
 
     def y1_copy(j):
         ring = lax.rem(j, 2)
-        return remote(
-            y1_send.at[ring, 1 - me_y], y1_recv.at[j], ss.at[2, ring], rs.at[1, j], to_y
-        )
+        return remote(y1_send.at[ring, 1 - me_y], y1_recv(j), ss.at[2, ring], rs.at[1, j], to_y)
 
     def x2_copy(j):
         ring = lax.rem(j, 2)
-        return remote(x2_send.at[ring], x2_recv.at[j], ss.at[3, ring], rs.at[2, j], to_x)
+        return remote(x2_send.at[ring], x2_recv(j), ss.at[3, ring], rs.at[2, j], to_x)
 
     def y2_copy(j):
         ring = lax.rem(j, 2)
-        return remote(y2_send.at[ring], y2_recv.at[j], ss.at[4, ring], rs.at[3, j], to_y)
+        return remote(y2_send.at[ring], y2_recv(j), ss.at[4, ring], rs.at[3, j], to_y)
 
     def z_copy(j, d):
         ring, other = lax.rem(j, 2), lax.rem(me_z + d, 4)
         return remote(
             z_send.at[ring, other],
-            z_recv.at[j, d - 1],
+            z_recv(j, d),
             z_ss.at[ring, d - 1],
             z_rs.at[j, d - 1],
             (dp, me_s, other),
@@ -920,11 +813,11 @@
         layer, i = place(j)
         return spread(j, (me_s, layer, pl.ds(0, 2), pl.ds(0, 4), i), 9, to_s)
 
-    def products(j, half, ahead, store):
+    def products(j, half, store):
         li, i = j // 9, lax.rem(j, 9)
         cols = pl.ds(pl.multiple_of(half * 256, 256), 256)
         for u in range(8):
-            x_to = ahead if u < 4 else 1 - ahead
+            x_to = 1 - me_x if u < 4 else me_x
             row = x_to * 2304 + (u % 4) * 576 + 64 * i
             tap = row // 512
             rows = pl.ds(pl.multiple_of(lax.rem(row, 512), 64), 64)
@@ -934,113 +827,150 @@
             for n in range(images):
                 p = jnp.dot(
                     at_v[li, rows, n * 128 : (n + 1) * 128],
-                    gr_v[li, shift + n, near, cols],
+                    gr_v[shift + n, near, cols],
                     preferred_element_type=full,
                 )
                 square = p * p if square is None else square + p * p
                 total = p if total is None else total + p
             store(u, x_to, u % 4, total, square)
 
+    def at_step(x):
+        j = jnp.where(x < 10, x, jnp.where(x < 14, x - 4, x - 5))
+        due = ((x >= 0) & (x < 6)) | ((x >= 10) & (x < 13)) | ((x >= 14) & (x < 23))
+        return j, due
+
     def step(k, carry):
-        @pl.when(k == 1)
-        def _():
-            load_grad(1).wait()
-
-        @pl.when((k >= 1) & (k < 9))
-        def _():
-            def few(n, carry):
-                shifted(1, (k - 1) * 4 + n)
-                return carry
-
-            lax.fori_loop(0, 4, few, 0)
-
-        @pl.when(k == 9)
-        def _():
-            load_act(1).wait()
-
-        @pl.when((k >= 2) & (k < steps))
-        def _():
-            side_copy(k - 2).wait_send()
-
-        @pl.when(k < steps)
-        def _():
-            ring = lax.rem(k, 2)
+        ja, due = at_step(k)
+
+        @pl.when(due & (ja >= 2))
+        def _():
+            side_copy(ja - 2).wait_send()
+
+        @pl.when(due)
+        def _():
+            ring = lax.rem(ja, 2)
 
             def store(u, x_to, z_to, total, square):
                 s_send[ring, u, 0] = total.astype(low)
                 s_send[ring, u, 1] = square.astype(low)
 
-            products(k, 1 - me_s, 0, store)
-            side_copy(k).start()
-
-        j = k - 1
-
-        @pl.when((j >= 2) & (j < steps))
-        def _():
-            x1_copy(j - 2).wait_send()
-            y1_copy(j - 2).wait_send()
-
-        @pl.when((j >= 0) & (j < steps))
-        def _():
-            ring, four = lax.rem(j, 2), lax.rem(j, 4)
-            side_copy(j).wait_recv()
+            products(ja, 1 - me_s, store)
+            side_copy(ja).start()
+
+        jb, due = at_step(k - 1)
+
+        @pl.when(due & (jb >= 2))
+        def _():
+            x1_copy(jb - 2).wait_send()
+            y1_copy(jb - 2).wait_send()
+
+        @pl.when(due)
+        def _():
+            ring, four = lax.rem(jb, 2), lax.rem(jb, 4)
+            side_copy(jb).wait_recv()
 
             def store(u, x_to, z_to, total, square):
-                got = s_recv[four, x_to * 4 + z_to].astype(full)
+                got = s_recv[four, u].astype(full)
                 both = (total + got[0], square + got[1])
                 for c in range(2):
                     if z_to < 2 and u < 4:
-                        x1_send[ring, z_to, c] = both[c].astype(low)
+                        x1_send[ring, z_to * 2 + c] = both[c].astype(low)
                     elif z_to < 2:
-                        x1_keep[ring, z_to, c] = both[c]
+                        x1_keep[ring, z_to * 2 + c] = both[c]
                     else:
+                        at = x_to * 2 + z_to - 2
                         for y_to in range(2):
-                            piece = both[c][y_to * 32 : y_to * 32 + 32]
-                            y1_send[ring, y_to, x_to, z_to - 2, c] = piece.astype(low)
-                            y1_keep[ring, y_to, x_to, z_to - 2, c] = piece
-
-            products(j, me_s, 1 - me_x, store)
-            x1_copy(j).start()
-            y1_copy(j).start()
-
-        j2 = k - 2
-
-        @pl.when((j2 >= 0) & (j2 < steps))
-        def _():
-            ring = lax.rem(j2, 2)
-
-            @pl.when(j2 >= 2)
+                            value = both[c][y_to * 32 : y_to * 32 + 32]
+                            y1_send[ring, y_to, at, c * 32 : c * 32 + 32, :] = value.astype(low)
+                            y1_keep[ring, y_to, at, c * 32 : c * 32 + 32, :] = value
+
+            products(jb, me_s, store)
+            x1_copy(jb).start()
+            y1_copy(jb).start()
+
+        j7, due = at_step(k - 12)
+
+        @pl.when(due)
+        def _():
+            @pl.when(j7 >= 2)
             def _():
-                x2_copy(j2 - 2).wait_send()
-                y2_copy(j2 - 2).wait_send()
-
-            x1_copy(j2).wait_recv()
-            here = pl.ds(pl.multiple_of(me_y * 32, 32), 32)
-            there = pl.ds(pl.multiple_of((1 - me_y) * 32, 32), 32)
-            for z_to in range(2):
-                for c in range(2):
-                    two_keep[ring, z_to, c] = x1_keep[ring, z_to, c, here, :] + x1_recv[
-                        j2, z_to, c, here, :
-                    ].astype(full)
-                    y2_send[ring, z_to, c] = (
-                        x1_keep[ring, z_to, c, there, :]
-                        + x1_recv[j2, z_to, c, there, :].astype(full)
-                    ).astype(low)
-            y2_copy(j2).start()
-            y1_copy(j2).wait_recv()
-            for z_to in range(2):
-                two_keep[ring, 2 + z_to] = y1_keep[ring, me_y, me_x, z_to] + y1_recv[
-                    j2, me_x, z_to
-                ].astype(full)
-                x2_send[ring, z_to] = (
-                    y1_keep[ring, me_y, 1 - me_x, z_to]
-                    + y1_recv[j2, 1 - me_x, z_to].astype(full)
-                ).astype(low)
-            x2_copy(j2).start()
-
-        j3 = k - 3
-
-        @pl.when((j3 >= 0) & (j3 < steps))
+                gs_copy(j7 - 2).wait_send()
+
+            g2x_copy(j7).wait_recv()
+            g2y_copy(j7).wait_recv()
+            gs_copy(j7).start()
+
+        j6, due = at_step(k - 10)
+
+        @pl.when(due)
+        def _():
+            @pl.when(j6 >= 2)
+            def _():
+                g2y_copy(j6 - 2).wait_send()
+                g2x_copy(j6 - 2).wait_send()
+
+            g1y_copy(j6).wait_recv()
+            g2x_copy(j6).start()
+            g1x_copy(j6).wait_recv()
+            g2y_copy(j6).start()
+
+        j5, due = at_step(k - 8)
+
+        @pl.when(due)
+        def _():
+            @pl.when(j5 >= 2)
+            def _():
+                g1y_copy(j5 - 2).wait_send()
+                g1x_copy(j5 - 2).wait_send()
+
+            local_copy(j5).wait()
+            for d in (1, 2, 3):
+                gz_copy(j5, d).wait_recv()
+            g1y_copy(j5).start()
+            g1x_copy(j5).start()
+
+        j4, due = at_step(k - 6)
+
+        @pl.when(due & (j4 == 0))
+        def _():
+            sc_local.wait()
+            sc_remote.wait_recv()
+
+        @pl.when(due)
+        def _():
+            ring, li, i = lax.rem(j4, 2), j4 // 9, lax.rem(j4, 9)
+
+            @pl.when(j4 >= 2)
+            def _():
+                for d in (1, 2, 3):
+                    gz_copy(j4 - 2, d).wait_send()
+
+            for d in (1, 2, 3):
+                z_copy(j4, d).wait_recv()
+            both = z_keep[ring, me_z]
+            for d in (1, 2, 3):
+                both = both + z_recv(j4, d)[...].astype(full)
+            scale = DECAY * sc_v[li, i] + (1.0 - DECAY) * both[32:64] / images_all
+            ns_v[li, i] = scale
+            div_v[ring] = (both[0:32] / total_out[3:4, 0:256] / (scale + DAMPING)).astype(low)
+            local_copy(j4).start()
+            for d in (1, 2, 3):
+                gz_copy(j4, d).start()
+
+        for li in range(2):
+            @pl.when(due & (j4 == 9 * li + 8) & (me_y == 1 - li))
+            def _():
+                pltpu.make_async_copy(ns_v.at[li], ns_out.at[:, me_y], misc_sem.at[3]).start()
+
+            @pl.when(due & (j4 == 9 * li + 8) & (me_y == li))
+            def _():
+                remote(
+                    ns_v.at[li], ns_out.at[:, me_y], misc_sem.at[4], misc_sem.at[5], to_y
+                ).start()
+
+        j3, due = at_step(k - 4)
+
+        @pl.when(due)
         def _():
             ring = lax.rem(j3, 2)
 
@@ -1052,105 +982,73 @@
             y2_copy(j3).wait_recv()
             x2_copy(j3).wait_recv()
             for z_to in range(4):
-                got = y2_recv[j3, z_to] if z_to < 2 else x2_recv[j3, z_to - 2]
+                got = y2_recv(j3)[z_to] if z_to < 2 else x2_recv(j3)[z_to - 2]
                 both = two_keep[ring, z_to] + got.astype(full)
                 z_keep[ring, z_to] = both
                 z_send[ring, z_to] = both.astype(low)
             for d in (1, 2, 3):
                 z_copy(j3, d).start()
 
-        j4 = k - 4
-
-        @pl.when(j4 == 0)
-        def _():
-            sc_local.wait()
-            sc_remote.wait_recv()
-
-        @pl.when((j4 >= 0) & (j4 < steps))
-        def _():
-            ring, li, i = lax.rem(j4, 2), j4 // 9, lax.rem(j4, 9)
-
-            @pl.when(j4 >= 2)
+        j2, due = at_step(k - 2)
+
+        @pl.when(due)
+        def _():
+            ring = lax.rem(j2, 2)
+
+            @pl.when(j2 >= 2)
             def _():
-                for d in (1, 2, 3):
-                    gz_copy(j4 - 2, d).wait_send()
-
-            for d in (1, 2, 3):
-                z_copy(j4, d).wait_recv()
-            got = z_recv[j4].astype(full)
-            both = z_keep[ring, me_z] + got[0] + got[1] + got[2]
-            scale = DECAY * sc_v[li, i] + (1.0 - DECAY) * both[1] / images_all
-            ns_v[li, i] = scale
-            div_v[ring] = (both[0] / weight_ref[3:4, 0:256] / (scale + DAMPING)).astype(low)
-            local_copy(j4).start()
-            for d in (1, 2, 3):
-                gz_copy(j4, d).start()
-
-        for li in range(2):
-            @pl.when((j4 == 9 * li + 8) & (me_y == 1 - li))
-            def _():
-                pltpu.make_async_copy(ns_v.at[li], ns_out.at[:, me_y], misc_sem.at[3]).start()
-
-            @pl.when((j4 == 9 * li + 8) & (me_y == li))
-            def _():
-                remote(
-                    ns_v.at[li], ns_out.at[:, me_y], misc_sem.at[4], misc_sem.at[5], to_y
-                ).start()
-
-        j5 = k - 5
-
-        @pl.when((j5 >= 0) & (j5 < steps))
-        def _():
-            @pl.when(j5 >= 2)
-            def _():
-                g1y_copy(j5 - 2).wait_send()
-                g1x_copy(j5 - 2).wait_send()
-
-            local_copy(j5).wait()
-            for d in (1, 2, 3):
-                gz_copy(j5, d).wait_recv()
-            g1y_copy(j5).start()
-            g1x_copy(j5).start()
-
-        j6 = k - 6
-
-        @pl.when((j6 >= 0) & (j6 < steps))
-        def _():
-            @pl.when(j6 >= 2)
-            def _():
-                g2y_copy(j6 - 2).wait_send()
-                g2x_copy(j6 - 2).wait_send()
-
-            g1y_copy(j6).wait_recv()
-            g2x_copy(j6).start()
-            g1x_copy(j6).wait_recv()
-            g2y_copy(j6).start()
-
-        j7 = k - 7
-
-        @pl.when(j7 >= 0)
-        def _():
-            @pl.when(j7 >= 2)
-            def _():
-                gs_copy(j7 - 2).wait_send()
-
-            g2x_copy(j7).wait_recv()
-            g2y_copy(j7).wait_recv()
-            gs_copy(j7).start()
+                x2_copy(j2 - 2).wait_send()
+                y2_copy(j2 - 2).wait_send()
+
+            x1_copy(j2).wait_recv()
+            here = pl.ds(pl.multiple_of(me_y * 32, 32), 32)
+            there = pl.ds(pl.multiple_of((1 - me_y) * 32, 32), 32)
+            got = x1_recv(j2)
+            for z_to in range(2):
+                for c in range(2):
+                    at, lines = z_to * 2 + c, slice(c * 32, c * 32 + 32)
+                    two_keep[ring, z_to, lines, :] = x1_keep[ring, at, here, :] + got[
+                        at, here, :
+                    ].astype(full)
+                    y2_send[ring, z_to, lines, :] = (
+                        x1_keep[ring, at, there, :] + got[at, there, :].astype(full)
+                    ).astype(low)
+            y2_copy(j2).start()
+            y1_copy(j2).wait_recv()
+            got = y1_recv(j2)
+            for z_to in range(2):
+                mine_at, other_at = me_x * 2 + z_to, (1 - me_x) * 2 + z_to
+                two_keep[ring, 2 + z_to] = y1_keep[ring, me_y, mine_at] + got[mine_at].astype(full)
+                x2_send[ring, z_to] = (
+                    y1_keep[ring, me_y, other_at] + got[other_at].astype(full)
+                ).astype(low)
+            x2_copy(j2).start()
+
+        @pl.when((k >= 6) & (k < 9))
+        def _():
+            lax.fori_loop(0, 3, lambda t, carry: back((k - 6) * 3 + t, carry), 0)
+
+        @pl.when(k == 8)
+        def _():
+            sum_middle(4, head_one, head_two)
+
+        @pl.when(k == 9)
+        def _():
+            gammas, betas = lax.fori_loop(0, 8, d_line, (zero, zero))
+            put_sums(3, gammas, betas)
+
+        @pl.when(k == 10)
+        def _():
+            sum_middle(3, small_one.at[3], small_two.at[3])
+
+        @pl.when(k == 13)
+        def _():
+            sum_arrived(3, small_two.at[3])
+            bottom()
 
         return carry
 
-    load_grad(0).wait()
-
-    def build(n, carry):
-        shifted(0, n)
-        return carry
-
-    lax.fori_loop(0, images, build, 0)
-    load_grad(1).start()
-    load_act(0).wait()
-    load_act(1).start()
-    lax.fori_loop(0, steps + 7, step, 0)
+    lax.fori_loop(0, steps + 5 + 12, step, 0)
 
     def finish(j, carry):
         gs_copy(j).wait_recv()
@@ -1171,49 +1069,72 @@
         for d in (1, 2, 3):
             z_copy(j, d).wait_send()
             gz_copy(j, d).wait_send()
-
-
-def statistics(act_turned, grad_turned, scales, total, images_all):
-    images = act_turned.shape[2] // 128
-    dma = pltpu.SemaphoreType.DMA
-    low, full = jnp.bfloat16, jnp.float32
-    tile, piece = (2, 64, 256), (2, 32, 256)
-    any_spec = pl.BlockSpec(memory_space=pl.ANY)
-    divided, new_scales = pl.pallas_call(
-        functools.partial(statistics_kernel, images, images_all),
+    for n in range(4):
+        sum_sent(n, small_one.at[n], small_two.at[n])
+    sum_sent(4, head_one, head_two)
+
+
+def whole_step(
+    feats, size_group, labels, class_wt, owners, basis_in, basis_out, master, norm_params, head, scales
+):
+    count_img, side_len, _, width = feats.shape
+    images_all = count_img * lax.axis_size("dp") * lax.axis_size("side") * lax.axis_size("blk")
+    low, full, dma = jnp.bfloat16, jnp.float32, pltpu.SemaphoreType.DMA
+    vmem, any_spec = pl.BlockSpec(memory_space=pltpu.VMEM), pl.BlockSpec(memory_space=pl.ANY)
+    smem = pl.BlockSpec(memory_space=pltpu.SMEM)
+    rows = count_img * side_len * side_len
+    divided, new_scales, total, norm_sums, head_sums = pl.pallas_call(
+        functools.partial(step_kernel, images_all),
         out_shape=[
             jax.ShapeDtypeStruct((2, 2, 2, 4, 9, 2, 32, 256), low),
             jax.ShapeDtypeStruct((9, 2, 32, 256), full),
+            jax.ShapeDtypeStruct((4, width), full),
+            jax.ShapeDtypeStruct((2, 4, width), full),
+            jax.ShapeDtypeStruct((24, width), full),
         ],
-        in_specs=[any_spec, any_spec, any_spec, pl.BlockSpec(memory_space=pltpu.VMEM)],
-        out_specs=[any_spec, any_spec],
+        in_specs=[vmem, smem, smem, smem, smem, any_spec, vmem, vmem, vmem, vmem, any_spec],
+        out_specs=[any_spec, any_spec, vmem, vmem, vmem],
         scratch_shapes=[
-            pltpu.VMEM((2, 512, images * 128), low),
-            pltpu.VMEM((images, 128, 512), low),
-            pltpu.VMEM((2, 3 * images, 160, 512), low),
+            pltpu.VMEM((18, 2, 4, 64, 512), low),
+            pltpu.VMEM((10, 10, 32, 512), low),
+            pltpu.VMEM((rows, 512), full),
+            pltpu.VMEM((rows, 512), full),
+            pltpu.VMEM((2, 512, 4096), low),
+            pltpu.VMEM((96, 160, 512), low),
+            pltpu.VMEM((32, 512), full),
+            pltpu.VMEM((32, 128), full),
+            pltpu.VMEM((32, 128), full),
+            pltpu.VMEM((10, 64, 512), full),
+            pltpu.VMEM((2, 512, 512), low),
+            pltpu.VMEM((4, 8, 4, 512), full),
+            pltpu.VMEM((4, 4, 4, 512), full),
+            pltpu.VMEM((8, 24, 512), full),
+            pltpu.VMEM((4, 24, 512), full),
             pltpu.VMEM((2, 9, 32, 256), full),
             pltpu.VMEM((2, 9, 32, 256), full),
             pltpu.VMEM((2, 32, 256), low),
-            pltpu.VMEM((2, 8) + tile, low),
-            pltpu.VMEM((4, 8) + tile, low),
-            pltpu.VMEM((2, 2) + tile, low),
-            pltpu.VMEM((18, 2) + tile, low),
-            pltpu.VMEM((2, 2) + tile, full),
-            pltpu.VMEM((2, 2, 2, 2) + piece, low),
-            pltpu.VMEM((18, 2, 2) + piece, low),
-            pltpu.VMEM((2, 2, 2, 2) + piece, full),
-            pltpu.VMEM((2, 2) + piece, low),
-            pltpu.VMEM((18, 2) + piece, low),
-            pltpu.VMEM((2, 2) + piece, low),
-            pltpu.VMEM((18, 2) + piece, low),
-            pltpu.VMEM((2, 4) + piece, full),
-            pltpu.VMEM((2, 4) + piece, low),
-            pltpu.VMEM((18, 3) + piece, low),
-            pltpu.VMEM((2, 4) + piece, full),
-            dma((4,)),
+            pltpu.VMEM((2, 8, 2, 64, 256), low),
+            pltpu.VMEM((4, 8, 2, 64, 256), low),
+            pltpu.VMEM((2, 4, 64, 256), low),
+            pltpu.VMEM((2, 4, 64, 256), full),
+            pltpu.VMEM((2, 2, 4, 64, 256), low),
+            pltpu.VMEM((2, 2, 4, 64, 256), full),
+            pltpu.VMEM((2, 2, 64, 256), low),
+            pltpu.VMEM((2, 2, 64, 256), low),
+            pltpu.VMEM((2, 4, 64, 256), full),
+            pltpu.VMEM((2, 4, 64, 256), low),
+            pltpu.VMEM((2, 4, 64, 256), full),
+            dma((1,)),
+            dma((6, 18)),
+            dma((6, 18)),
+            dma((5, 8)),
+            dma((5, 8)),
+            dma((5, 4)),
+            dma((5, 4)),
             dma((6,)),
             dma((2,)),
             dma((10, 2)),
+            dma((2,)),
             dma((4,)),
             dma((9, 18)),
             dma((2, 3)),
@@ -1221,61 +1142,209 @@
             dma((2, 3)),
             dma((18, 3)),
         ],
-        name="statistics",
+        name="whole_step",
         compiler_params=pltpu.CompilerParams(
             collective_id=0, has_side_effects=True, vmem_limit_bytes=63 * 2**20
         ),
     )(
-        act_turned,
-        grad_turned,
+        feats,
+        size_group,
+        labels,
+        class_wt,
+        owners,
+        master,
+        norm_params,
+        head,
+        basis_in,
+        basis_out,
         scales.reshape(9, 2, 32, 256),
+    )
+    return (
+        divided.reshape(2, 18, 512, 256),
+        new_scales.reshape(576, 256),
         total,
+        norm_sums,
+        head_sums,
     )
-    return divided.reshape(2, 18, 512, 256), new_scales.reshape(576, 256)
-
-
-def owned_kernel(
-    which, divided, rows_ref, cols_ref, w_ref, m_ref, v_ref, new_w, new_m, new_v
+
+
+def update_kernel(
+    owners_ref,
+    divided,
+    basis_in,
+    basis_out,
+    w_hbm,
+    m_hbm,
+    v_hbm,
+    total_ref,
+    norm_sums,
+    head_sums,
+    norm_w,
+    norm_m,
+    norm_v,
+    head_w,
+    head_m,
+    head_v,
+    w_out,
+    m_out,
+    v_out,
+    norm_w_out,
+    norm_m_out,
+    norm_v_out,
+    head_w_out,
+    head_m_out,
+    head_v_out,
+    loss_out,
+    weight_out,
+    matrix,
+    p_v,
+    rows_v,
+    cols_v,
+    w_v,
+    m_v,
+    v_v,
+    gradients,
+    in_sem,
+    out_sem,
 ):
     low, full = jnp.bfloat16, jnp.float32
-    held = which[1, pl.program_id(0)].astype(full)
-    rows = rows_ref[0]
-    turned = [
-        jnp.dot(rows, divided[s, 0], preferred_element_type=full).astype(low) for s in range(2)
-    ]
-    gradient = lax.dot_general(
-        jnp.concatenate(turned, axis=1),
-        cols_ref[0],
-        (((1,), (1,)), ((), ())),
-        preferred_element_type=full,
+    slots, half, width = w_v.shape
+    blk, side = lax.axis_index("blk"), lax.axis_index("side")
+
+    def state_in(q):
+        return [
+            pltpu.make_async_copy(src.at[q], dst.at[q], in_sem.at[n, q])
+            for n, (src, dst) in enumerate(((w_hbm, w_v), (m_hbm, m_v), (v_hbm, v_v)))
+        ]
+
+    def state_out(q):
+        return [
+            pltpu.make_async_copy(src.at[q], dst.at[q], out_sem.at[n, q])
+            for n, (src, dst) in enumerate(((w_v, w_out), (m_v, m_out), (v_v, v_out)))
+        ]
+
+    rows_in = pltpu.make_async_copy(
+        basis_in.at[:, pl.ds(pl.multiple_of(side * half, half), half)], rows_v, in_sem.at[4, 0]
     )
-    new_w[0], new_m[0], new_v[0] = adamw(
-        w_ref[0], m_ref[0], v_ref[0], gradient * held, RATE_CONV
+    cols_in = pltpu.make_async_copy(basis_out, cols_v, in_sem.at[4, 1])
+    rows_in.start()
+    cols_in.start()
+
+    for q in range(slots):
+        matrix[q] = 0
+    count = jnp.zeros((), jnp.int32)
+    for m in range(owners_ref.shape[0]):
+        mine = owners_ref[m] == blk
+
+        @pl.when(mine)
+        def _():
+            matrix[count] = m
+
+        count = count + jnp.where(mine, 1, 0)
+
+    def part_in(q):
+        return pltpu.make_async_copy(divided.at[:, matrix[q]], p_v.at[q], in_sem.at[3, q])
+
+    for q in range(slots):
+        part_in(q).start()
+        for copy in state_in(q):
+            copy.start()
+    weight = total_ref[3:4, 0:1]
+    weight_out[0, 0] = total_ref[3, 0]
+    loss_out[0, 0] = head_sums[17, 0]
+    for layer in range(2):
+        norm_w_out[layer], norm_m_out[layer], norm_v_out[layer] = adamw(
+            norm_w[layer],
+            norm_m[layer],
+            norm_v[layer],
+            norm_sums[layer, 0:2, :] / weight,
+            RATE_NORM,
+        )
+    classes = head_w.shape[0]
+    here = lax.broadcasted_iota(jnp.int32, (classes, classes), 0)
+    there = lax.broadcasted_iota(jnp.int32, (classes, classes), 1)
+    line = jnp.broadcast_to(head_sums[16:17, 0:classes], (classes, classes))
+    bias = jnp.sum(jnp.where(here == there, line, 0.0), axis=1, keepdims=True)
+    for at, gradient in (
+        (slice(0, width), head_sums[0:classes, :]),
+        (slice(width, width + 1), bias),
+    ):
+        head_w_out[:, at], head_m_out[:, at], head_v_out[:, at] = adamw(
+            head_w[:, at], head_m[:, at], head_v[:, at], gradient / weight, RATE_HEAD
+        )
+    rows_in.wait()
+    cols_in.wait()
+
+    def gradient(q):
+        layer = matrix[q] // TAPS
+        held = jnp.where(q < count, 1.0, 0.0).astype(full)
+        both = [
+            jnp.dot(rows_v[layer], p_v[q, s], preferred_element_type=full).astype(low)
+            for s in range(2)
+        ]
+        return held * lax.dot_general(
+            jnp.concatenate(both, axis=1),
+            cols_v[layer],
+            (((1,), (1,)), ((), ())),
+            preferred_element_type=full,
+        )
+
+    part_in(0).wait()
+    gradients[0] = gradient(0)
+    for q in range(slots):
+        for copy in state_in(q):
+            copy.wait()
+        if q + 1 < slots:
+            part_in(q + 1).wait()
+            gradients[(q + 1) % 2] = gradient(q + 1)
+        w_v[q], m_v[q], v_v[q] = adamw(w_v[q], m_v[q], v_v[q], gradients[q % 2], RATE_CONV)
+        for copy in state_out(q):
+            copy.start()
+    for q in range(slots):
+        for copy in state_out(q):
+            copy.wait()
+
+
+def update(
+    owners, divided, basis_in, basis_out, states, total, norm_sums, head_sums, norm_states, head_states
+):
+    full, dma = jnp.float32, pltpu.SemaphoreType.DMA
+    slots, half, width = states[0].shape
+    vmem, any_spec = pl.BlockSpec(memory_space=pltpu.VMEM), pl.BlockSpec(memory_space=pl.ANY)
+    smem = pl.BlockSpec(memory_space=pltpu.SMEM)
+    like = [jax.ShapeDtypeStruct(x.shape, full) for x in (*states, *norm_states, *head_states)]
+    one = jax.ShapeDtypeStruct((1, 1), full)
+    return pl.pallas_call(
+        update_kernel,
+        out_shape=like + [one, one],
+        in_specs=[smem] + [any_spec] * 6 + [vmem] * 9,
+        out_specs=[any_spec] * 3 + [vmem] * 6 + [smem] * 2,
+        scratch_shapes=[
+            pltpu.SMEM((slots,), jnp.int32),
+            pltpu.VMEM((slots, 2, width, half), jnp.bfloat16),
+            pltpu.VMEM((2, half, width), jnp.bfloat16),
+            pltpu.VMEM((2, width, width), jnp.bfloat16),
+            pltpu.VMEM(states[0].shape, full),
+            pltpu.VMEM(states[0].shape, full),
+            pltpu.VMEM(states[0].shape, full),
+            pltpu.VMEM((2, half, width), full),
+            dma((5, slots)),
+            dma((3, slots)),
+        ],
+        name="update",
+        compiler_params=pltpu.CompilerParams(vmem_limit_bytes=63 * 2**20),
+    )(
+        owners,
+        divided,
+        basis_in,
+        basis_out,
+        *states,
+        total,
+        norm_sums,
+        head_sums,
+        *norm_states,
+        *head_states,
     )
-
-
-def owned_update(divided, basis_in, basis_out, master, moment1, moment2, which):
-    slots, half, width = master.shape
-    block = pl.BlockSpec((1, half, width), lambda q, which: (q, 0, 0))
-    return pl.pallas_call(
-        owned_kernel,
-        grid_spec=pltpu.PrefetchScalarGridSpec(
-            num_scalar_prefetch=1,
-            grid=(slots,),
-            in_specs=[
-                pl.BlockSpec((2, 1, width, half), lambda q, which: (0, which[0, q], 0, 0)),
-                pl.BlockSpec((1, half, width), lambda q, which: (which[0, q] // TAPS, which[2, q], 0)),
-                pl.BlockSpec((1, width, width), lambda q, which: (which[0, q] // TAPS, 0, 0)),
-                block,
-                block,
-                block,
-            ],
-            out_specs=[block, block, block],
-        ),
-        out_shape=[jax.ShapeDtypeStruct(master.shape, jnp.float32)] * 3,
-        name="owned_update",
-        compiler_params=pltpu.CompilerParams(vmem_limit_bytes=63 * 2**20),
-    )(which, divided, basis_in, basis_out, master, moment1, moment2)
 
 
 def shards_general(
@@ -1457,13 +1526,7 @@
     head_m,
     head_v,
 ):
-    classes = class_wt.shape[0]
-    width = feats.shape[3]
-    slots_dev = master.shape[0]
-    index = jnp.arange(owners.shape[0])
-    earlier = (owners[:, None] == owners[None, :]) & (index[None, :] < index[:, None])
-    slot = owners * slots_dev + jnp.sum(earlier.astype(jnp.int32), axis=1)
-    act_turned, grad_turned, total, norm_sums, head_sums = sweep(
+    divided, new_scales, total, norm_sums, head_sums = whole_step(
         feats,
         size_group,
         labels,
@@ -1473,42 +1536,23 @@
         basis_out,
         master,
         norm_params,
-        head,
+        head.T,
+        scales,
     )
-    weight_all = total[3, 0]
-    images_all = feats.shape[0] * lax.axis_size("dp") * lax.axis_size("side") * lax.axis_size("blk")
-    slot_ids = lax.axis_index("blk") * slots_dev + jnp.arange(slots_dev)
-    hits = slot[None, :] == slot_ids[:, None]
-    which = jnp.stack(
-        [
-            jnp.sum(jnp.where(hits, index[None, :], 0), axis=1),
-            jnp.sum(hits.astype(jnp.int32), axis=1),
-            jnp.full((slots_dev,), lax.axis_index("side"), jnp.int32),
-        ]
-    ).astype(jnp.int32)
-    divided, new_scales = statistics(act_turned, grad_turned, scales, total, images_all)
-    new_master, new_moment1, new_moment2 = owned_update(
-        divided, basis_in, basis_out, master, moment1, moment2, which
+    results = update(
+        owners,
+        divided,
+        basis_in,
+        basis_out,
+        (master, moment1, moment2),
+        total,
+        norm_sums,
+        head_sums,
+        (norm_params, norm_m, norm_v),
+        (head.T, head_m.T, head_v.T),
     )
-    new_norm, new_norm_m, new_norm_v = adamw(
-        norm_params, norm_m, norm_v, norm_sums[:, :2] / weight_all, RATE_NORM
-    )
-    head_all = jnp.concatenate([head_sums[:classes].T, head_sums[16:17, :classes]], axis=0)
-    new_head, new_head_m, new_head_v = adamw(head, head_m, head_v, head_all / weight_all, RATE_HEAD)
-    return (
-        head_sums[17, 0],
-        weight_all,
-        new_scales,
-        new_master,
-        new_moment1,
-        new_moment2,
-        new_norm,
-        new_norm_m,
-        new_norm_v,
-        new_head,
-        new_head_m,
-        new_head_v,
-    )
+    loss_all, weight_all = results[9][0, 0], results[10][0, 0]
+    return (loss_all, weight_all, new_scales, *results[:6], *(x.T for x in results[6:9]))
 
 
 def shards(*args):

time: 308 us -> 294 us (0.955)
  local copies, waits for them, and re-layouts: 4.99 us -> 0.82 us
  Pallas kernels: 296 us -> 292 us
  other arithmetic: 3.63 us -> 0 us
    pallas_call x3 -> x2, Pallas kernels: 296 us -> 292 us  [the longest x1 274 us: whole_step(): pl.pallas_call(functools.partial(step_kernel, images_all), out_shape=[jax...]
where the time goes in v5:
time: 294 us; the launch traced here: 293 us
  Pallas kernels  292 us (99%)
    pallas_call x1, Pallas kernels, whole_step(): pl.pallas_call(functools.partial(step_kernel, images_all), out_shape=[jax...  274 us
    pallas_call x1, Pallas kernels, update(): pl.pallas_call(update_kernel, out_shape=like + [one, one], in_specs=[smem...  17.8 us

profile of v5, /device:TPU:0, one launch (start us, length us, event | category | flops | bytes accessed | tf_op | source)
XLA Modules:
  0.0 293.4 jit_solution(13467808173149901956)
XLA Ops:
  0.6 274.1 %whole_step.1 = (bf16[2,2,2,4,9,2,32,256]{7,6,5,4,3,2,1,0:T(8,128)(2,1)}, f32[9,2,32,256]{3,2,1,0:T(8,128)}, f32[4,512]{1,0:T(4,128)}, f32[2,4,512]{2,1,0:T(4,128)}, f32[24,512]{1,0:T(8,128)}) custom-call(bf16[32,8,8,512]{3,2,1,0:T(8,128)(2,1)} %feats_ref.1, s32[32]{0:T(128)} %image_group.1, s32[32]{0:T(128)} %labels_ref.1, s32[10]{0:T(128)} %class_ref.1, ...), custom_call_target="tpu_custom_call" | custom-call | tf_op jit(solution)/shard_map/whole_step/pallas_call | solution.py:1086
  274.8 0.0 copy-start
  274.8 17.8 %update.1 = (f32[10,256,512]{2,1,0:T(8,128)}, f32[10,256,512]{2,1,0:T(8,128)}, f32[10,256,512]{2,1,0:T(8,128)}, f32[2,2,512]{2,1,0:T(2,128)}, f32[2,2,512]{2,1,0...) custom-call(s32[18]{0:T(128)} %owners_ref.3, ...), custom_call_target="tpu_custom_call" | custom-call | tf_op jit(solution)/shard_map/update/pallas_call | solution.py:1317
  292.6 0.0 copy-done
  292.6 0.8 copy.30
Async XLA Ops:
  274.8 17.8 %copy-start = (f32[9,2,32,256]{3,2,1,0:T(8,128)S(1)}, f32[9,2,32,256]{3,2,1,0:T(8,128)}, u32[]{:S(2)}) copy-start(f32[9,2,32,256]{3,2,1,0:T(8,128)} %get-tuple-element.34) | copy-start | bytes 1769476

commit v6 on v5

--- a/solution.py
+++ b/solution.py
@@ -306,7 +306,7 @@
             def _():
                 odd_copy(m4).start()
 
-        m6 = t - 10
+        m6 = t - 11
 
         @pl.when((m6 >= 0) & (m6 < matrices))
         def _():
@@ -525,7 +525,7 @@
         core_copy(TAPS + tap).wait_recv()
         conv_tap(tap, TAPS + tap, conv_b)
 
-        @pl.when(tap < 4)
+        @pl.when(tap < 5)
         def _():
             gather(24 + tap)
 
@@ -571,6 +571,52 @@
     picked = jnp.sum(hot * log_prob, axis=1, keepdims=True)
     loss = -column(weight_ref[:, 0:1] * picked)
     d_logits = image_weight * (jnp.exp(log_prob) - hot)
+    d_pooled = (
+        lax.dot_general(
+            d_logits,
+            head_low.astype(full),
+            (((1,), (0,)), ((), ())),
+            precision=highest,
+            preferred_element_type=full,
+        )
+        / pixels
+    )
+
+    def d_line_top(p, carry):
+        gammas, betas = carry
+        for q in range(8):
+            at = cell(p * 8 + q)
+            normed, pre, sigma = activation(conv_b[at, :], 1, average_b, inv_b)
+            d_pre = d_pooled * mask_of(p, q) * sigma * (1.0 + pre * (1.0 - sigma))
+            gammas = gammas + d_pre * normed
+            betas = betas + d_pre
+        return gammas, betas
+
+    gammas, betas = lax.fori_loop(0, 8, d_line_top, (zero, zero))
+
+    def put_sums(n, gammas, betas):
+        small_one[n, mine, 0:1, :] = column(gammas)
+        small_one[n, mine, 1:2, :] = column(betas)
+        small_one[n, mine, 2:4, :] = jnp.zeros((2, width), full)
+        sum_start(n, small_one.at[n])
+
+    def sent(m, carry):
+        @pl.when(me_z < 3)
+        def _():
+            right_copy(m).wait_send()
+
+        @pl.when(me_z > 0)
+        def _():
+            left_copy(m).wait_send()
+
+        x_copy(m).wait_send()
+        y_copy(m).wait_send()
+        even_copy(m).wait_send()
+        core_copy(m).wait_send()
+        return carry
+
+    lax.fori_loop(0, matrices, sent, 0)
+    put_sums(2, gammas, betas)
     grad_head = lax.dot_general(
         d_logits,
         pooled_low.astype(full),
@@ -582,52 +628,13 @@
     head_one[mine, 0:classes, :] = grad_head
     head_one[mine, 16:17, 0:classes] = column(d_logits)
     head_one[mine, 17:18, :] = jnp.broadcast_to(loss, (1, width))
-    d_pooled = (
-        lax.dot_general(
-            d_logits,
-            head_low.astype(full),
-            (((1,), (0,)), ((), ())),
-            precision=highest,
-            preferred_element_type=full,
-        )
-        / pixels
-    )
-
-    def d_line_top(p, carry):
-        gammas, betas = carry
-        for q in range(8):
-            at = cell(p * 8 + q)
-            normed, pre, sigma = activation(conv_b[at, :], 1, average_b, inv_b)
-            d_pre = d_pooled * mask_of(p, q) * sigma * (1.0 + pre * (1.0 - sigma))
-            gammas = gammas + d_pre * normed
-            betas = betas + d_pre
-        return gammas, betas
-
-    gammas, betas = lax.fori_loop(0, 8, d_line_top, (zero, zero))
-
-    def put_sums(n, gammas, betas):
-        small_one[n, mine, 0:1, :] = column(gammas)
-        small_one[n, mine, 1:2, :] = column(betas)
-        small_one[n, mine, 2:4, :] = jnp.zeros((2, width), full)
-        sum_start(n, small_one.at[n])
-
-    def sent(m, carry):
-        @pl.when(me_z < 3)
-        def _():
-            right_copy(m).wait_send()
-
-        @pl.when(me_z > 0)
-        def _():
-            left_copy(m).wait_send()
-
-        x_copy(m).wait_send()
-        y_copy(m).wait_send()
-        even_copy(m).wait_send()
-        core_copy(m).wait_send()
+
+    def clear(n, carry):
+        gr_v[n, 0:16, :] = jnp.zeros((16, width), low)
+        gr_v[n, 144:160, :] = jnp.zeros((16, width), low)
         return carry
 
-    lax.fori_loop(0, matrices, sent, 0)
-    put_sums(2, gammas, betas)
+    lax.fori_loop(0, 3 * images, clear, 0)
 
     sum_middle(2, small_one.at[2], small_two.at[2])
     total_b = sum_end(2, small_two.at[2])
@@ -697,12 +704,6 @@
 
         return line
 
-    def clear(n, carry):
-        gr_v[n, 0:16, :] = jnp.zeros((16, width), low)
-        gr_v[n, 144:160, :] = jnp.zeros((16, width), low)
-        return carry
-
-    lax.fori_loop(0, 3 * images, clear, 0)
     lax.fori_loop(0, 8, turn_grads(1), 0)
 
     def bottom():
@@ -719,7 +720,6 @@
 
         lax.fori_loop(0, 8, line, 0)
         lax.fori_loop(0, 8, turn_grads(0), 0)
-        head_out[...] = sum_end(4, head_two)
 
     def x1_recv(j):
         return w_full.at[j, 0, :, :, 0:256]
@@ -1040,6 +1040,10 @@
         @pl.when(k == 10)
         def _():
             sum_middle(3, small_one.at[3], small_two.at[3])
+
+        @pl.when(k == 25)
+        def _():
+            head_out[...] = sum_end(4, head_two)
 
         @pl.when(k == 13)
         def _():
@@ -1203,7 +1207,6 @@
     w_v,
     m_v,
     v_v,
-    gradients,
     in_sem,
     out_sem,
 ):
@@ -1289,17 +1292,17 @@
             preferred_element_type=full,
         )
 
-    part_in(0).wait()
-    gradients[0] = gradient(0)
-    for q in range(slots):
+    def slot(q, carry):
+        part_in(q).wait()
+        change = gradient(q)
         for copy in state_in(q):
             copy.wait()
-        if q + 1 < slots:
-            part_in(q + 1).wait()
-            gradients[(q + 1) % 2] = gradient(q + 1)
-        w_v[q], m_v[q], v_v[q] = adamw(w_v[q], m_v[q], v_v[q], gradients[q % 2], RATE_CONV)
+        w_v[q], m_v[q], v_v[q] = adamw(w_v[q], m_v[q], v_v[q], change, RATE_CONV)
         for copy in state_out(q):
             copy.start()
+        return carry
+
+    lax.fori_loop(0, slots, slot, 0)
     for q in range(slots):
         for copy in state_out(q):
             copy.wait()
@@ -1327,7 +1330,6 @@
             pltpu.VMEM(states[0].shape, full),
             pltpu.VMEM(states[0].shape, full),
             pltpu.VMEM(states[0].shape, full),
-            pltpu.VMEM((2, half, width), full),
             dma((5, slots)),
             dma((3, slots)),
         ],

time: 294 us -> 289 us (0.983)
  Pallas kernels: 292 us -> 288 us
where the time goes in v6:
time: 289 us
  Pallas kernels  288 us (100%)
    pallas_call x1, Pallas kernels, whole_step(): pl.pallas_call(functools.partial(step_kernel, images_all), out_shape=[jax...  272 us
    pallas_call x1, Pallas kernels, update(): pl.pallas_call(update_kernel, out_shape=like + [one, one], in_specs=[smem...  15.8 us

profile of v6, /device:TPU:0, one launch (start us, length us, event | category | flops | bytes accessed | tf_op | source)
XLA Modules:
  0.0 289.2 jit_solution(211363886631075747)
XLA Ops:
  0.6 271.8 %whole_step.1 = (bf16[2,2,2,4,9,2,32,256]{7,6,5,4,3,2,1,0:T(8,128)(2,1)}, f32[9,2,32,256]{3,2,1,0:T(8,128)}, f32[4,512]{1,0:T(4,128)}, f32[2,4,512]{2,1,0:T(4,128)}, f32[24,512]{1,0:T(8,128)}) custom-call(bf16[32,8,8,512]{3,2,1,0:T(8,128)(2,1)} %feats_ref.1, s32[32]{0:T(128)} %image_group.1, s32[32]{0:T(128)} %labels_ref.1, s32[10]{0:T(128)} %class_ref.1, ...), custom_call_target="tpu_custom_call" | custom-call | tf_op jit(solution)/shard_map/whole_step/pallas_call | solution.py:1090
  272.5 0.0 copy-start
  272.5 15.8 %update.1 = (f32[10,256,512]{2,1,0:T(8,128)}, f32[10,256,512]{2,1,0:T(8,128)}, f32[10,256,512]{2,1,0:T(8,128)}, f32[2,2,512]{2,1,0:T(2,128)}, f32[2,2,512]{2,1,0...) custom-call(s32[18]{0:T(128)} %owners_ref.3, ...), custom_call_target="tpu_custom_call" | custom-call | tf_op jit(solution)/shard_map/update/pallas_call | solution.py:1320
  288.3 0.0 copy-done
  288.4 0.8 copy.30
Async XLA Ops:
  272.5 15.9 %copy-start = (f32[9,2,32,256]{3,2,1,0:T(8,128)S(1)}, f32[9,2,32,256]{3,2,1,0:T(8,128)}, u32[]{:S(2)}) copy-start(f32[9,2,32,256]{3,2,1,0:T(8,128)} %get-tuple-element.34) | copy-start | bytes 1769476

commit v7 on v6

--- a/solution.py
+++ b/solution.py
@@ -81,7 +81,7 @@
 
 def step_kernel(
     images_all,
-    feats_ref,
+    feats_hbm,
     image_group,
     labels_ref,
     class_ref,
@@ -89,8 +89,8 @@
     master_hbm,
     params_ref,
     head_ref,
-    basis_in_ref,
-    basis_out_ref,
+    basis_in_hbm,
+    basis_out_hbm,
     scales_hbm,
     out,
     ns_out,
@@ -126,6 +126,9 @@
     two_keep,
     z_send,
     z_keep,
+    feats_ref,
+    basis_in_ref,
+    basis_out_ref,
     out_sem,
     g_ss,
     g_rs,
@@ -187,6 +190,12 @@
         master_hbm.at[:, pl.ds(pl.multiple_of(dp * 64, 64), 64)], piece, out_sem.at[0]
     )
     piece_copy.start()
+    feats_in = pltpu.make_async_copy(feats_hbm, feats_ref, out_sem.at[1])
+    basis_in_in = pltpu.make_async_copy(basis_in_hbm, basis_in_ref, out_sem.at[2])
+    basis_out_in = pltpu.make_async_copy(basis_out_hbm, basis_out_ref, out_sem.at[3])
+    feats_in.start()
+    basis_in_in.start()
+    basis_out_in.start()
 
     near = [(a, b) for a in range(4) for b in range(2) if a or b]
     barrier = pltpu.get_barrier_semaphore()
@@ -364,12 +373,16 @@
     for t in range(3):
         gather(t)
     xpad[...] = jnp.zeros_like(xpad)
+    basis_in_in.wait()
     basis_t[0] = basis_in_ref[0].T
     place = lax.broadcasted_iota(jnp.int32, (1, 128), 1)
     for n in range(images):
         group_ref[n : n + 1, :] = jnp.full((1, width), full_map(n), full)
         hot_ref[n : n + 1, :] = jnp.where(place == labels_ref[n], 1.0, 0.0).astype(full)
         weight_ref[n : n + 1, :] = jnp.full((1, 128), class_ref[labels_ref[n]].astype(full), full)
+
+    feats_in.wait()
+    basis_out_in.wait()
 
     def first(t, carry):
         gather(t)
@@ -506,6 +519,10 @@
         return jnp.swapaxes(jnp.stack(values), 0, 1)
 
     def act_line(p, carry):
+        @pl.when(lax.rem(p, 4) == 3)
+        def _():
+            gather(24 + p // 4)
+
         for g in range(2):
             acts = []
             for q in range(8):
@@ -525,9 +542,9 @@
         core_copy(TAPS + tap).wait_recv()
         conv_tap(tap, TAPS + tap, conv_b)
 
-        @pl.when(tap < 5)
-        def _():
-            gather(24 + tap)
+        @pl.when(tap < 3)
+        def _():
+            gather(26 + tap)
 
         return carry
 
@@ -1096,7 +1113,7 @@
             jax.ShapeDtypeStruct((2, 4, width), full),
             jax.ShapeDtypeStruct((24, width), full),
         ],
-        in_specs=[vmem, smem, smem, smem, smem, any_spec, vmem, vmem, vmem, vmem, any_spec],
+        in_specs=[any_spec, smem, smem, smem, smem, any_spec, vmem, vmem, any_spec, any_spec, any_spec],
         out_specs=[any_spec, any_spec, vmem, vmem, vmem],
         scratch_shapes=[
             pltpu.VMEM((18, 2, 4, 64, 512), low),
@@ -1128,7 +1145,10 @@
             pltpu.VMEM((2, 4, 64, 256), full),
             pltpu.VMEM((2, 4, 64, 256), low),
             pltpu.VMEM((2, 4, 64, 256), full),
-            dma((1,)),
+            pltpu.VMEM(feats.shape, low),
+            pltpu.VMEM(basis_in.shape, low),
+            pltpu.VMEM(basis_out.shape, low),
+            dma((4,)),
             dma((6, 18)),
             dma((6, 18)),
             dma((5, 8)),
@@ -1175,6 +1195,7 @@
 def update_kernel(
     owners_ref,
     divided,
+    scales_in,
     basis_in,
     basis_out,
     w_hbm,
@@ -1200,6 +1221,7 @@
     head_v_out,
     loss_out,
     weight_out,
+    scales_out,
     matrix,
     p_v,
     rows_v,
@@ -1207,6 +1229,7 @@
     w_v,
     m_v,
     v_v,
+    scales_v,
     in_sem,
     out_sem,
 ):
@@ -1230,6 +1253,9 @@
         basis_in.at[:, pl.ds(pl.multiple_of(side * half, half), half)], rows_v, in_sem.at[4, 0]
     )
     cols_in = pltpu.make_async_copy(basis_out, cols_v, in_sem.at[4, 1])
+    scales_read = pltpu.make_async_copy(scales_in, scales_v, in_sem.at[4, 2])
+    scales_write = pltpu.make_async_copy(scales_v, scales_out, in_sem.at[4, 3])
+    scales_read.start()
     rows_in.start()
     cols_in.start()
 
@@ -1302,14 +1328,17 @@
             copy.start()
         return carry
 
+    scales_read.wait()
+    scales_write.start()
     lax.fori_loop(0, slots, slot, 0)
     for q in range(slots):
         for copy in state_out(q):
             copy.wait()
+    scales_write.wait()
 
 
 def update(
-    owners, divided, basis_in, basis_out, states, total, norm_sums, head_sums, norm_states, head_states
+    owners, divided, scales, basis_in, basis_out, states, total, norm_sums, head_sums, norm_states, head_states
 ):
     full, dma = jnp.float32, pltpu.SemaphoreType.DMA
     slots, half, width = states[0].shape
@@ -1319,9 +1348,9 @@
     one = jax.ShapeDtypeStruct((1, 1), full)
     return pl.pallas_call(
         update_kernel,
-        out_shape=like + [one, one],
-        in_specs=[smem] + [any_spec] * 6 + [vmem] * 9,
-        out_specs=[any_spec] * 3 + [vmem] * 6 + [smem] * 2,
+        out_shape=like + [one, one, jax.ShapeDtypeStruct(scales.shape, full)],
+        in_specs=[smem] + [any_spec] * 7 + [vmem] * 9,
+        out_specs=[any_spec] * 3 + [vmem] * 6 + [smem] * 2 + [any_spec],
         scratch_shapes=[
             pltpu.SMEM((slots,), jnp.int32),
             pltpu.VMEM((slots, 2, width, half), jnp.bfloat16),
@@ -1330,6 +1359,7 @@
             pltpu.VMEM(states[0].shape, full),
             pltpu.VMEM(states[0].shape, full),
             pltpu.VMEM(states[0].shape, full),
+            pltpu.VMEM(scales.shape, full),
             dma((5, slots)),
             dma((3, slots)),
         ],
@@ -1338,6 +1368,7 @@
     )(
         owners,
         divided,
+        scales,
         basis_in,
         basis_out,
         *states,
@@ -1544,6 +1575,7 @@
     results = update(
         owners,
         divided,
+        new_scales,
         basis_in,
         basis_out,
         (master, moment1, moment2),
@@ -1554,7 +1586,7 @@
         (head.T, head_m.T, head_v.T),
     )
     loss_all, weight_all = results[9][0, 0], results[10][0, 0]
-    return (loss_all, weight_all, new_scales, *results[:6], *(x.T for x in results[6:9]))
+    return (loss_all, weight_all, results[11], *results[:6], *(x.T for x in results[6:9]))
 
 
 def shards(*args):

time: 289 us -> 288 us (level)
  no operation moved by 1% of the time
where the time goes in v7:
time: 288 us; the launch traced here: 287 us
  Pallas kernels  287 us (100%)
    pallas_call x1, Pallas kernels, whole_step(): pl.pallas_call(functools.partial(step_kernel, images_all), out_shape=[jax...  270 us
    pallas_call x1, Pallas kernels, update(): pl.pallas_call(update_kernel, out_shape=like + [one, one, jax.ShapeDtypeS...  16.2 us

profile of v7, /device:TPU:0, one launch (start us, length us, event | category | flops | bytes accessed | tf_op | source)
XLA Modules:
  0.0 287.5 jit_solution(12699683430913682005)
XLA Ops:
  0.6 270.5 %whole_step.1 = (bf16[2,2,2,4,9,2,32,256]{7,6,5,4,3,2,1,0:T(8,128)(2,1)}, f32[9,2,32,256]{3,2,1,0:T(8,128)}, f32[4,512]{1,0:T(4,128)}, f32[2,4,512]{2,1,0:T(4,128)}, f32[24,512]{1,0:T(8,128)}) custom-call(bf16[32,8,8,512]{3,2,1,0:T(8,128)(2,1)} %feats_hbm.1, s32[32]{0:T(128)} %image_group.1, s32[32]{0:T(128)} %labels_ref.1, s32[10]{0:T(128)} %class_ref.1, ...), custom_call_target="tpu_custom_call" | custom-call | tf_op jit(solution)/shard_map/whole_step/pallas_call | solution.py:1107
  271.1 16.2 %update.1 = (f32[10,256,512]{2,1,0:T(8,128)}, f32[10,256,512]{2,1,0:T(8,128)}, f32[10,256,512]{2,1,0:T(8,128)}, f32[2,2,512]{2,1,0:T(2,128)}, f32[2,2,512]{2,1,0...) custom-call(s32[18]{0:T(128)} %owners_ref.3, ...), custom_call_target="tpu_custom_call" | custom-call | tf_op jit(solution)/shard_map/update/pallas_call | solution.py:1349

commit v8 on v7

--- a/solution.py
+++ b/solution.py
@@ -874,38 +874,7 @@
             products(ja, 1 - me_s, store)
             side_copy(ja).start()
 
-        jb, due = at_step(k - 1)
-
-        @pl.when(due & (jb >= 2))
-        def _():
-            x1_copy(jb - 2).wait_send()
-            y1_copy(jb - 2).wait_send()
-
-        @pl.when(due)
-        def _():
-            ring, four = lax.rem(jb, 2), lax.rem(jb, 4)
-            side_copy(jb).wait_recv()
-
-            def store(u, x_to, z_to, total, square):
-                got = s_recv[four, u].astype(full)
-                both = (total + got[0], square + got[1])
-                for c in range(2):
-                    if z_to < 2 and u < 4:
-                        x1_send[ring, z_to * 2 + c] = both[c].astype(low)
-                    elif z_to < 2:
-                        x1_keep[ring, z_to * 2 + c] = both[c]
-                    else:
-                        at = x_to * 2 + z_to - 2
-                        for y_to in range(2):
-                            value = both[c][y_to * 32 : y_to * 32 + 32]
-                            y1_send[ring, y_to, at, c * 32 : c * 32 + 32, :] = value.astype(low)
-                            y1_keep[ring, y_to, at, c * 32 : c * 32 + 32, :] = value
-
-            products(jb, me_s, store)
-            x1_copy(jb).start()
-            y1_copy(jb).start()
-
-        j7, due = at_step(k - 12)
+        j7, due = at_step(k - 13)
 
         @pl.when(due)
         def _():
@@ -917,7 +886,7 @@
             g2y_copy(j7).wait_recv()
             gs_copy(j7).start()
 
-        j6, due = at_step(k - 10)
+        j6, due = at_step(k - 11)
 
         @pl.when(due)
         def _():
@@ -931,7 +900,7 @@
             g1x_copy(j6).wait_recv()
             g2y_copy(j6).start()
 
-        j5, due = at_step(k - 8)
+        j5, due = at_step(k - 9)
 
         @pl.when(due)
         def _():
@@ -946,7 +915,7 @@
             g1y_copy(j5).start()
             g1x_copy(j5).start()
 
-        j4, due = at_step(k - 6)
+        j4, due = at_step(k - 7)
 
         @pl.when(due & (j4 == 0))
         def _():
@@ -985,7 +954,7 @@
                     ns_v.at[li], ns_out.at[:, me_y], misc_sem.at[4], misc_sem.at[5], to_y
                 ).start()
 
-        j3, due = at_step(k - 4)
+        j3, due = at_step(k - 5)
 
         @pl.when(due)
         def _():
@@ -1006,7 +975,7 @@
             for d in (1, 2, 3):
                 z_copy(j3, d).start()
 
-        j2, due = at_step(k - 2)
+        j2, due = at_step(k - 3)
 
         @pl.when(due)
         def _():
@@ -1041,6 +1010,37 @@
                 ).astype(low)
             x2_copy(j2).start()
 
+        jb, due = at_step(k - 1)
+
+        @pl.when(due & (jb >= 2))
+        def _():
+            x1_copy(jb - 2).wait_send()
+            y1_copy(jb - 2).wait_send()
+
+        @pl.when(due)
+        def _():
+            ring, four = lax.rem(jb, 2), lax.rem(jb, 4)
+            side_copy(jb).wait_recv()
+
+            def store(u, x_to, z_to, total, square):
+                got = s_recv[four, u].astype(full)
+                both = (total + got[0], square + got[1])
+                for c in range(2):
+                    if z_to < 2 and u < 4:
+                        x1_send[ring, z_to * 2 + c] = both[c].astype(low)
+                    elif z_to < 2:
+                        x1_keep[ring, z_to * 2 + c] = both[c]
+                    else:
+                        at = x_to * 2 + z_to - 2
+                        for y_to in range(2):
+                            value = both[c][y_to * 32 : y_to * 32 + 32]
+                            y1_send[ring, y_to, at, c * 32 : c * 32 + 32, :] = value.astype(low)
+                            y1_keep[ring, y_to, at, c * 32 : c * 32 + 32, :] = value
+
+            products(jb, me_s, store)
+            x1_copy(jb).start()
+            y1_copy(jb).start()
+
         @pl.when((k >= 6) & (k < 9))
         def _():
             lax.fori_loop(0, 3, lambda t, carry: back((k - 6) * 3 + t, carry), 0)
@@ -1069,7 +1069,7 @@
 
         return carry
 
-    lax.fori_loop(0, steps + 5 + 12, step, 0)
+    lax.fori_loop(0, steps + 5 + 13, step, 0)
 
     def finish(j, carry):
         gs_copy(j).wait_recv()

time: 288 us -> 287 us (level)
  no operation moved by 1% of the time
where the time goes in v8:
time: 287 us; the launch traced here: 286 us
  Pallas kernels  286 us (100%)
    pallas_call x1, Pallas kernels, whole_step(): pl.pallas_call(functools.partial(step_kernel, images_all), out_shape=[jax...  269 us
    pallas_call x1, Pallas kernels, update(): pl.pallas_call(update_kernel, out_shape=like + [one, one, jax.ShapeDtypeS...  16.2 us

profile of v8, /device:TPU:0, one launch (start us, length us, event | category | flops | bytes accessed | tf_op | source)
XLA Modules:
  0.0 286.4 jit_solution(3557399615227195193)
XLA Ops:
  0.6 269.4 %whole_step.1 = (bf16[2,2,2,4,9,2,32,256]{7,6,5,4,3,2,1,0:T(8,128)(2,1)}, f32[9,2,32,256]{3,2,1,0:T(8,128)}, f32[4,512]{1,0:T(4,128)}, f32[2,4,512]{2,1,0:T(4,128)}, f32[24,512]{1,0:T(8,128)}) custom-call(bf16[32,8,8,512]{3,2,1,0:T(8,128)(2,1)} %feats_hbm.1, s32[32]{0:T(128)} %image_group.1, s32[32]{0:T(128)} %labels_ref.1, s32[10]{0:T(128)} %class_ref.1, ...), custom_call_target="tpu_custom_call" | custom-call | tf_op jit(solution)/shard_map/whole_step/pallas_call | solution.py:1107
  270.1 16.2 %update.1 = (f32[10,256,512]{2,1,0:T(8,128)}, f32[10,256,512]{2,1,0:T(8,128)}, f32[10,256,512]{2,1,0:T(8,128)}, f32[2,2,512]{2,1,0:T(2,128)}, f32[2,2,512]{2,1,0...) custom-call(s32[18]{0:T(128)} %owners_ref.3, ...), custom_call_target="tpu_custom_call" | custom-call | tf_op jit(solution)/shard_map/update/pallas_call | solution.py:1349
